TPU v7x, 128 devices: a whole 4x4x4 slice. The times are simulated.
128 devices in a mesh: gx: 16 (over z, x), gy: 8 (over y, core).
Axes of the slice: x: 4, y: 4, z: 4, core: 2. Of those that a mesh axis runs over, the one named last changes fastest.
Arguments:
- increment: bfloat16 [64, 768, 1024], P(None, 'gx', 'gy'), may hold values from -6 to 6
- ensemble: bfloat16 [4, 64, 768, 1024], P(None, None, 'gx', 'gy'), may hold values from -6 to 6
- wind_u: bfloat16 [64, 768, 1024], P(None, 'gx', 'gy'), may hold values from -0.94921875 to 0.94921875
- wind_v: bfloat16 [64, 768, 1024], P(None, 'gx', 'gy'), may hold values from -0.94921875 to 0.94921875
- filter_length: float32 [64], replicated, may hold values from 8 to 6144
- jacobian: bfloat16 [128, 512, 64], P(('gx', 'gy')), may hold values from -0.75 to 0.75
- obs_weight: float32 [128, 512], P(('gx', 'gy')), may hold values from 0.1 to 1
- departure: bfloat16 [8192, 512, 128], P(('gx', 'gy')), may hold values from -6 to 6
- obs_home: int32 [8192], P(('gx', 'gy')), may hold values from 0 to 127, as said below
- obs_line: int32 [8192], P(('gx', 'gy')), may hold values from 0 to 47
- obs_count: int32 [8192], P(('gx', 'gy')), may hold values from 1 to 128
Outputs:
- grad_alpha: float32 [4, 64, 768, 1024], P(None, None, 'gx', 'gy')
- grad_static: float32 [64, 768, 1024], P(None, 'gx', 'gy')
Inputs may be any that keep to these rules, and one draw needn't show every extreme that they name: `obs_home`: the records of one device name 64 distinct grid devices, each exactly 1 times.
All inputs are finite; a program needn't handle non-finite values.
Results may differ from a plain program's by a relative error of at most 0.003.
Values may be sent and summed in bfloat16 or wider, within the bound.
No kernel may reach another device: no remote copies, remote signals or barrier semaphores. Data moves between devices by JAX's collectives and lax.ppermute only.
A program may use at most 192 MiB of HBM per device.

v0:
```python
import jax
import jax.numpy as jnp
from jax import lax
from jax.sharding import Mesh
from jax.sharding import PartitionSpec as P

GX_GY = ("gx_0", "gx_1", "gy")
GX = ("gx_0", "gx_1")


precise = lax.Precision.HIGHEST


def nothing_yet(array, identity):
    return jax.tree.map(
        lambda a, e: jnp.broadcast_to(jnp.asarray(e, a.dtype), a.shape), array, identity
    )


def carried_in(array, axes, combine, identity, reverse):
    before = start = nothing_yet(array, identity)
    subtotal = array
    for axis in reversed(axes):
        length, position = (lax.axis_size(axis), lax.axis_index(axis))
        pieces = jax.tree.map(lambda part: lax.all_gather(part, axis), subtotal)
        inside, subtotal = (start, start)
        for k in reversed(range(length)) if reverse else range(length):
            passed = k > position if reverse else k < position
            subtotal = combine(subtotal, jax.tree.map(lambda part: part[k], pieces))
            inside = jax.tree.map(lambda new, old: jnp.where(passed, new, old), subtotal, inside)
        before = combine(inside, before)
    return before


def sent_to_all(array, axis):
    copies = jnp.broadcast_to(array, (lax.axis_size(axis), *array.shape))
    return lax.all_to_all(copies, axis, split_axis=0, concat_axis=0, tiled=True)


def collected_together(array, axis):
    leaves = jax.tree.leaves(array)
    order = sorted(range(len(leaves)), key=lambda k: -leaves[k].size)
    width = (1, *leaves[order[0]].shape)[-1]
    lines = [
        jnp.pad(leaves[k].reshape(-1), (0, -leaves[k].size % width)).reshape(-1, width)
        for k in order
    ]
    both, at, found = (sent_to_all(jnp.concatenate(lines), axis), 0, {})
    for k, line in zip(order, lines):
        share = both[:, at : at + len(line)].reshape(len(both), -1)
        found[k] = share[:, : leaves[k].size].reshape(-1, *leaves[k].shape)
        at += len(line)
    numbers = iter(range(len(leaves)))
    return jax.tree.map(lambda _: found[next(numbers)], array)


def collected_alike(array, axis):
    leaves, found = (jax.tree.leaves(array), {})
    for initial, a in enumerate(leaves):
        if initial not in found:
            alike = [k for k, b in enumerate(leaves) if b.dtype == a.dtype]
            got = (
                collected_together([leaves[k] for k in alike], axis)
                if len(alike) > 1
                else [sent_to_all(a, axis)]
            )
            for k, b in zip(alike, got):
                found[k] = b
    numbers = iter(range(len(leaves)))
    return jax.tree.map(lambda _: found[next(numbers)], array)


def folded_in_pairs(pieces, combine):
    while len(jax.tree.leaves(pieces)[0]) > 1:
        pieces = jax.vmap(combine)(
            *(jax.tree.map(lambda part: part[side::2], pieces) for side in (0, 1))
        )
    return jax.tree.map(lambda part: part[0], pieces)


def prefix(array, axis, combine, identity, reverse):
    length, position = (lax.axis_size(axis), lax.axis_index(axis))
    passed = jnp.arange(length) > position if reverse else jnp.arange(length) < position

    def kept(part, zero, own):
        part = jnp.where(
            passed.reshape(-1, *(1 for _ in own.shape)), part, jnp.asarray(zero, own.dtype)
        )
        return part[::-1] if reverse else part

    pieces = collected_alike(array, axis)
    return folded_in_pairs(jax.tree.map(kept, pieces, identity, array), combine)


def as_sent(array):
    return jax.tree.map(lambda a: a.astype(jnp.bfloat16) if a.dtype == jnp.float32 else a, array)


def padded_2(cells, sides, width):
    for axis, dim in sides:
        count = lax.axis_size(axis)
        ends = count - 1
        head = lax.slice_in_dim(cells, 0, width, axis=dim)
        tail = lax.slice_in_dim(cells, cells.shape[dim] - width, cells.shape[dim], axis=dim)
        cells = jnp.concatenate(
            [
                lax.ppermute(tail, axis, [(i, (i + 1) % count) for i in range(ends)]),
                cells,
                lax.ppermute(head, axis, [((i + 1) % count, i) for i in range(ends)]),
            ],
            axis=dim,
        )
    return cells


def trade_lines(requests):
    return lax.all_to_all(requests, GX_GY, split_axis=0, concat_axis=0, tiled=True)


def trade_columns(payload):
    return lax.all_to_all(payload, GX_GY, split_axis=0, concat_axis=0, tiled=True)


def triangle(lengths, count, coefs, upward):
    row_pos = jnp.arange(count, dtype=jnp.float32)[:, None]
    col_pos = jnp.arange(count, dtype=jnp.float32)[None, :]
    if upward:
        spacing = col_pos - row_pos
    else:
        spacing = row_pos - col_pos
    values = coefs[:, None, None] * jnp.exp(
        -jnp.maximum(spacing, 0.0)[None] / lengths[:, None, None]
    )
    return jnp.where(spacing[None] >= 0.0, values, 0.0)


def chain(earlier, later):
    return (earlier[0] * later[0], later[0] * earlier[1] + later[1])


def body(
    increment,
    ensemble,
    wind_u,
    wind_v,
    filter_length,
    jacobian,
    obs_weight,
    departure,
    obs_home,
    obs_line,
    obs_count,
):
    home_count = lax.axis_size(GX_GY)
    records_here = obs_home.shape[0]
    most = (records_here + home_count - 1) // home_count
    lev_all, cells_x, cells_y = increment.shape
    slot_count = home_count * most
    onehot_home = (obs_home[:, None] == jnp.arange(home_count, dtype=jnp.int32)[None, :]).astype(
        jnp.int32
    )
    ranking = jnp.cumsum(onehot_home, axis=0) - 1
    rank_of = jnp.sum(onehot_home * ranking, axis=1)
    slot_of = obs_home * most + rank_of
    placing = slot_of[:, None] == jnp.arange(slot_count, dtype=jnp.int32)[None, :]
    requests = jnp.sum(placing.astype(jnp.int32) * (obs_line[:, None] + 1), axis=0) - 1
    asked_lines = trade_lines(requests.reshape(home_count, most)).reshape(slot_count)
    select = (asked_lines[:, None] == jnp.arange(cells_x, dtype=jnp.int32)[None, :]).astype(
        jnp.bfloat16
    )
    outgoing = jnp.einsum(
        "sx,lxy->sly", select, increment, preferred_element_type=jnp.float32
    ).astype(jnp.bfloat16)
    arrived = trade_columns(outgoing.reshape(home_count, most, lev_all, cells_y)).reshape(
        slot_count, lev_all, cells_y
    )
    gathered = jnp.take(arrived, slot_of, axis=0)
    matrix = jacobian[0]
    predicted = jnp.einsum("cl,oly->ocy", matrix, gathered, preferred_element_type=jnp.float32)
    observed = (jnp.arange(cells_y, dtype=jnp.int32)[None, :] < obs_count[:, None]).astype(
        jnp.float32
    )
    weighted = (
        obs_weight[0][None, :, None]
        * (predicted - departure.astype(jnp.float32))
        * observed[:, None, :]
    ).astype(jnp.bfloat16)
    adjoint = jnp.einsum(
        "cl,ocy->oly", matrix, weighted, preferred_element_type=jnp.float32
    ).astype(jnp.bfloat16)
    returning = jnp.einsum(
        "os,oly->sly", placing.astype(jnp.bfloat16), adjoint, preferred_element_type=jnp.float32
    ).astype(jnp.bfloat16)
    received = trade_columns(returning.reshape(home_count, most, lev_all, cells_y)).reshape(
        slot_count, lev_all, cells_y
    )
    grad_obs = jnp.einsum("sx,sly->lxy", select, received, preferred_element_type=jnp.float32)
    forward_coef = jnp.sqrt(-jnp.expm1(-2.0 / filter_length))
    backward_coef = -jnp.expm1(-1.0 / filter_length)
    fields = jnp.concatenate(
        [grad_obs[None], ensemble.astype(jnp.float32) * grad_obs[None]], axis=0
    )
    span_x = jnp.exp(-cells_x / filter_length)[None, :, None]
    position = jnp.arange(cells_x, dtype=jnp.float32)
    local = jnp.einsum(
        "lij,mljy->mliy",
        triangle(filter_length, cells_x, forward_coef, False),
        fields,
        precision=precise,
    )
    start_id = (jnp.ones_like(span_x), jnp.zeros_like(local[:, :, 0, :]))
    entering = carried_in((span_x, local[:, :, -1, :]), GX, chain, start_id, False)[1]
    rise = jnp.exp(-(position[None, :] + 1.0) / filter_length[:, None])
    fields = local + rise[None, :, :, None] * entering[:, :, None, :]
    local = jnp.einsum(
        "lij,mljy->mliy",
        triangle(filter_length, cells_x, backward_coef, True),
        fields,
        precision=precise,
    )
    entering = carried_in((span_x, local[:, :, 0, :]), GX, chain, start_id, True)[1]
    rise = jnp.exp(-(cells_x - position[None, :]) / filter_length[:, None])
    fields = local + rise[None, :, :, None] * entering[:, :, None, :]
    span_y = jnp.exp(-cells_y / filter_length)[None, :, None]
    position_y = jnp.arange(cells_y, dtype=jnp.float32)
    local = jnp.einsum(
        "lij,mlxj->mlxi",
        triangle(filter_length, cells_y, forward_coef, False),
        fields,
        precision=precise,
    )
    start_y = (jnp.ones_like(span_y), jnp.zeros_like(local[:, :, :, 0]))
    entering = prefix((span_y, local[:, :, :, -1]), "gy", chain, start_y, False)[1]
    rise = jnp.exp(-(position_y[None, :] + 1.0) / filter_length[:, None])
    fields = local + rise[None, :, None, :] * entering[:, :, :, None]
    local = jnp.einsum(
        "lij,mlxj->mlxi",
        triangle(filter_length, cells_y, backward_coef, True),
        fields,
        precision=precise,
    )
    entering = prefix((span_y, local[:, :, :, 0]), "gy", chain, start_y, True)[1]
    rise = jnp.exp(-(cells_y - position_y[None, :]) / filter_length[:, None])
    fields = local + rise[None, :, None, :] * entering[:, :, :, None]
    grad_alpha = fields[1:]
    static = fields[0]
    speed_x = wind_u.astype(jnp.float32)
    speed_y = wind_v.astype(jnp.float32)
    for sweep_index in range(3):
        padded = padded_2(as_sent(static), ((GX, 1),), 1).astype(static.dtype)
        static = (
            static
            + jnp.maximum(speed_x, 0.0) * (padded[:, :-2, :] - static)
            + jnp.maximum(-speed_x, 0.0) * (padded[:, 2:, :] - static)
        )
        padded = padded_2(as_sent(static), (("gy", 2),), 1).astype(static.dtype)
        static = (
            static
            + jnp.maximum(speed_y, 0.0) * (padded[:, :, :-2] - static)
            + jnp.maximum(-speed_y, 0.0) * (padded[:, :, 2:] - static)
        )
    return (grad_alpha, static)


def solution(mesh):
    finer = Mesh(mesh.devices.reshape(4, 4, mesh.shape["gy"]), ("gx_0", "gx_1", "gy"))
    placed = (
        P(None, GX, "gy"),
        P(None, None, GX, "gy"),
        P(None, GX, "gy"),
        P(None, GX, "gy"),
        P(),
        P(GX_GY, None, None),
        P(GX_GY, None),
        P(GX_GY, None, None),
        P(GX_GY),
        P(GX_GY),
        P(GX_GY),
    )
    return jax.shard_map(
        body,
        mesh=finer,
        in_specs=placed,
        out_specs=(P(None, None, GX, "gy"), P(None, GX, "gy")),
        check_vma=False,
    )
```

profile of v0, /device:TPU:1, one launch (start us, length us, event | category | flops | bytes accessed | tf_op | source)
XLA Modules:
  0.0 373.9 jit_solution(14104801456273148694)
XLA Ops:
  3.9 20.9 %all_to_all.26 = s32[128,1,1]{2,1,0:T(1,128)S(1)} all-to-all(s32[128,1,1]{2,1,0:T(1,128)S(1)} %copy.334), channel_id=1, replica_groups=mesh['gx_0'=4,'gx_1'=4,'gy'=8] {'gx_0','gx_1','gy'}, dimensions={0} | all-to-all | bytes 1024 | tf_op jit(solution)/shard_map/all_to_all | solution.py:117
  35.1 12.0 %copy.336 = bf16[64,512,128]{1,2,0:T(8,128)(2,1)} copy(bf16[64,512,128]{2,1,0:T(8,128)(2,1)} %param.18) | data formatting | bytes 16777216 | tf_op args[7]
  48.6 13.6 %all-reduce.1 = f32[256]{0:T(256)S(1)} all-reduce(f32[256]{0:T(256)S(1)} %get-tuple-element.80), channel_id=2, replica_groups=mesh['gx_0'=4,'gx_1'=4,'gy'=8] {'gx_1'}, use_global_device_ids=true, to_apply=%add.1 | all-reduce | flops 256 | bytes 2048
  62.3 8.2 %all_gather.27 = f32[4,1,64,1]{2,3,1,0:T(1,128)S(1)} all-gather(f32[1,1,64,1]{2,3,1,0:T(1,128)S(1)} %get-tuple-element.72), channel_id=1, replica_groups=mesh['gx_0'=4,'gx_1'=4,'gy'=8] {'gx_0'}, dimensions={0}, use_global_device_ids=true | all-gather | bytes 1280 | tf_op jit(solution)/shard_map/all_gather | solution.py:25
  70.5 5.7 %all_gather.30 = f32[4,1,64,1]{2,3,1,0:T(1,128)S(1)} all-gather(f32[1,1,64,1]{2,3,1,0:T(1,128)S(1)} %get-tuple-element.71), channel_id=1, replica_groups=mesh['gx_0'=4,'gx_1'=4,'gy'=8] {'gx_0'}, dimensions={0}, use_global_device_ids=true | all-gather | bytes 1280 | tf_op jit(solution)/shard_map/all_gather | solution.py:25
  78.0 10.2 %fusion.96 = bf16[64,64,128]{2,1,0:T(8,128)(2,1)S(1)} fusion(bf16[64,512,128]{1,2,0:T(8,128)(2,1)} %copy.336, f32[64,128]{1,0:T(8,128)S(1)} %fusion.145, f32[512]{0:T(512)S(1)} %bitcast.290, bf16[64,64,128]{2,1,0:T(8,128)(2,1)} %gather_fusion, pred[64]{0:T(512)(128)(4,1)S(1)} %get-tuple-element.34, bf16[1,512,64]{1,2,0:T(8,128)(2,1)S(1)} %copy-done.12), kind=kOutput, calls=%fused_computation.110 | convolution fusion | flops 1095761920 | bytes 10586176 | tf_op jit(solution)/shard_map/cl,ocy->oly/dot_general | solution.py:188
  92.0 11.5 %all-to-all-start.2 = ((bf16[128,1,64,128]{3,2,1,0:T(8,128)(2,1)}), bf16[128,1,64,128]{3,2,1,0:T(8,128)(2,1)S(1)}, u32[]{:S(2)}, u32[]{:S(2)}) async-start(bf16[128,1,64,128]{3,2,1,0:T(8,128)(2,1)} %copy.339), calls=%async_computation.2 | async-start | bytes 4194304 | tf_op jit(solution)/shard_map/all_to_all | solution.py:121
  104.0 29.9 %all-to-all-done.2 = bf16[128,1,64,128]{3,2,1,0:T(8,128)(2,1)S(1)} async-done(((bf16[128,1,64,128]{3,2,1,0:T(8,128)(2,1)}), bf16[128,1,64,128]{3,2,1,0:T(8,128)(2,1)S(1)}, u32[]{:S(2)}, u32[]{:S(2)}) %all-to-all-start.2) | async-done | bytes 2097184 | tf_op jit(solution)/shard_map/all_to_all | solution.py:121
  136.7 8.2 %fusion.33 = f32[5,64,48,128]{3,2,0,1:T(8,128)S(1)} fusion(f32[4,64,48,128]{3,2,0,1:T(8,128)S(1)} %convert_multiply_fusion, f32[1,64,48,128]{3,2,0,1:T(8,128)S(1)} %bitcast.282, f32[64]{0:T(128)S(1)} %copy-done.10, f32[48,48]{1,0:T(8,128)S(1)} %maximum_negate_fusion.3, f32[64]{0:T(128)S(1)} %get-tuple-element.81, pred[48,48]{1,0:T(8,128)(4,1)S(1)} %fusion.147), kind=kOutput, calls=%fused_computation.35 | convolution fusion | flops 1134870528 | bytes 15740672 | tf_op jit(solution)/shard_map/lij,mljy->mliy/dot_general | solution.py:205
  145.1 11.5 %all-gather.1 = f32[20,64,1,128]{3,2,0,1:T(1,128)S(1)} all-gather(f32[5,64,1,128]{3,2,0,1:T(1,128)S(1)} %slice.388), channel_id=3, replica_groups=mesh['gx_0'=4,'gx_1'=4,'gy'=8] {'gx_1'}, dimensions={0}, use_global_device_ids=true | all-gather | bytes 819200 | tf_op jit(solution)/shard_map/all_gather | solution.py:25
  157.2 10.8 %all_gather.29 = f32[4,5,64,128]{3,2,1,0:T(8,128)S(1)} all-gather(f32[1,5,64,128]{3,2,1,0:T(8,128)S(1)} %bitcast_add_fusion.12), channel_id=1, replica_groups=mesh['gx_0'=4,'gx_1'=4,'gy'=8] {'gx_0'}, dimensions={0}, use_global_device_ids=true | all-gather | bytes 819200 | tf_op jit(solution)/shard_map/all_gather | solution.py:25
  168.4 8.7 %fusion.30 = f32[5,64,48,128]{3,2,0,1:T(8,128)S(1)} fusion(f32[5,64,48,128]{3,2,0,1:T(8,128)S(1)} %fusion.33, f32[5,64,128]{2,0,1:T(8,128)S(1)} %copy.351, f32[64,48]{1,0:T(8,128)S(1)} %get-tuple-element.83, f32[48,48]{1,0:T(8,128)S(1)} %maximum_negate_fusion.2, f32[64]{0:T(128)S(1)} %get-tuple-element.79, f32[64]{0:T(128)S(1)} %copy-done.10, ...), kind=kOutput, calls=%fused_computation.34 | convolution fusion | flops 1136836608 | bytes 15916800 | tf_op jit(solution)/shard_map/lij,mljy->mliy/dot_general | solution.py:215
  177.2 11.4 %all-gather.2 = f32[20,64,1,128]{3,2,0,1:T(1,128)S(1)} all-gather(f32[5,64,1,128]{3,2,0,1:T(1,128)S(1)} %slice.401), channel_id=4, replica_groups=mesh['gx_0'=4,'gx_1'=4,'gy'=8] {'gx_1'}, dimensions={0}, use_global_device_ids=true | all-gather | bytes 819200 | tf_op jit(solution)/shard_map/all_gather | solution.py:25
  189.3 10.6 %all_gather.32 = f32[4,5,64,128]{3,2,1,0:T(8,128)S(1)} all-gather(f32[1,5,64,128]{3,2,1,0:T(8,128)S(1)} %bitcast_add_fusion.4), channel_id=1, replica_groups=mesh['gx_0'=4,'gx_1'=4,'gy'=8] {'gx_0'}, dimensions={0}, use_global_device_ids=true | all-gather | bytes 819200 | tf_op jit(solution)/shard_map/all_gather | solution.py:25
  200.2 10.1 %fusion.36 = f32[5,64,48,128]{3,2,0,1:T(8,128)S(1)} fusion(f32[5,64,48,128]{3,2,0,1:T(8,128)S(1)} %fusion.30, f32[5,64,128]{2,0,1:T(8,128)S(1)} %copy.360, f32[64,48]{1,0:T(8,128)S(1)} %get-tuple-element.82, f32[64]{0:T(128)S(1)} %copy-done.10, f32[128,128]{1,0:T(8,128)S(1)} %maximum_negate_fusion.1, f32[64]{0:T(128)S(1)} %get-tuple-element.81, ...), kind=kOutput, calls=%fused_computation.36 | convolution fusion | flops 3026976768 | bytes 15987200 | tf_op jit(solution)/shard_map/lij,mlxj->mlxi/dot_general | solution.py:226
  213.4 5.2 %slice.410 = f32[5,64,48,1]{3,2,0,1:T(8,128)} slice(f32[5,64,48,128]{3,2,0,1:T(8,128)S(1)} %fusion.36), slice={[0:5], [0:64], [0:48], [127:128]} | slice | bytes 122880 | tf_op jit(solution)/shard_map/slice | solution.py:233
  218.5 6.7 %copy.361 = f32[5,64,48,1]{1,0,2,3:T(8,128)S(1)} copy(f32[5,64,48,1]{3,2,0,1:T(8,128)} %slice.410) | data formatting | bytes 122880 | tf_op jit(solution)/shard_map/slice | solution.py:233
  226.2 14.9 %all-to-all-start.3 = ((f32[8,322,48]{1,2,0:T(8,128)}), f32[8,322,48]{1,2,0:T(8,128)S(1)}, u32[]{:S(2)}, u32[]{:S(2)}) async-start(f32[8,322,48]{1,2,0:T(8,128)} %broadcast_in_dim.162), calls=%async_computation.3 | async-start | bytes 1179648 | tf_op jit(solution)/shard_map/all_to_all | solution.py:37
  241.3 10.1 %all-to-all-done.3 = f32[8,322,48]{1,2,0:T(8,128)S(1)} async-done(((f32[8,322,48]{1,2,0:T(8,128)}), f32[8,322,48]{1,2,0:T(8,128)S(1)}, u32[]{:S(2)}, u32[]{:S(2)}) %all-to-all-start.3) | async-done | bytes 494624 | tf_op jit(solution)/shard_map/all_to_all | solution.py:37
  252.8 12.8 %fusion.41 = f32[5,64,48,128]{3,2,0,1:T(8,128)} fusion(f32[5,64,48,128]{3,2,0,1:T(8,128)} %copy-done.3, f32[5,64,48]{2,0,1:T(8,128)S(1)} %copy.364, f32[64,128]{1,0:T(8,128)S(1)} %get-tuple-element.77, f32[128,128]{1,0:T(8,128)S(1)} %maximum_negate_fusion, f32[64]{0:T(128)S(1)} %get-tuple-element.79, f32[64]{0:T(128)S(1)} %copy-done.10, ...), kind=kOutput, calls=%fused_computation.37 | convolution fusion | flops 3026976768 | bytes 15905280 | tf_op jit(solution)/shard_map/lij,mlxj->mlxi/dot_general | solution.py:236
  265.6 6.5 %copy.365 = f32[5,64,48,1]{1,0,2,3:T(8,128)S(1)} copy(f32[5,64,48,1]{3,2,0,1:T(8,128)} %bitcast.280) | data formatting | bytes 122880 | tf_op jit(solution)/shard_map/slice | solution.py:242
  277.4 10.2 %all-to-all-done.4 = f32[8,322,48]{1,2,0:T(8,128)S(1)} async-done(((f32[8,322,48]{1,2,0:T(8,128)}), f32[8,322,48]{1,2,0:T(8,128)S(1)}, u32[]{:S(2)}, u32[]{:S(2)}) %all-to-all-start.4) | async-done | bytes 494624 | tf_op jit(solution)/shard_map/all_to_all | solution.py:37
  289.2 5.0 %multiply_add_fusion = f32[5,64,48,128]{3,2,0,1:T(8,128)S(1)} fusion(f32[5,64,48,128]{3,2,0,1:T(8,128)} %fusion.41, f32[5,64,48]{2,0,1:T(8,128)S(1)} %copy.368, f32[64,128]{1,0:T(8,128)S(1)} %get-tuple-element.76), kind=kLoop, calls=%fused_computation.9 | loop fusion | flops 3932160 | bytes 15822848 | tf_op jit(solution)/shard_map/add | solution.py:244
  344.3 4.8 %collective-permute-start.8 = (bf16[64,1,128]{2,1,0:T(2,128)(2,1)S(1)}, bf16[64,1,128]{2,1,0:T(2,128)(2,1)S(1)}, u32[]{:S(2)}, u32[]{:S(2)}) collective-permute-start(bf16[64,1,128]{2,1,0:T(2,128)(2,1)S(1)} %get-tuple-element.40), channel_id=1, source_target_pairs={{0,8},{8,16},{16,24},{24,32},{32,40},{40,48},{48,56},{56,64},{64,7... | collective-permute-start | bytes 49160 | tf_op jit(solution)/shard_map/ppermute | solution.py:107
  (187 shorter events, 111.7 us)
Async XLA Ops:
  0.6 26.6 %copy-start = (bf16[64,48,128]{2,1,0:T(8,128)(2,1)S(1)}, bf16[64,48,128]{2,1,0:T(8,128)(2,1)}, u32[]{:S(2)}) copy-start(bf16[64,48,128]{2,1,0:T(8,128)(2,1)} %param.11) | copy-start | bytes 2359300
  30.6 45.7 %all-to-all-start.1 = ((bf16[128,1,64,128]{3,2,1,0:T(8,128)(2,1)}), bf16[128,1,64,128]{3,2,1,0:T(8,128)(2,1)S(1)}, u32[]{:S(2)}, u32[]{:S(2)}) async-start(bf16[128,1,64,128]{3,2,1,0:T(8,128)(2,1)} %copy.335), calls=%async_computation.1 | async-start | bytes 4194304 | tf_op jit(solution)/shard_map/all_to_all | solution.py:121
  35.1 12.0 %copy-start.14 = (u32[128]{0:T(128)S(1)}, u32[128]{0:T(128)}, u32[]{:S(2)}) copy-start(u32[128]{0:T(128)} %constant.82) | copy-start | bytes 1540
  35.1 13.2 %copy-start.10 = (f32[64]{0:T(128)S(1)}, f32[64]{0:T(128)}, u32[]{:S(2)}) copy-start(f32[64]{0:T(128)} %param.15) | copy-start | bytes 772
  35.1 41.1 %copy-start.11 = (s32[64]{0:T(128)S(1)}, s32[64]{0:T(128)}, u32[]{:S(2)}) copy-start(s32[64]{0:T(128)} %param.21) | copy-start | bytes 772
  47.1 30.9 %copy-start.12 = (bf16[1,512,64]{1,2,0:T(8,128)(2,1)S(1)}, bf16[1,512,64]{1,2,0:T(8,128)(2,1)}, u32[]{:S(2)}) copy-start(bf16[1,512,64]{1,2,0:T(8,128)(2,1)} %param.16) | copy-start | bytes 196612
  47.1 30.9 %copy-start.13 = (f32[1,512]{1,0:T(1,128)S(1)}, f32[1,512]{1,0:T(1,128)}, u32[]{:S(2)}) copy-start(f32[1,512]{1,0:T(1,128)} %param.17) | copy-start | bytes 6148
  92.0 42.0 %all-to-all-start.2 = ((bf16[128,1,64,128]{3,2,1,0:T(8,128)(2,1)}), bf16[128,1,64,128]{3,2,1,0:T(8,128)(2,1)S(1)}, u32[]{:S(2)}, u32[]{:S(2)}) async-start(bf16[128,1,64,128]{3,2,1,0:T(8,128)(2,1)} %copy.339), calls=%async_computation.2 | async-start | bytes 4194304 | tf_op jit(solution)/shard_map/all_to_all | solution.py:121
  226.2 25.2 %all-to-all-start.3 = ((f32[8,322,48]{1,2,0:T(8,128)}), f32[8,322,48]{1,2,0:T(8,128)S(1)}, u32[]{:S(2)}, u32[]{:S(2)}) async-start(f32[8,322,48]{1,2,0:T(8,128)} %broadcast_in_dim.162), calls=%async_computation.3 | async-start | bytes 1179648 | tf_op jit(solution)/shard_map/all_to_all | solution.py:37
  273.1 14.5 %all-to-all-start.4 = ((f32[8,322,48]{1,2,0:T(8,128)}), f32[8,322,48]{1,2,0:T(8,128)S(1)}, u32[]{:S(2)}, u32[]{:S(2)}) async-start(f32[8,322,48]{1,2,0:T(8,128)} %broadcast_in_dim.168), calls=%async_computation.4 | async-start | bytes 1179648 | tf_op jit(solution)/shard_map/all_to_all | solution.py:37
  294.2 8.7 %copy-start.2 = (f32[5,64,48,128]{3,2,0,1:T(8,128)}, f32[5,64,48,128]{3,2,0,1:T(8,128)S(1)}, u32[]{:S(2)}) copy-start(f32[5,64,48,128]{3,2,0,1:T(8,128)S(1)} %multiply_add_fusion) | copy-start | bytes 23592964
  294.2 6.9 %copy-start.5 = (bf16[64,48,128]{2,1,0:T(8,128)(2,1)S(1)}, bf16[64,48,128]{2,1,0:T(8,128)(2,1)}, u32[]{:S(2)}) copy-start(bf16[64,48,128]{2,1,0:T(8,128)(2,1)} %param.13) | copy-start | bytes 2359300
  294.4 3.1 collective-permute-start
  296.0 4.7 %collective-permute-start.1 = (bf16[64,1,128]{2,1,0:T(2,128)(2,1)S(1)}, bf16[64,1,128]{2,1,0:T(2,128)(2,1)S(1)}, u32[]{:S(2)}, u32[]{:S(2)}) collective-permute-start(bf16[64,1,128]{2,1,0:T(2,128)(2,1)S(1)} %get-tuple-element.49), channel_id=1, source_target_pairs={{8,0},{16,8},{24,16},{32,24},{40,32},{48,40},{56,48},{64,56},{72,6... | collective-permute-start | bytes 49160 | tf_op jit(solution)/shard_map/ppermute | solution.py:109
  303.9 7.0 %collective-permute-start.2 = (bf16[64,48,1]{0,1,2:T(8,128)(2,1)S(1)}, bf16[64,48,1]{0,1,2:T(8,128)(2,1)S(1)}, u32[]{:S(2)}, u32[]{:S(2)}) collective-permute-start(bf16[64,48,1]{0,1,2:T(8,128)(2,1)S(1)} %copy.369), channel_id=1, source_target_pairs={{0,1},{1,2},{2,3},{3,4},{4,5},{5,6},{6,7},{8,9},{9,10},{10,11},{11... | collective-permute-start | bytes 18440 | tf_op jit(solution)/shard_map/ppermute | solution.py:107
  308.9 5.0 %collective-permute-start.3 = (bf16[64,48,1]{0,1,2:T(8,128)(2,1)S(1)}, bf16[64,48,1]{0,1,2:T(8,128)(2,1)S(1)}, u32[]{:S(2)}, u32[]{:S(2)}) collective-permute-start(bf16[64,48,1]{0,1,2:T(8,128)(2,1)S(1)} %copy.370), channel_id=1, source_target_pairs={{1,0},{2,1},{3,2},{4,3},{5,4},{6,5},{7,6},{9,8},{10,9},{11,10},{12... | collective-permute-start | bytes 18440 | tf_op jit(solution)/shard_map/ppermute | solution.py:109
  318.4 3.9 %collective-permute-start.4 = (bf16[64,1,128]{2,1,0:T(2,128)(2,1)S(1)}, bf16[64,1,128]{2,1,0:T(2,128)(2,1)S(1)}, u32[]{:S(2)}, u32[]{:S(2)}) collective-permute-start(bf16[64,1,128]{2,1,0:T(2,128)(2,1)S(1)} %get-tuple-element.44), channel_id=1, source_target_pairs={{0,8},{8,16},{16,24},{24,32},{32,40},{40,48},{48,56},{56,64},{64,7... | collective-permute-start | bytes 49160 | tf_op jit(solution)/shard_map/ppermute | solution.py:107
  321.0 4.7 %collective-permute-start.5 = (bf16[64,1,128]{2,1,0:T(2,128)(2,1)S(1)}, bf16[64,1,128]{2,1,0:T(2,128)(2,1)S(1)}, u32[]{:S(2)}, u32[]{:S(2)}) collective-permute-start(bf16[64,1,128]{2,1,0:T(2,128)(2,1)S(1)} %get-tuple-element.45), channel_id=1, source_target_pairs={{8,0},{16,8},{24,16},{32,24},{40,32},{48,40},{56,48},{64,56},{72,6... | collective-permute-start | bytes 49160 | tf_op jit(solution)/shard_map/ppermute | solution.py:109
  330.8 6.0 %collective-permute-start.6 = (bf16[64,48,1]{0,1,2:T(8,128)(2,1)S(1)}, bf16[64,48,1]{0,1,2:T(8,128)(2,1)S(1)}, u32[]{:S(2)}, u32[]{:S(2)}) collective-permute-start(bf16[64,48,1]{0,1,2:T(8,128)(2,1)S(1)} %copy.373), channel_id=1, source_target_pairs={{0,1},{1,2},{2,3},{3,4},{4,5},{5,6},{6,7},{8,9},{9,10},{10,11},{11... | collective-permute-start | bytes 18440 | tf_op jit(solution)/shard_map/ppermute | solution.py:107
  334.9 5.0 %collective-permute-start.7 = (bf16[64,48,1]{0,1,2:T(8,128)(2,1)S(1)}, bf16[64,48,1]{0,1,2:T(8,128)(2,1)S(1)}, u32[]{:S(2)}, u32[]{:S(2)}) collective-permute-start(bf16[64,48,1]{0,1,2:T(8,128)(2,1)S(1)} %copy.374), channel_id=1, source_target_pairs={{1,0},{2,1},{3,2},{4,3},{5,4},{6,5},{7,6},{9,8},{10,9},{11,10},{12... | collective-permute-start | bytes 18440 | tf_op jit(solution)/shard_map/ppermute | solution.py:109
  344.3 6.4 %collective-permute-start.8 = (bf16[64,1,128]{2,1,0:T(2,128)(2,1)S(1)}, bf16[64,1,128]{2,1,0:T(2,128)(2,1)S(1)}, u32[]{:S(2)}, u32[]{:S(2)}) collective-permute-start(bf16[64,1,128]{2,1,0:T(2,128)(2,1)S(1)} %get-tuple-element.40), channel_id=1, source_target_pairs={{0,8},{8,16},{16,24},{24,32},{32,40},{40,48},{48,56},{56,64},{64,7... | collective-permute-start | bytes 49160 | tf_op jit(solution)/shard_map/ppermute | solution.py:107
  349.1 4.9 %collective-permute-start.9 = (bf16[64,1,128]{2,1,0:T(2,128)(2,1)S(1)}, bf16[64,1,128]{2,1,0:T(2,128)(2,1)S(1)}, u32[]{:S(2)}, u32[]{:S(2)}) collective-permute-start(bf16[64,1,128]{2,1,0:T(2,128)(2,1)S(1)} %get-tuple-element.41), channel_id=1, source_target_pairs={{8,0},{16,8},{24,16},{32,24},{40,32},{48,40},{56,48},{64,56},{72,6... | collective-permute-start | bytes 49160 | tf_op jit(solution)/shard_map/ppermute | solution.py:109
  357.3 11.8 %collective-permute-start.10 = (bf16[64,48,1]{0,1,2:T(8,128)(2,1)S(1)}, bf16[64,48,1]{0,1,2:T(8,128)(2,1)S(1)}, u32[]{:S(2)}, u32[]{:S(2)}) collective-permute-start(bf16[64,48,1]{0,1,2:T(8,128)(2,1)S(1)} %copy.377), channel_id=1, source_target_pairs={{0,1},{1,2},{2,3},{3,4},{4,5},{5,6},{6,7},{8,9},{9,10},{10,11},{11... | collective-permute-start | bytes 18440 | tf_op jit(solution)/shard_map/ppermute | solution.py:107
  361.0 8.7 %collective-permute-start.11 = (bf16[64,48,1]{0,1,2:T(8,128)(2,1)S(1)}, bf16[64,48,1]{0,1,2:T(8,128)(2,1)S(1)}, u32[]{:S(2)}, u32[]{:S(2)}) collective-permute-start(bf16[64,48,1]{0,1,2:T(8,128)(2,1)S(1)} %copy.378), channel_id=1, source_target_pairs={{1,0},{2,1},{3,2},{4,3},{5,4},{6,5},{7,6},{9,8},{10,9},{11,10},{12... | collective-permute-start | bytes 18440 | tf_op jit(solution)/shard_map/ppermute | solution.py:109
  (8 other events, 17.9 us)
where the time goes:
time: 381 us; the launch traced here: 374 us
  blocking collectives  92.7 us (24%)
  local copies, waits for them, and re-layouts  66.5 us (17%)
  starting transfers between devices  65.1 us (17%)
  waiting for transfers between devices  64.9 us (17%)
  matrix products  53.4 us (14%)
  other arithmetic  28.9 us (8%)
    all_gather x6, blocking collectives, carried_in(): pieces = jax.tree.map(lambda part: lax.all_gather(part, axis), subtotal)  58.3 us
    all_to_all x2, waiting for transfers between devices, trade_columns(): lax.all_to_all(payload, GX_GY, split_axis=0, concat_axis=0, tiled=True)  29.9 us
    all_to_all x1, blocking collectives, trade_lines(): lax.all_to_all(requests, GX_GY, split_axis=0, concat_axis=0, tiled=True)  20.9 us
    all_to_all x2, waiting for transfers between devices, sent_to_all(): return lax.all_to_all(copies, axis, split_axis=0, concat_axis=0, tiled=True)  20.3 us
    unnamed x34, local copies, waits for them, and re-layouts  20 us
    ppermute x6, starting transfers between devices, padded_2(): lax.ppermute(tail, axis, [(i, (i + 1) % count) for i in range(ends)])  19.9 us
    all_to_all x2, starting transfers between devices, sent_to_all(): return lax.all_to_all(copies, axis, split_axis=0, concat_axis=0, tiled=True)  19.3 us
    all_to_all x2, starting transfers between devices, trade_columns(): lax.all_to_all(payload, GX_GY, split_axis=0, concat_axis=0, tiled=True)  15.9 us
  transfers between devices with their start and end apart: 16, of which 8 were waited for; matrix products, arithmetic and copies ran while one was open for 6% of the time, Pallas kernels for 0%

commit v1 on v0

v1 whole, which is shorter than its diff:
```python
import functools

import jax
import jax.numpy as jnp
import numpy as np
from jax import lax
from jax.experimental import pallas as pl
from jax.experimental.pallas import tpu as pltpu
from jax.sharding import PartitionSpec as P

GX, GY = "gx", "gy"
BOTH = (GX, GY)
CHUNKS = 1
MIB = 2**20
F32, BF16 = jnp.float32, jnp.bfloat16

NT = (((1,), (1,)), ((), ()))
TN = (((0,), (0,)), ((), ()))


def vmem():
    return pl.BlockSpec(memory_space=pltpu.VMEM)


def smem():
    return pl.BlockSpec(memory_space=pltpu.SMEM)


def params(mib):
    return pltpu.CompilerParams(vmem_limit_bytes=mib * MIB)


def split(value):
    high = value.astype(BF16)
    return high, (value - high.astype(F32)).astype(BF16)


def sensor_kernel(jt_ref, w_ref, meta_ref, b_ref, out_ref):
    lev = jt_ref.shape[0]
    high, low = split(jt_ref[...].astype(F32) * w_ref[...])
    b_ref[:lev] = high
    b_ref[lev:] = low
    a = lax.dot_general(high, jt_ref[...], NT, preferred_element_type=F32)
    a += lax.dot_general(low, jt_ref[...], NT, preferred_element_type=F32)
    row = lax.broadcasted_iota(jnp.int32, a.shape, 0)
    col = lax.broadcasted_iota(jnp.int32, a.shape, 1)
    high = a.astype(BF16).astype(F32)
    packed = jnp.where(col >= row, high, a - high)
    diagonal = jnp.sum(jnp.where(col == row, a - high, 0.0), axis=0, keepdims=True)
    half = lev // 2
    out_ref[:half] = jnp.concatenate([packed[:half], packed[half:]], axis=1).astype(BF16)
    meta = meta_ref[...].astype(F32)
    first = lax.broadcasted_iota(jnp.int32, meta.shape, 0) == 0
    out_ref[half:] = jnp.where(
        first, jnp.concatenate([diagonal, jnp.zeros_like(diagonal)], axis=1), meta
    ).astype(BF16)


def records_kernel(home_ref, count_ref, b_ref, dep_ref, *outs):
    step, per = pl.program_id(0), dep_ref.shape[0]
    lev = b_ref.shape[0] // 2
    part = lev // len(outs)

    @pl.when(step == 0)
    def _():
        for out in outs:
            out[...] = jnp.zeros_like(out)

    lane = lax.broadcasted_iota(jnp.int32, (lev, dep_ref.shape[2]), 1)
    for k in range(per):
        both = jnp.dot(b_ref[...], dep_ref[k], preferred_element_type=F32)
        q = both[:lev] + both[lev:]
        q = jnp.where(lane < count_ref[step * per + k], q, 0.0).astype(BF16)
        for c, out in enumerate(outs):
            out[home_ref[step * per + k]] = q[c * part : (c + 1) * part]


def columns_kernel(line_ref, count_ref, gathered_ref, inc_ref, g_ref, x_ref):
    lev, nx, ny = inc_ref.shape
    for l in range(lev):
        x_ref[pl.ds(l * nx, nx), :] = inc_ref[l].astype(F32)
    g_ref[...] = jnp.zeros_like(g_ref)
    lane = lax.broadcasted_iota(jnp.int32, (lev, ny), 1)
    half = lev // 2
    eye = lax.broadcasted_iota(jnp.int32, (lev, lev), 0) == lax.broadcasted_iota(
        jnp.int32, (lev, lev), 1
    )
    group = 4

    def some(i, carry):
        found = []
        for k in range(group):
            s = i * group + k
            at = jnp.maximum(line_ref[s] - 1, 0)
            x = x_ref[pl.ds(at, lev, stride=nx), :].astype(BF16)
            kept = gathered_ref[s, :half].astype(F32)
            m = jnp.concatenate([kept[:, :lev], kept[:, lev:]], axis=0)
            diagonal = gathered_ref[s, half : half + 16].astype(F32)[:1, :lev]
            other = jnp.where(eye, diagonal, jnp.transpose(m))
            y = jnp.dot(
                jnp.concatenate([m, other], axis=1).astype(BF16),
                jnp.concatenate([x, x], axis=0),
                preferred_element_type=F32,
            )
            found.append((at, jnp.where(lane < count_ref[s], y, 0.0)))
        for at, y in found:
            g_ref[pl.ds(at, lev, stride=nx), :] += y
        return carry

    lax.fori_loop(0, line_ref.shape[0] // group, some, 0)


def lay_fields(g1_ref, g2_ref, ens_ref, f_ref):
    members, block, nx, ny = ens_ref.shape
    rows = (members + 1) * nx + 8
    for l in range(block):
        g = g1_ref[l] - g2_ref[l]
        f_ref[pl.ds(l * rows + members * nx, nx), :] = g
        for m in range(members):
            f_ref[pl.ds(l * rows + m * nx, nx), :] = ens_ref[m, l].astype(F32) * g


def edges_kernel(g1_ref, g2_ref, ens_ref, coef_ref, h_ref, f_ref, tmp_ref):
    members, block, nx, ny = ens_ref.shape
    fields = members + 1
    rows = fields * nx + 8
    lay_fields(g1_ref, g2_ref, ens_ref, f_ref)

    for base in range(0, block, 8):
        d, fc, rt, d49, inv = (coef_ref[k, base : base + 8] for k in range(5))

        def line(m, x, base=base):
            return f_ref[pl.ds(base * rows + m * nx + x, 8, stride=rows), :]

        ahead = [line(m, 0) for m in range(fields)]
        back = [line(m, nx - 1) for m in range(fields)]
        for x in range(1, nx):
            for m in range(fields):
                ahead[m] = d * ahead[m] + line(m, x)
                back[m] = d * back[m] + line(m, nx - 1 - x)

        def put(row, value, base=base):
            tmp_ref[pl.ds(base * 16 + row, 8, stride=16), :] = value

        for m in range(fields):
            put(3 + m, fc * ahead[m])
            put(8 + m, rt * (back[m] - d49 * ahead[m]))
        e, p = ahead[members], back[members]
        f0, f1 = line(members, 0), line(members, 1)
        f46, f47 = line(members, nx - 2), line(members, nx - 1)
        d48, d47 = d49 * inv, d49 * inv * inv
        p1 = (p - f0) * inv
        p2 = (p1 - f1) * inv
        put(0, rt * (p - d49 * e))
        put(1, rt * (d * f0 + p1 - d48 * e))
        put(2, rt * (d * (d * f0 + f1) + p2 - d47 * e))
        e1 = (e - f47) * inv
        e2 = (e1 - f46) * inv
        put(13, rt * (e2 + d * (f46 + d * f47) - d * d * d * d * e))
        put(14, rt * (e1 + d * f47 - d * d * d * e))
        put(15, rt * (e - d * d * e))
    for l in range(block):
        h_ref[l] = tmp_ref[pl.ds(l * 16, 16), :]


def scan_x_kernel(in_ref, coef_ref, out_ref):
    count, levels = in_ref.shape[:2]
    row = lax.broadcasted_iota(jnp.int32, (8, in_ref.shape[3]), 0)
    for l in range(levels):
        d0, d1, kappa, a0, b0, a1, b1 = (coef_ref[k, l] for k in range(7))
        first, second = [], []
        for g in range(count):
            v = in_ref[g, l].astype(F32)
            first.append(v[:8])
            second.append(v[8:])
        ahead = [jnp.zeros_like(row, F32)]
        for g in range(count - 1):
            ahead.append(first[g] + d0 * ahead[g])
        turned = [pltpu.roll(a, 5, 0) for a in ahead]
        back = [jnp.zeros_like(row, F32)] * count
        for g in range(count - 1, 0, -1):
            back[g - 1] = second[g] + kappa * turned[g] + d1 * back[g]
        static = [(ahead[g][7:8], back[g][4:5]) for g in range(count)]
        low = [first[g] + a0 * static[g][0] + b0 * static[g][1] for g in range(count)]
        high = [second[g] + a1 * static[g][0] + b1 * static[g][1] for g in range(count)]
        none = jnp.zeros_like(row, F32)
        for g in range(count):
            after = low[g + 1] if g + 1 < count else none
            before = high[g - 1] if g > 0 else none
            out_ref[g, l] = jnp.concatenate(
                [jnp.where(row < 3, after, ahead[g]), jnp.where(row < 5, back[g], before)], axis=0
            )


def filter_x_kernel(
    g1_ref,
    g2_ref,
    ens_ref,
    fb_ref,
    coef_ref,
    v_ref,
    hi_ref,
    lo_ref,
    es_ref,
    right_ref,
    left_ref,
    f_ref,
    xs_ref,
    st_ref,
    ey_ref,
):
    members, block, nx, _ = ens_ref.shape
    fields = members + 1
    used = fields * nx
    rows = used + 8
    lay_fields(g1_ref, g2_ref, ens_ref, f_ref)
    deep = hi_ref.shape[1]
    wide = deep + 8
    for l in range(block):
        st_ref[pl.ds(l * 16, 16), :] = fb_ref[l]
    for base in range(0, block, 8):
        d, fc, bc = (coef_ref[k, base : base + 8] for k in range(3))

        def at(m, x, base=base):
            return pl.ds(base * wide + m * nx + x, 8, stride=wide)

        state = [st_ref[pl.ds(base * 16 + 3 + m, 8, stride=16), :] for m in range(fields)]
        for x in range(nx):
            for m in range(fields):
                f = f_ref[pl.ds(base * rows + m * nx + x, 8, stride=rows), :]
                state[m] = fc * f + d * state[m]
                xs_ref[at(m, x), :] = state[m]
        state = [st_ref[pl.ds(base * 16 + 8 + m, 8, stride=16), :] for m in range(fields)]
        for x in range(nx - 1, -1, -1):
            for m in range(fields):
                state[m] = bc * xs_ref[at(m, x), :] + d * state[m]
                xs_ref[at(m, x), :] = state[m]
    row = lax.broadcasted_iota(jnp.int32, (8, f_ref.shape[1]), 0)
    for l in range(block):
        after, before = st_ref[pl.ds(l * 16, 8), :], st_ref[pl.ds(l * 16 + 8, 8), :]
        halo = jnp.where(row < 3, after, jnp.where(row < 5, 0.0, before))
        xs_ref[pl.ds(l * wide + used, 8), :] = halo
        xs_ref[pl.ds(l * wide + used + 8, 8), :] = jnp.zeros_like(halo)
        hi, lo = split(xs_ref[pl.ds(l * wide, deep), :])
        hi_ref[l] = hi
        lo_ref[l] = lo
        one = lax.dot_general(v_ref[l], hi, NT, preferred_element_type=F32)
        two = lax.dot_general(v_ref[l], lo, NT, preferred_element_type=F32)
        ey_ref[pl.ds(l, 8, stride=block), :] = (one[:8] + one[8:] + two[:8])[:, : deep // 2]
        ey_ref[pl.ds(8 * block + l, 8, stride=block), :] = (one[:8] + one[8:] + two[:8])[
            :, deep // 2 :
        ]

    def both(q, side):
        return ey_ref[pl.ds((8 * side + q) * block, block), :].astype(BF16)

    for q in range(2):
        for side in range(2):
            got = both(q, side)
            lanes = pl.ds(side * got.shape[1], got.shape[1])
            for k in range(es_ref.shape[0]):
                es_ref[k, q, :, lanes] = got
    for q in range(3):
        left_ref[q] = both(1 + q, 1)
        right_ref[q] = both(4 + q, 1)


def scan_y_kernel(me_ref, es_ref, fl_ref, fr_ref, coef_ref, out_ref, ahead_ref, back_ref, tmp_ref):
    count, _, lev, lanes = es_ref.shape
    half = lanes // 2
    me = me_ref[0]
    decay, kappa = coef_ref[0], coef_ref[1]
    for side in range(2):
        part = pl.ds(side * half, half)
        state = jnp.zeros((lev, half), F32)
        ahead_ref[0, :, part] = state
        for k in range(count - 1):
            state = es_ref[k, 0, :, part].astype(F32) + decay * state
            ahead_ref[k + 1, :, part] = state
        state = jnp.zeros((lev, half), F32)
        back_ref[count - 1, :, part] = state
        for k in range(count - 1, 0, -1):
            state = (
                es_ref[k, 1, :, part].astype(F32)
                + kappa * ahead_ref[k, :, part]
                + decay * state
            )
            back_ref[k - 1, :, part] = state
    none = jnp.zeros((lev, half), F32)

    def put(q, side, value):
        tmp_ref[side, pl.ds(q, lev, stride=16), :] = value

    for side in range(2):
        part = pl.ds(side * half, half)
        for first, ref in ((0, ahead_ref), (3, back_ref)):
            value = ref[me, :, part]
            high = value.astype(BF16).astype(F32)
            put(first, side, high)
            put(first + 1, side, value - high)
            put(first + 2, side, high)
        for q in (6, 7, 14, 15):
            put(q, side, none)
    before, after = jnp.maximum(me - 1, 0), jnp.minimum(me + 1, count - 1)
    part = pl.ds(half, half)
    for q in range(3):
        put(8 + q, 0, none)
        put(11 + q, 0, none)
        value = (
            fl_ref[q].astype(F32)
            + coef_ref[2 + q] * ahead_ref[before, :, part]
            + coef_ref[5 + q] * back_ref[before, :, part]
        )
        put(8 + q, 1, jnp.where(me > 0, value, 0.0))
        value = (
            fr_ref[q].astype(F32)
            + coef_ref[8 + q] * ahead_ref[after, :, part]
            + coef_ref[11 + q] * back_ref[after, :, part]
        )
        put(11 + q, 1, jnp.where(me < count - 1, value, 0.0))
    for side in range(2):
        out_ref[:, pl.ds(side * half, half)] = tmp_ref[side].astype(BF16)


def final_kernel(hi_ref, lo_ref, nh_ref, nl_ref, fb_ref, ab_ref, u_ref, v_ref, *rest):
    alpha_ref, static_ref = rest[-2:]
    block = hi_ref.shape[0]
    members, _, nx, ny = alpha_ref.shape
    first = members * nx
    deep = nx + 8
    wide = 2 * ny
    for l in range(block):
        hi = hi_ref[l]
        more = lax.dot_general(
            fb_ref[pl.ds(l * 16, 16), :], ab_ref[l], TN, preferred_element_type=F32
        )
        got = jnp.dot(hi, nh_ref[l], preferred_element_type=F32)
        got += jnp.dot(hi, nl_ref[l], preferred_element_type=F32)
        got += jnp.dot(lo_ref[l], nh_ref[l], preferred_element_type=F32)
        got += more[:, :ny]
        for m in range(members):
            alpha_ref[m, l] = got[m * nx : (m + 1) * nx]
        s = jnp.concatenate(
            [got[first : first + deep], more[first : first + deep, ny:]], axis=1
        )
        u, v = u_ref[l].astype(F32), v_ref[l].astype(F32)
        up, vp = u > 0.0, v > 0.0
        u, v = jnp.abs(u), jnp.abs(v)
        for _ in range(3):
            s = s + u * (jnp.where(up, pltpu.roll(s, 1, 0), pltpu.roll(s, deep - 1, 0)) - s)
            s = s + v * (jnp.where(vp, pltpu.roll(s, 1, 1), pltpu.roll(s, wide - 1, 1)) - s)
        static_ref[l] = s[:nx, :ny]


def sent_to_all(array, axis):
    copies = jnp.broadcast_to(array[None], (lax.axis_size(axis), *array.shape))
    return lax.all_to_all(copies, axis, split_axis=0, concat_axis=0, tiled=True)


def from_before(array, axis):
    count = lax.axis_size(axis)
    return lax.ppermute(array, axis, [(i, i + 1) for i in range(count - 1)])


def from_after(array, axis):
    count = lax.axis_size(axis)
    return lax.ppermute(array, axis, [(i + 1, i) for i in range(count - 1)])


def wind_rows_kernel(u_ref, v_ref, first_ref, last_ref):
    nx = u_ref.shape[1]
    for l in range(u_ref.shape[0]):
        u, v = u_ref[l].astype(F32), v_ref[l].astype(F32)
        first_ref[l] = jnp.concatenate([u[:8], v[:8]], axis=0).astype(BF16)
        last_ref[l] = jnp.concatenate([u[nx - 8 :], v[nx - 8 :]], axis=0).astype(BF16)


def taller(u_ref, v_ref, before_ref, after_ref, l):
    before, after = before_ref[l].astype(F32), after_ref[l].astype(F32)
    row = lax.broadcasted_iota(jnp.int32, (8, before.shape[1]), 0)
    both = []
    for k, ref in enumerate((u_ref, v_ref)):
        part = slice(8 * k, 8 * k + 8)
        halo = jnp.where(row < 3, after[part], jnp.where(row > 4, before[part], 0.0))
        both.append(jnp.concatenate([ref[l].astype(F32), halo], axis=0))
    return both


def wind_columns_kernel(u_ref, v_ref, before_ref, after_ref, pick_ref, right_ref, left_ref):
    for l in range(u_ref.shape[0]):
        u, v = taller(u_ref, v_ref, before_ref, after_ref, l)
        gap = jnp.zeros((8, u.shape[1]), F32)
        both = jnp.concatenate([u, gap, v, gap], axis=0).astype(BF16)
        got = lax.dot_general(pick_ref[...], both, NT, preferred_element_type=F32)
        half = got.shape[1] // 2
        for k, ref in enumerate((right_ref, left_ref)):
            some = got[8 * k : 8 * k + 8]
            ref[l] = jnp.concatenate([some[:, :half], some[:, half:]], axis=0).astype(BF16)


def wind_pad_kernel(
    u_ref, v_ref, before_ref, after_ref, left_ref, right_ref, place_ref, out_u_ref, out_v_ref
):
    ny = u_ref.shape[2]
    for l in range(u_ref.shape[0]):
        u, v = taller(u_ref, v_ref, before_ref, after_ref, l)
        sides = jnp.concatenate([left_ref[l], right_ref[l]], axis=0)
        got = lax.dot_general(sides, place_ref[...], TN, preferred_element_type=F32)[: len(u)]
        out_u_ref[l] = jnp.concatenate([u, got[:, :ny]], axis=1).astype(BF16)
        out_v_ref[l] = jnp.concatenate([v, got[:, ny:]], axis=1).astype(BF16)


def levels(*shape):
    return pl.BlockSpec((16, *shape), lambda i: (i, *(0 for _ in shape)))


def whole(*shape):
    return pl.BlockSpec(shape, lambda i: tuple(0 for _ in shape))


def wind_halos(wind_u, wind_v):
    lev, nx, ny = wind_u.shape
    deep = nx + 16
    steps = (lev // 16,)
    first, last = pl.pallas_call(
        wind_rows_kernel,
        grid=steps,
        in_specs=[levels(nx, ny)] * 2,
        out_specs=(levels(16, ny),) * 2,
        out_shape=(jax.ShapeDtypeStruct((lev, 16, ny), BF16),) * 2,
        name="wind_rows",
    )(wind_u, wind_v)
    before, after = from_before(last, GX), from_after(first, GX)
    pick = np.zeros((16, ny), np.float32)
    for k in range(3):
        pick[k, ny - 3 + k] = pick[8 + k, k] = 1
    right, left = pl.pallas_call(
        wind_columns_kernel,
        grid=steps,
        in_specs=[levels(nx, ny)] * 2 + [levels(16, ny)] * 2 + [whole(16, ny)],
        out_specs=(levels(16, deep),) * 2,
        out_shape=(jax.ShapeDtypeStruct((lev, 16, deep), BF16),) * 2,
        name="wind_columns",
    )(wind_u, wind_v, before, after, jnp.asarray(pick, BF16))
    return before, after, from_before(right, GY), from_after(left, GY)


def padded_winds(wind_u, wind_v, halos):
    lev, nx, ny = wind_u.shape
    deep = nx + 16
    place = np.zeros((32, 2 * ny), np.float32)
    for k in range(3):
        place[k, ny - 3 + k] = place[16 + k, k] = 1
        place[8 + k, 2 * ny - 3 + k] = place[24 + k, ny + k] = 1
    return pl.pallas_call(
        wind_pad_kernel,
        grid=(lev // 16,),
        in_specs=[levels(nx, ny)] * 2
        + [levels(16, ny)] * 2
        + [levels(16, deep)] * 2
        + [whole(32, 2 * ny)],
        out_specs=(levels(nx + 8, 2 * ny),) * 2,
        out_shape=(jax.ShapeDtypeStruct((lev, nx + 8, 2 * ny), BF16),) * 2,
        name="wind_pad",
    )(wind_u, wind_v, *halos, jnp.asarray(place, BF16))


def product(length, count, i, j):
    ratio = -jnp.expm1(-1.0 / length) / jnp.sqrt(-jnp.expm1(-2.0 / length))
    last = jnp.maximum(i, j)
    return ratio * jnp.exp(-jnp.abs(i - j) / length) * -jnp.expm1(-2.0 * (count - last) / length)


def entered(length, count, i):
    ratio = jnp.expm1(-1.0 / length) / jnp.expm1(-2.0 / length)
    return ratio * jnp.exp(-(i + 1.0) / length) * -jnp.expm1(-2.0 * (count - i) / length)


def body(
    increment,
    ensemble,
    wind_u,
    wind_v,
    filter_length,
    jacobian,
    obs_weight,
    departure,
    obs_home,
    obs_line,
    obs_count,
):
    count_x, count_y = lax.axis_size(GX), lax.axis_size(GY)
    homes = count_x * count_y
    pos_x, pos_y = lax.axis_index(GX), lax.axis_index(GY)
    lev, nx, ny = increment.shape
    members = ensemble.shape[0]
    channels = jacobian.shape[1]
    records = obs_home.shape[0]
    part = lev // CHUNKS
    share = part // count_x
    rows = (members + 1) * nx + 8
    deep = rows + 8

    named = (obs_home[:, None] == jnp.arange(homes, dtype=jnp.int32)[None, :]).astype(jnp.int32)
    table = jnp.stack(
        [
            jnp.sum(named * (obs_line[:, None] + 1), axis=0),
            jnp.sum(named * obs_count[:, None], axis=0),
        ]
    ).astype(BF16)
    meta = jnp.pad(table, ((1, 13), (0, 128 - homes)))
    jt = jnp.transpose(jacobian[0])
    b, mine = pl.pallas_call(
        sensor_kernel,
        out_shape=(
            jax.ShapeDtypeStruct((2 * lev, channels), BF16),
            jax.ShapeDtypeStruct((lev // 2 + 16, 2 * lev), BF16),
        ),
        in_specs=[vmem()] * 3,
        out_specs=(vmem(), vmem()),
        name="sensor",
    )(jt, obs_weight, meta)
    gathered = sent_to_all(mine, BOTH)

    per = min(8, records)
    qs = pl.pallas_call(
        records_kernel,
        grid_spec=pltpu.PrefetchScalarGridSpec(
            num_scalar_prefetch=2,
            grid=(records // per,),
            in_specs=[
                pl.BlockSpec((2 * lev, channels), lambda i, *_: (0, 0)),
                pl.BlockSpec((per, channels, ny), lambda i, *_: (i, 0, 0)),
            ],
            out_specs=[pl.BlockSpec((homes, part, ny), lambda i, *_: (0, 0, 0))] * CHUNKS,
        ),
        out_shape=[jax.ShapeDtypeStruct((homes, part, ny), BF16)] * CHUNKS,
        compiler_params=params(56),
        name="records",
    )(obs_home, obs_count, b, departure)
    qs, wind_u, wind_v = lax.optimization_barrier((qs, wind_u, wind_v))
    winds = wind_halos(wind_u, wind_v)
    qs, winds = lax.optimization_barrier((qs, winds))
    arrived = [lax.all_to_all(q, BOTH, split_axis=0, concat_axis=0, tiled=True) for q in qs]

    seen = lax.dynamic_slice_in_dim(
        gathered[:, lev // 2 + 1 : lev // 2 + 3, :], pos_x * count_y + pos_y, 1, axis=2
    )[:, :, 0].astype(jnp.int32)
    asked, counts = seen[:, 0], seen[:, 1]
    g1 = pl.pallas_call(
        columns_kernel,
        out_shape=jax.ShapeDtypeStruct((lev * nx, ny), F32),
        in_specs=[smem(), smem(), vmem(), vmem()],
        out_specs=vmem(),
        scratch_shapes=[pltpu.VMEM((lev * nx, ny), F32)],
        compiler_params=params(24),
        cost_estimate=pl.CostEstimate(flops=2**33, bytes_accessed=2**23, transcendentals=0),
        name="columns",
    )(asked, counts, gathered, increment).reshape(lev, nx, ny)
    select = (asked[:, None] == jnp.arange(1, nx + 1, dtype=jnp.int32)[None, :]).astype(BF16)

    length = filter_length
    fc = jnp.sqrt(-jnp.expm1(-2.0 / length))
    bc = -jnp.expm1(-1.0 / length)
    d = jnp.exp(-1.0 / length)

    def wide(columns, tail):
        got = jnp.stack(columns).reshape(len(columns), lev, *(1 for _ in tail))
        return jnp.broadcast_to(got, (len(columns), lev, *tail))

    coef_e = wide([d, fc, bc / fc, jnp.exp(-(nx + 1.0) / length), jnp.exp(1.0 / length)], (ny,))
    coef_f = wide([d, fc, bc], (ny,))
    jump, zero = jnp.exp(-nx / length), jnp.zeros_like(length)
    low = [entered(length, nx, float(i)) for i in range(3)]
    high = [entered(length, nx, float(nx - 3 + i)) for i in range(3)]
    low_b = [jnp.exp(-(nx - i) / length) for i in range(3)]
    high_b = [jnp.exp(-(3.0 - i) / length) for i in range(3)]
    kappa = entered(length, nx, 0.0)
    table_x = jnp.stack(
        [
            jnp.stack(line)
            for line in (
                [zero] * 3 + [jump] * 5,
                [jump] * 5 + [zero] * 3,
                [kappa] * 5 + [zero] * 3,
                low + [zero] * 5,
                low_b + [zero] * 5,
                [zero] * 5 + high,
                [zero] * 5 + high_b,
            )
        ]
    )
    table_x = jnp.transpose(table_x, (0, 2, 1))
    cells = jnp.arange(ny, dtype=F32)
    big = product(length[:, None, None], ny, cells[None, :, None], cells[None, None, :])
    nh, nl = split(big)
    edge = jnp.stack(
        [fc[:, None] * jnp.exp(-(ny - 1.0 - cells)[None] / length[:, None])]
        + [
            product(length[:, None], ny, float(i), cells[None, :])
            for i in (0, 1, 2, ny - 3, ny - 2, ny - 1)
        ]
        + [jnp.zeros((lev, ny), F32)],
        axis=1,
    )
    edge = jnp.concatenate(split(edge), axis=1)
    enter_a = entered(length[:, None], ny, cells[None, :])
    enter_b = jnp.exp(-(ny - cells)[None, :] / length[:, None])
    ah, al = split(enter_a)
    bh, bl = split(enter_b)
    none = jnp.zeros((lev, ny), BF16)
    place = jnp.stack([jnp.arange(ny) == k for k in (ny - 3, ny - 2, ny - 1, 0, 1, 2)]).astype(BF16)
    blank = jnp.zeros((8, ny), BF16)
    place = jnp.concatenate([blank, place, blank[:2]], axis=0)
    spread = jnp.concatenate(
        [
            jnp.stack([ah, ah, al, bh, bh, bl] + [none] * 10, axis=1),
            jnp.broadcast_to(place[None], (lev, 16, ny)),
        ],
        axis=2,
    )
    coef_y = wide(
        [jnp.exp(-ny / length), entered(length, ny, 0.0)]
        + [entered(length, ny, ny - 3.0 + i) for i in range(3)]
        + [jnp.exp(-(3.0 - i) / length) for i in range(3)]
        + [entered(length, ny, float(i)) for i in range(3)]
        + [jnp.exp(-(ny - float(i)) / length) for i in range(3)],
        (ny,),
    )
    halo_u, halo_v = padded_winds(wind_u, wind_v, winds)
    arrived, halo_u, halo_v, g1 = lax.optimization_barrier((arrived, halo_u, halo_v, g1))

    alpha = static = None
    for c in range(CHUNKS):
        g2 = jnp.einsum("sx,sly->lxy", select, arrived[c], preferred_element_type=F32)
        steps = part // 16
        off = c * steps
        h = pl.pallas_call(
            edges_kernel,
            grid=(steps,),
            in_specs=[
                pl.BlockSpec((16, nx, ny), lambda i, off=off: (off + i, 0, 0)),
                pl.BlockSpec((16, nx, ny), lambda i: (i, 0, 0)),
                pl.BlockSpec((members, 16, nx, ny), lambda i, off=off: (0, off + i, 0, 0)),
                pl.BlockSpec((5, 16, ny), lambda i, off=off: (0, off + i, 0)),
            ],
            out_specs=pl.BlockSpec((16, 16, ny), lambda i: (i, 0, 0)),
            out_shape=jax.ShapeDtypeStruct((part, 16, ny), F32),
            scratch_shapes=[pltpu.VMEM((16 * rows, ny), F32), pltpu.VMEM((16 * 16, ny), F32)],
            compiler_params=params(56),
            name=f"edges_{c}",
        )(g1, g2, ensemble, coef_e)
        h = lax.all_to_all(
            h.reshape(count_x, share, 16, ny), GX, split_axis=0, concat_axis=0, tiled=True
        )
        mine_x = lax.dynamic_slice_in_dim(table_x, c * part + pos_x * share, share, axis=1)
        mine_x = jnp.broadcast_to(mine_x[:, :, :, None], (7, share, 8, ny))
        h = pl.pallas_call(
            scan_x_kernel,
            out_shape=jax.ShapeDtypeStruct(h.shape, F32),
            in_specs=[vmem(), vmem()],
            out_specs=vmem(),
            name=f"scan_x_{c}",
        )(h, mine_x)
        h = lax.all_to_all(h, GX, split_axis=0, concat_axis=0, tiled=True).reshape(part, 16, ny)
        hi, lo, es, to_right, to_left = pl.pallas_call(
            filter_x_kernel,
            grid=(steps,),
            in_specs=[
                pl.BlockSpec((16, nx, ny), lambda i, off=off: (off + i, 0, 0)),
                pl.BlockSpec((16, nx, ny), lambda i: (i, 0, 0)),
                pl.BlockSpec((members, 16, nx, ny), lambda i, off=off: (0, off + i, 0, 0)),
                pl.BlockSpec((16, 16, ny), lambda i: (i, 0, 0)),
                pl.BlockSpec((3, 16, ny), lambda i, off=off: (0, off + i, 0)),
                pl.BlockSpec((16, 16, ny), lambda i, off=off: (off + i, 0, 0)),
            ],
            out_specs=(
                pl.BlockSpec((16, deep, ny), lambda i: (i, 0, 0)),
                pl.BlockSpec((16, deep, ny), lambda i: (i, 0, 0)),
                pl.BlockSpec((count_y, 2, 16, deep), lambda i: (0, 0, i, 0)),
                pl.BlockSpec((3, 16, ny), lambda i: (0, i, 0)),
                pl.BlockSpec((3, 16, ny), lambda i: (0, i, 0)),
            ),
            out_shape=(
                jax.ShapeDtypeStruct((part, deep, ny), BF16),
                jax.ShapeDtypeStruct((part, deep, ny), BF16),
                jax.ShapeDtypeStruct((count_y, 2, part, deep), BF16),
                jax.ShapeDtypeStruct((3, part, ny), BF16),
                jax.ShapeDtypeStruct((3, part, ny), BF16),
            ),
            scratch_shapes=[
                pltpu.VMEM((16 * rows, ny), F32),
                pltpu.VMEM((16 * (deep + 8), ny), F32),
                pltpu.VMEM((16 * 16, ny), F32),
                pltpu.VMEM((16 * 16, ny), F32),
            ],
            compiler_params=params(56),
            name=f"filter_x_{c}",
        )(g1, g2, ensemble, h, coef_f, edge)
        es = lax.all_to_all(es, GY, split_axis=0, concat_axis=0, tiled=True)
        from_left = from_before(to_right, GY)
        from_right = from_after(to_left, GY)
        fb = pl.pallas_call(
            scan_y_kernel,
            out_shape=jax.ShapeDtypeStruct((part * 16, deep), BF16),
            in_specs=[smem()] + [vmem()] * 4,
            out_specs=vmem(),
            scratch_shapes=[
                pltpu.VMEM((count_y, part, deep), F32),
                pltpu.VMEM((count_y, part, deep), F32),
                pltpu.VMEM((2, part * 16, deep // 2), F32),
            ],
            compiler_params=params(16),
            name=f"scan_y_{c}",
        )(pos_y.reshape(1), es, from_left, from_right, coef_y[:, c * part : (c + 1) * part])
        steps = part // 8
        off = c * steps
        extra = () if c == 0 else (alpha, static)
        alpha, static = pl.pallas_call(
            final_kernel,
            grid=(steps,),
            in_specs=[
                pl.BlockSpec((8, deep, ny), lambda i: (i, 0, 0)),
                pl.BlockSpec((8, deep, ny), lambda i: (i, 0, 0)),
                pl.BlockSpec((8, ny, ny), lambda i, off=off: (off + i, 0, 0)),
                pl.BlockSpec((8, ny, ny), lambda i, off=off: (off + i, 0, 0)),
                pl.BlockSpec((8 * 16, deep), lambda i: (i, 0)),
                pl.BlockSpec((8, 16, 2 * ny), lambda i, off=off: (off + i, 0, 0)),
                pl.BlockSpec((8, nx + 8, 2 * ny), lambda i, off=off: (off + i, 0, 0)),
                pl.BlockSpec((8, nx + 8, 2 * ny), lambda i, off=off: (off + i, 0, 0)),
            ]
            + [pl.BlockSpec(memory_space=pl.ANY)] * len(extra),
            out_specs=(
                pl.BlockSpec((members, 8, nx, ny), lambda i, off=off: (0, off + i, 0, 0)),
                pl.BlockSpec((8, nx, ny), lambda i, off=off: (off + i, 0, 0)),
            ),
            out_shape=(
                jax.ShapeDtypeStruct((members, lev, nx, ny), F32),
                jax.ShapeDtypeStruct((lev, nx, ny), F32),
            ),
            input_output_aliases={8: 0, 9: 1} if extra else {},
            compiler_params=params(56),
            name=f"final_{c}",
        )(hi, lo, nh, nl, fb, spread, halo_u, halo_v, *extra)
    return alpha, static


def solution(mesh):
    grid = P(None, GX, GY)
    placed = (
        grid,
        P(None, None, GX, GY),
        grid,
        grid,
        P(),
        P(BOTH, None, None),
        P(BOTH, None),
        P(BOTH, None, None),
        P(BOTH),
        P(BOTH),
        P(BOTH),
    )
    return jax.shard_map(
        body,
        mesh=mesh,
        in_specs=placed,
        out_specs=(P(None, None, GX, GY), grid),
        check_vma=False,
    )
```

time: 381 us -> 190 us (0.50); the launches traced: 374 us -> 188 us
  blocking collectives: 92.7 us -> 0 us
  Pallas kernels: 0 us -> 72.5 us
  local copies, waits for them, and re-layouts: 66.5 us -> 9.2 us
  matrix products: 53.4 us -> 4.13 us
  waiting for transfers between devices: 64.9 us -> 38.7 us
  other arithmetic: 28.9 us -> 9.53 us
  starting transfers between devices: 65.1 us -> 52.9 us
    pallas_call x0 -> x11, Pallas kernels: none -> 72.5 us  [the longest x1 16.2 us: body(): pl.pallas_call(final_kernel, grid=(steps,), in_specs=[pl.BlockSpec((8, de...]
    all_gather x6 -> x0, blocking collectives: 58.3 us -> none  [carried_in(): pieces = jax.tree.map(lambda part: lax.all_gather(part, axis), subtotal)]
    dot_general x8 -> x1, matrix products: 53.4 us -> 4.13 us  [body(): jnp.einsum('sx,sly->lxy', select, arrived[c], preferred_element_type=F32)]
    slice x37 -> x2, local copies, waits for them, and re-layouts: 30.3 us -> 0.07 us  [the longest x1 0.07 us: body(): gathered[:, lev // 2 + 1:lev // 2 + 3, :]]
    all_to_all x1 -> x0, blocking collectives: 20.9 us -> none  [trade_lines(): lax.all_to_all(requests, GX_GY, split_axis=0, concat_axis=0, tiled=True)]
    all_to_all x2 -> x1, waiting for transfers between devices: 20.3 us -> 0.01 us  [sent_to_all(): return lax.all_to_all(copies, axis, split_axis=0, concat_axis=0, tiled=True)]
    unnamed x34 -> x26, local copies, waits for them, and re-layouts: 20 us -> 2.7 us
    unnamed x1 -> x0, blocking collectives: 13.6 us -> none
  transfers between devices with their start and end apart: 16 -> 11, of which waited for: 8 -> 8; matrix products, arithmetic and copies ran while one was open for 6% -> 5% of each run, Pallas kernels for 0% -> 19%
where the time goes in v1:
time: 190 us; the launch traced here: 188 us
  Pallas kernels  72.5 us (38%)
  starting transfers between devices  52.9 us (28%)
  waiting for transfers between devices  38.7 us (20%)
  other arithmetic  9.53 us (5%)
  local copies, waits for them, and re-layouts  9.2 us (5%)
  matrix products  4.13 us (2%)
    pallas_call x1, Pallas kernels, body(): pl.pallas_call(final_kernel, grid=(steps,), in_specs=[pl.BlockSpec((8, de...  16.2 us
    pallas_call x1, Pallas kernels, body(): pl.pallas_call(columns_kernel, out_shape=jax.ShapeDtypeStruct((lev * nx,...  14 us
    all_to_all x1, starting transfers between devices, sent_to_all(): return lax.all_to_all(copies, axis, split_axis=0, concat_axis=0, tiled=True)  11.5 us
    ppermute x3, starting transfers between devices, from_before(): return lax.ppermute(array, axis, [(i, i + 1) for i in range(count - 1)])  11.3 us
    all_to_all x1, starting transfers between devices, body(): lax.all_to_all(q, BOTH, split_axis=0, concat_axis=0, tiled=True)  11.3 us
    ppermute x3, waiting for transfers between devices, from_after(): return lax.ppermute(array, axis, [(i + 1, i) for i in range(count - 1)])  11 us
    pallas_call x1, Pallas kernels, body(): pl.pallas_call(filter_x_kernel, grid=(steps,), in_specs=[pl.BlockSpec((16...  10 us
    pallas_call x1, Pallas kernels, body(): pl.pallas_call(records_kernel, grid_spec=pltpu.PrefetchScalarGridSpec(num...  9.71 us
  transfers between devices with their start and end apart: 11, of which 8 were waited for; matrix products, arithmetic and copies ran while one was open for 5% of the time, Pallas kernels for 19%

profile of v1, /device:TPU:1, one launch (start us, length us, event | category | flops | bytes accessed | tf_op | source)
XLA Modules:
  0.0 188.1 jit_solution(17671568806161947788)
XLA Ops:
  6.4 11.5 %all-to-all-start.1 = ((bf16[128,48,128]{2,1,0:T(8,128)(2,1)}), bf16[128,48,128]{2,1,0:T(8,128)(2,1)S(1)}, u32[]{:S(2)}, u32[]{:S(2)}) async-start(bf16[128,48,128]{2,1,0:T(8,128)(2,1)} %broadcast_in_dim.14), calls=%async_computation.1 | async-start | bytes 3145728 | tf_op jit(solution)/shard_map/all_to_all | solution.py:357
  18.0 9.7 %records.1 = bf16[128,64,128]{2,1,0:T(8,128)(2,1)} custom-call(s32[64]{0:T(128)} %home_ref.1, s32[64]{0:T(128)} %count_ref.1, bf16[128,512]{1,0:T(8,128)(2,1)} %get-tuple-element.27.b_ref, bf16[64,512,128]{2,1,0:T(8,128)(2,1)} %dep_ref.1), custom_call_target="tpu_custom_call" | custom-call | tf_op jit(solution)/shard_map/records/pallas_call | solution.py:526
  27.7 3.5 %wind_rows.1 = (bf16[64,16,128]{2,1,0:T(8,128)(2,1)}, bf16[64,16,128]{2,1,0:T(8,128)(2,1)}) custom-call(bf16[64,48,128]{2,1,0:T(8,128)(2,1)} %u_ref.2, bf16[64,48,128]{2,1,0:T(8,128)(2,1)} %v_ref.2), custom_call_target="tpu_custom_call" | custom-call | tf_op jit(solution)/shard_map/wind_rows/pallas_call | solution.py:425
  31.1 3.3 %collective-permute-start = (bf16[64,16,128]{2,1,0:T(8,128)(2,1)}, bf16[64,16,128]{2,1,0:T(8,128)(2,1)S(1)}, u32[]{:S(2)}, u32[]{:S(2)}) collective-permute-start(bf16[64,16,128]{2,1,0:T(8,128)(2,1)} %get-tuple-element.31), channel_id=1, source_target_pairs={{0,8},{8,16},{16,24},{24,32},{32,40},{40,48},{48,56},{56,64},{64,7... | collective-permute-start | bytes 786440 | tf_op jit(solution)/shard_map/ppermute | solution.py:362
  40.0 3.7 %collective-permute-done.1.after_ref = bf16[64,16,128]{2,1,0:T(8,128)(2,1)S(1)} collective-permute-done((bf16[64,16,128]{2,1,0:T(8,128)(2,1)}, bf16[64,16,128]{2,1,0:T(8,128)(2,1)S(1)}, u32[]{:S(2)}, u32[]{:S(2)}) %collective-permute-start.1) | collective-permute-done | bytes 262176 | tf_op jit(solution)/shard_map/ppermute | solution.py:367
  44.5 4.3 %wind_columns.1 = (bf16[64,16,64]{2,1,0:T(8,128)(2,1)}, bf16[64,16,64]{2,1,0:T(8,128)(2,1)}) custom-call(bf16[64,48,128]{2,1,0:T(8,128)(2,1)} %u_ref.2, bf16[64,48,128]{2,1,0:T(8,128)(2,1)} %v_ref.2, bf16[64,16,128]{2,1,0:T(8,128)(2,1)} %copy-done.5, bf16[64,16,128]{2,1,0:T(8,128)(2,1)} %copy-done.6, bf16[16,128]{1,0:T(8,128)(2,1)} %constant.27.clone.pick_ref), custom_call_target="tpu_custom_call" | custom-call | tf_op jit(solution)/shard_map/wind_columns/pallas_call | solution.py:437
  48.8 4.5 %collective-permute-start.2 = (bf16[64,16,64]{2,1,0:T(8,128)(2,1)}, bf16[64,16,64]{2,1,0:T(8,128)(2,1)S(1)}, u32[]{:S(2)}, u32[]{:S(2)}) collective-permute-start(bf16[64,16,64]{2,1,0:T(8,128)(2,1)} %get-tuple-element.33), channel_id=1, source_target_pairs={{0,1},{1,2},{2,3},{3,4},{4,5},{5,6},{6,7},{8,9},{9,10},{10,11},{11... | collective-permute-start | bytes 393224 | tf_op jit(solution)/shard_map/ppermute | solution.py:362
  56.9 4.3 %collective-permute-done.3.right_ref = bf16[64,16,64]{2,1,0:T(8,128)(2,1)S(1)} collective-permute-done((bf16[64,16,64]{2,1,0:T(8,128)(2,1)}, bf16[64,16,64]{2,1,0:T(8,128)(2,1)S(1)}, u32[]{:S(2)}, u32[]{:S(2)}) %collective-permute-start.3) | collective-permute-done | bytes 131104 | tf_op jit(solution)/shard_map/ppermute | solution.py:367
  61.2 11.3 %all-to-all-start = ((bf16[128,64,128]{2,1,0:T(8,128)(2,1)}), bf16[128,64,128]{2,1,0:T(8,128)(2,1)}, u32[]{:S(2)}, u32[]{:S(2)}) async-start(bf16[128,64,128]{2,1,0:T(8,128)(2,1)} %records.1), calls=%async_computation | async-start | bytes 4194304 | tf_op jit(solution)/shard_map/all_to_all | solution.py:544
  72.5 4.1 %subtract_convert_fusion = (bf16[64,128,128]{2,1,0:T(8,128)(2,1)}, bf16[64,128,128]{2,1,0:T(8,128)(2,1)}) fusion(f32[128,128]{1,0:T(8,128)S(1)} %get-tuple-element.135, f32[64]{0:T(128)S(1)} %copy-done.9, f32[128,128]{1,0:T(8,128)S(1)} %get-tuple-element.136, f32[64]{0:T(128)S(1)} %get-tuple-element.95), kind=kLoop, calls=%fused_computation.5 | loop fusion | flops 9437184 | bytes 4325888 | tf_op jit(solution)/shard_map/convert_element_type | solution.py:35
  76.6 4.9 %wind_pad.1 = (bf16[64,56,256]{2,1,0:T(8,128)(2,1)}, bf16[64,56,256]{2,1,0:T(8,128)(2,1)}) custom-call(bf16[64,48,128]{2,1,0:T(8,128)(2,1)} %u_ref.2, bf16[64,48,128]{2,1,0:T(8,128)(2,1)} %v_ref.2, bf16[64,16,128]{2,1,0:T(8,128)(2,1)} %copy-done.5, bf16[64,16,128]{2,1,0:T(8,128)(2,1)} %copy-done.6, bf16[64,16,64]{2,1,0:T(8,128)(2,1)} %copy-done.7, ...), custom_call_target="tpu_custom_call" | custom-call | tf_op jit(solution)/shard_map/wind_pad/pallas_call | solution.py:455
  81.9 14.0 %columns.1 = f32[3072,128]{1,0:T(8,128)S(1)} custom-call(s32[128]{0:T(128)S(1)} %get-tuple-element.106.line_ref, s32[128]{0:T(128)S(1)} %get-tuple-element.105.count_ref, bf16[128,48,128]{2,1,0:T(8,128)(2,1)S(1)} %all-to-all-done.1.gathered_ref, bf16[64,48,128]{2,1,0:T(8,128)(2,1)S(1)} %copy-done.2), custom_call_target="tpu_custom_call" | custom-call | flops 8589934592 | bytes 8388608 | tf_op jit(solution)/shard_map/columns/pallas_call | solution.py:550
  97.0 5.6 %all-to-all-done = bf16[128,64,128]{2,1,0:T(8,128)(2,1)} async-done(((bf16[128,64,128]{2,1,0:T(8,128)(2,1)}), bf16[128,64,128]{2,1,0:T(8,128)(2,1)}, u32[]{:S(2)}, u32[]{:S(2)}) %all-to-all-start) | async-done | bytes 2097184 | tf_op jit(solution)/shard_map/all_to_all | solution.py:544
  102.7 4.1 %fusion.6.g2_ref = f32[64,48,128]{2,1,0:T(8,128)} fusion(bf16[128,64,128]{2,1,0:T(8,128)(2,1)} %all-to-all-done, s32[128]{0:T(128)S(1)} %get-tuple-element.106.line_ref, s32[48]{0:T(128)S(1)} %iota_add_fusion), kind=kOutput, calls=%fused_computation.9 | convolution fusion | flops 100669440 | bytes 3670720 | tf_op jit(solution)/shard_map/sx,sly->lxy/dot_general | solution.py:635
  107.6 5.4 %edges_0.1 = f32[64,16,128]{2,1,0:T(8,128)} custom-call(f32[64,48,128]{2,1,0:T(8,128)} %bitcast.91, f32[64,48,128]{2,1,0:T(8,128)} %fusion.6.g2_ref, bf16[4,64,48,128]{3,2,1,0:T(8,128)(2,1)} %ens_ref.3, f32[5,64,128]{2,1,0:T(8,128)} %broadcast_in_dim.15.coef_ref), custom_call_target="tpu_custom_call" | custom-call | tf_op jit(solution)/shard_map/edges_0/pallas_call | solution.py:638
  113.0 3.6 %all-to-all-start.2 = ((f32[16,4,16,128]{3,2,1,0:T(8,128)}), f32[16,4,16,128]{3,2,1,0:T(8,128)S(1)}, u32[]{:S(2)}, u32[]{:S(2)}) async-start(f32[16,4,16,128]{3,2,1,0:T(8,128)} %bitcast.94), calls=%async_computation.2 | async-start | bytes 1048576 | tf_op jit(solution)/shard_map/all_to_all | solution.py:653
  117.3 9.7 %all-to-all-done.2.in_ref = f32[16,4,16,128]{3,2,1,0:T(8,128)S(1)} async-done(((f32[16,4,16,128]{3,2,1,0:T(8,128)}), f32[16,4,16,128]{3,2,1,0:T(8,128)S(1)}, u32[]{:S(2)}, u32[]{:S(2)}) %all-to-all-start.2) | async-done | bytes 524320 | tf_op jit(solution)/shard_map/all_to_all | solution.py:653
  129.8 3.8 %all-to-all-start.3 = ((f32[16,4,16,128]{3,2,1,0:T(8,128)}), f32[16,4,16,128]{3,2,1,0:T(8,128)S(1)}, u32[]{:S(2)}, u32[]{:S(2)}) async-start(f32[16,4,16,128]{3,2,1,0:T(8,128)} %scan_x_0.1), calls=%async_computation.3 | async-start | bytes 1048576 | tf_op jit(solution)/shard_map/all_to_all | solution.py:665
  134.8 8.1 %all-to-all-done.3 = f32[16,4,16,128]{3,2,1,0:T(8,128)S(1)} async-done(((f32[16,4,16,128]{3,2,1,0:T(8,128)}), f32[16,4,16,128]{3,2,1,0:T(8,128)S(1)}, u32[]{:S(2)}, u32[]{:S(2)}) %all-to-all-start.3) | async-done | bytes 524320 | tf_op jit(solution)/shard_map/all_to_all | solution.py:665
  143.8 10.0 %filter_x_0.1 = (bf16[64,256,128]{2,1,0:T(8,128)(2,1)}, bf16[64,256,128]{2,1,0:T(8,128)(2,1)}, bf16[8,2,64,256]{3,2,1,0:T(8,128)(2,1)}, bf16[3,64,128]{2,1,0:T(8,128)(2,1)}, bf16[3,64,128]{2,1,0:T(8,128)(2,1)}) custom-call(f32[64,48,128]{2,1,0:T(8,128)} %bitcast.92, f32[64,48,128]{2,1,0:T(8,128)} %fusion.6.g2_ref, bf16[4,64,48,128]{3,2,1,0:T(8,128)(2,1)} %ens_ref.3, ...), custom_call_target="tpu_custom_call" | custom-call | tf_op jit(solution)/shard_map/filter_x_0/pallas_call | solution.py:666
  153.8 6.4 %all-to-all-start.4 = ((bf16[8,2,64,256]{3,2,1,0:T(8,128)(2,1)}), bf16[8,2,64,256]{3,2,1,0:T(8,128)(2,1)S(1)}, u32[]{:S(2)}, u32[]{:S(2)}) async-start(bf16[8,2,64,256]{3,2,1,0:T(8,128)(2,1)} %get-tuple-element.47), calls=%async_computation.4 | async-start | bytes 1048576 | tf_op jit(solution)/shard_map/all_to_all | solution.py:700
  160.8 3.5 %collective-permute-start.4 = (bf16[3,64,128]{2,1,0:T(8,128)(2,1)}, bf16[3,64,128]{2,1,0:T(8,128)(2,1)S(1)}, u32[]{:S(2)}, u32[]{:S(2)}) collective-permute-start(bf16[3,64,128]{2,1,0:T(8,128)(2,1)} %get-tuple-element.48), channel_id=1, source_target_pairs={{0,1},{1,2},{2,3},{3,4},{4,5},{5,6},{6,7},{8,9},{9,10},{10,11},{11... | collective-permute-start | bytes 147464 | tf_op jit(solution)/shard_map/ppermute | solution.py:362
  167.2 3.0 %collective-permute-done.5.fr_ref = bf16[3,64,128]{2,1,0:T(8,128)(2,1)S(1)} collective-permute-done((bf16[3,64,128]{2,1,0:T(8,128)(2,1)}, bf16[3,64,128]{2,1,0:T(8,128)(2,1)S(1)}, u32[]{:S(2)}, u32[]{:S(2)}) %collective-permute-start.5) | collective-permute-done | bytes 49184 | tf_op jit(solution)/shard_map/ppermute | solution.py:367
  171.9 16.2 %final_0.1 = (f32[4,64,48,128]{3,2,1,0:T(8,128)}, f32[64,48,128]{2,1,0:T(8,128)}) custom-call(bf16[64,256,128]{2,1,0:T(8,128)(2,1)} %get-tuple-element.45.hi_ref, bf16[64,256,128]{2,1,0:T(8,128)(2,1)} %get-tuple-element.46.lo_ref, bf16[64,128,128]{2,1,0:T(8,128)(2,1)} %get-tuple-element.80.nh_ref, bf16[64,128,128]{2,1,0:T(8,128)(2,1)} %get-tuple-element.79.nl_ref, ...), custom_call_target="tpu_custom_call" | custom-call | tf_op jit(solution)/shard_map/final_0/pallas_call | solution.py:719
  (105 shorter events, 28.5 us)
Async XLA Ops:
  6.4 54.8 %all-to-all-start.1 = ((bf16[128,48,128]{2,1,0:T(8,128)(2,1)}), bf16[128,48,128]{2,1,0:T(8,128)(2,1)S(1)}, u32[]{:S(2)}, u32[]{:S(2)}) async-start(bf16[128,48,128]{2,1,0:T(8,128)(2,1)} %broadcast_in_dim.14), calls=%async_computation.1 | async-start | bytes 3145728 | tf_op jit(solution)/shard_map/all_to_all | solution.py:357
  17.9 17.9 %copy-start.9 = (f32[64]{0:T(128)S(1)}, f32[64]{0:T(128)}, u32[]{:S(2)}) copy-start(f32[64]{0:T(128)} %param.17) | copy-start | bytes 772
  31.1 8.9 %collective-permute-start = (bf16[64,16,128]{2,1,0:T(8,128)(2,1)}, bf16[64,16,128]{2,1,0:T(8,128)(2,1)S(1)}, u32[]{:S(2)}, u32[]{:S(2)}) collective-permute-start(bf16[64,16,128]{2,1,0:T(8,128)(2,1)} %get-tuple-element.31), channel_id=1, source_target_pairs={{0,8},{8,16},{16,24},{24,32},{32,40},{40,48},{48,56},{56,64},{64,7... | collective-permute-start | bytes 786440 | tf_op jit(solution)/shard_map/ppermute | solution.py:362
  34.4 9.3 %collective-permute-start.1 = (bf16[64,16,128]{2,1,0:T(8,128)(2,1)}, bf16[64,16,128]{2,1,0:T(8,128)(2,1)S(1)}, u32[]{:S(2)}, u32[]{:S(2)}) collective-permute-start(bf16[64,16,128]{2,1,0:T(8,128)(2,1)} %get-tuple-element.32), channel_id=1, source_target_pairs={{8,0},{16,8},{24,16},{32,24},{40,32},{48,40},{56,48},{64,56},{72,6... | collective-permute-start | bytes 786440 | tf_op jit(solution)/shard_map/ppermute | solution.py:367
  40.0 3.7 %copy-start.5 = (bf16[64,16,128]{2,1,0:T(8,128)(2,1)}, bf16[64,16,128]{2,1,0:T(8,128)(2,1)S(1)}, u32[]{:S(2)}) copy-start(bf16[64,16,128]{2,1,0:T(8,128)(2,1)S(1)} %collective-permute-done.before_ref) | copy-start | bytes 786436
  43.7 0.7 copy-start.6
  48.8 8.1 %collective-permute-start.2 = (bf16[64,16,64]{2,1,0:T(8,128)(2,1)}, bf16[64,16,64]{2,1,0:T(8,128)(2,1)S(1)}, u32[]{:S(2)}, u32[]{:S(2)}) collective-permute-start(bf16[64,16,64]{2,1,0:T(8,128)(2,1)} %get-tuple-element.33), channel_id=1, source_target_pairs={{0,1},{1,2},{2,3},{3,4},{4,5},{5,6},{6,7},{8,9},{9,10},{10,11},{11... | collective-permute-start | bytes 393224 | tf_op jit(solution)/shard_map/ppermute | solution.py:362
  53.3 7.9 %collective-permute-start.3 = (bf16[64,16,64]{2,1,0:T(8,128)(2,1)}, bf16[64,16,64]{2,1,0:T(8,128)(2,1)S(1)}, u32[]{:S(2)}, u32[]{:S(2)}) collective-permute-start(bf16[64,16,64]{2,1,0:T(8,128)(2,1)} %get-tuple-element.34), channel_id=1, source_target_pairs={{1,0},{2,1},{3,2},{4,3},{5,4},{6,5},{7,6},{9,8},{10,9},{11,10},{12... | collective-permute-start | bytes 393224 | tf_op jit(solution)/shard_map/ppermute | solution.py:367
  56.9 19.7 %copy-start.7 = (bf16[64,16,64]{2,1,0:T(8,128)(2,1)}, bf16[64,16,64]{2,1,0:T(8,128)(2,1)S(1)}, u32[]{:S(2)}) copy-start(bf16[64,16,64]{2,1,0:T(8,128)(2,1)S(1)} %collective-permute-done.2.left_ref) | copy-start | bytes 393220
  61.2 15.4 %copy-start.8 = (bf16[64,16,64]{2,1,0:T(8,128)(2,1)}, bf16[64,16,64]{2,1,0:T(8,128)(2,1)S(1)}, u32[]{:S(2)}) copy-start(bf16[64,16,64]{2,1,0:T(8,128)(2,1)S(1)} %collective-permute-done.3.right_ref) | copy-start | bytes 393220
  61.2 41.5 %all-to-all-start = ((bf16[128,64,128]{2,1,0:T(8,128)(2,1)}), bf16[128,64,128]{2,1,0:T(8,128)(2,1)}, u32[]{:S(2)}, u32[]{:S(2)}) async-start(bf16[128,64,128]{2,1,0:T(8,128)(2,1)} %records.1), calls=%async_computation | async-start | bytes 4194304 | tf_op jit(solution)/shard_map/all_to_all | solution.py:544
  72.5 9.4 %copy-start.2 = (bf16[64,48,128]{2,1,0:T(8,128)(2,1)S(1)}, bf16[64,48,128]{2,1,0:T(8,128)(2,1)}, u32[]{:S(2)}) copy-start(bf16[64,48,128]{2,1,0:T(8,128)(2,1)} %inc_ref.1) | copy-start | bytes 2359300
  95.9 1.1 copy-start
  113.0 14.0 %all-to-all-start.2 = ((f32[16,4,16,128]{3,2,1,0:T(8,128)}), f32[16,4,16,128]{3,2,1,0:T(8,128)S(1)}, u32[]{:S(2)}, u32[]{:S(2)}) async-start(f32[16,4,16,128]{3,2,1,0:T(8,128)} %bitcast.94), calls=%async_computation.2 | async-start | bytes 1048576 | tf_op jit(solution)/shard_map/all_to_all | solution.py:653
  127.0 0.9 copy-start.4
  129.8 13.1 %all-to-all-start.3 = ((f32[16,4,16,128]{3,2,1,0:T(8,128)}), f32[16,4,16,128]{3,2,1,0:T(8,128)S(1)}, u32[]{:S(2)}, u32[]{:S(2)}) async-start(f32[16,4,16,128]{3,2,1,0:T(8,128)} %scan_x_0.1), calls=%async_computation.3 | async-start | bytes 1048576 | tf_op jit(solution)/shard_map/all_to_all | solution.py:665
  143.0 0.8 copy-start.3
  153.8 16.4 %all-to-all-start.4 = ((bf16[8,2,64,256]{3,2,1,0:T(8,128)(2,1)}), bf16[8,2,64,256]{3,2,1,0:T(8,128)(2,1)S(1)}, u32[]{:S(2)}, u32[]{:S(2)}) async-start(bf16[8,2,64,256]{3,2,1,0:T(8,128)(2,1)} %get-tuple-element.47), calls=%async_computation.4 | async-start | bytes 1048576 | tf_op jit(solution)/shard_map/all_to_all | solution.py:700
  160.8 6.5 %collective-permute-start.4 = (bf16[3,64,128]{2,1,0:T(8,128)(2,1)}, bf16[3,64,128]{2,1,0:T(8,128)(2,1)S(1)}, u32[]{:S(2)}, u32[]{:S(2)}) collective-permute-start(bf16[3,64,128]{2,1,0:T(8,128)(2,1)} %get-tuple-element.48), channel_id=1, source_target_pairs={{0,1},{1,2},{2,3},{3,4},{4,5},{5,6},{6,7},{8,9},{9,10},{10,11},{11... | collective-permute-start | bytes 147464 | tf_op jit(solution)/shard_map/ppermute | solution.py:362
  164.3 5.9 %collective-permute-start.5 = (bf16[3,64,128]{2,1,0:T(8,128)(2,1)}, bf16[3,64,128]{2,1,0:T(8,128)(2,1)S(1)}, u32[]{:S(2)}, u32[]{:S(2)}) collective-permute-start(bf16[3,64,128]{2,1,0:T(8,128)(2,1)} %get-tuple-element.49), channel_id=1, source_target_pairs={{1,0},{2,1},{3,2},{4,3},{5,4},{6,5},{7,6},{9,8},{10,9},{11,10},{12... | collective-permute-start | bytes 147464 | tf_op jit(solution)/shard_map/ppermute | solution.py:367
  171.1 0.8 copy-start.1

commit v2 on v1

--- a/solution.py
+++ b/solution.py
@@ -48,12 +48,17 @@
     packed = jnp.where(col >= row, high, a - high)
     diagonal = jnp.sum(jnp.where(col == row, a - high, 0.0), axis=0, keepdims=True)
     half = lev // 2
-    out_ref[:half] = jnp.concatenate([packed[:half], packed[half:]], axis=1).astype(BF16)
+    packed = jnp.concatenate([packed[:half], packed[half:]], axis=1)
     meta = meta_ref[...].astype(F32)
     first = lax.broadcasted_iota(jnp.int32, meta.shape, 0) == 0
-    out_ref[half:] = jnp.where(
-        first, jnp.concatenate([diagonal, jnp.zeros_like(diagonal)], axis=1), meta
-    ).astype(BF16)
+    meta = jnp.where(first, jnp.concatenate([diagonal, jnp.zeros_like(diagonal)], axis=1), meta)
+    whole = jnp.concatenate([packed, meta], axis=0).astype(BF16)
+
+    def copy(k, carry):
+        out_ref[k] = whole
+        return carry
+
+    lax.fori_loop(0, out_ref.shape[0], copy, 0, unroll=8)
 
 
 def records_kernel(home_ref, count_ref, b_ref, dep_ref, *outs):
@@ -352,11 +357,6 @@
         static_ref[l] = s[:nx, :ny]
 
 
-def sent_to_all(array, axis):
-    copies = jnp.broadcast_to(array[None], (lax.axis_size(axis), *array.shape))
-    return lax.all_to_all(copies, axis, split_axis=0, concat_axis=0, tiled=True)
-
-
 def from_before(array, axis):
     count = lax.axis_size(axis)
     return lax.ppermute(array, axis, [(i, i + 1) for i in range(count - 1)])
@@ -418,9 +418,8 @@
     return pl.BlockSpec(shape, lambda i: tuple(0 for _ in shape))
 
 
-def wind_halos(wind_u, wind_v):
+def wind_ends(wind_u, wind_v):
     lev, nx, ny = wind_u.shape
-    deep = nx + 16
     steps = (lev // 16,)
     first, last = pl.pallas_call(
         wind_rows_kernel,
@@ -428,9 +427,16 @@
         in_specs=[levels(nx, ny)] * 2,
         out_specs=(levels(16, ny),) * 2,
         out_shape=(jax.ShapeDtypeStruct((lev, 16, ny), BF16),) * 2,
+        compiler_params=params(8),
         name="wind_rows",
     )(wind_u, wind_v)
-    before, after = from_before(last, GX), from_after(first, GX)
+    return from_before(last, GX), from_after(first, GX)
+
+
+def wind_sides(wind_u, wind_v, before, after):
+    lev, nx, ny = wind_u.shape
+    deep = nx + 16
+    steps = (lev // 16,)
     pick = np.zeros((16, ny), np.float32)
     for k in range(3):
         pick[k, ny - 3 + k] = pick[8 + k, k] = 1
@@ -440,9 +446,10 @@
         in_specs=[levels(nx, ny)] * 2 + [levels(16, ny)] * 2 + [whole(16, ny)],
         out_specs=(levels(16, deep),) * 2,
         out_shape=(jax.ShapeDtypeStruct((lev, 16, deep), BF16),) * 2,
+        compiler_params=params(8),
         name="wind_columns",
     )(wind_u, wind_v, before, after, jnp.asarray(pick, BF16))
-    return before, after, from_before(right, GY), from_after(left, GY)
+    return from_before(right, GY), from_after(left, GY)
 
 
 def padded_winds(wind_u, wind_v, halos):
@@ -461,6 +468,7 @@
         + [whole(32, 2 * ny)],
         out_specs=(levels(nx + 8, 2 * ny),) * 2,
         out_shape=(jax.ShapeDtypeStruct((lev, nx + 8, 2 * ny), BF16),) * 2,
+        compiler_params=params(8),
         name="wind_pad",
     )(wind_u, wind_v, *halos, jnp.asarray(place, BF16))
 
@@ -514,13 +522,14 @@
         sensor_kernel,
         out_shape=(
             jax.ShapeDtypeStruct((2 * lev, channels), BF16),
-            jax.ShapeDtypeStruct((lev // 2 + 16, 2 * lev), BF16),
+            jax.ShapeDtypeStruct((homes, lev // 2 + 16, 2 * lev), BF16),
         ),
         in_specs=[vmem()] * 3,
         out_specs=(vmem(), vmem()),
+        compiler_params=params(8),
         name="sensor",
     )(jt, obs_weight, meta)
-    gathered = sent_to_all(mine, BOTH)
+    gathered = lax.all_to_all(mine, BOTH, split_axis=0, concat_axis=0, tiled=True)
 
     per = min(8, records)
     qs = pl.pallas_call(
@@ -539,8 +548,8 @@
         name="records",
     )(obs_home, obs_count, b, departure)
     qs, wind_u, wind_v = lax.optimization_barrier((qs, wind_u, wind_v))
-    winds = wind_halos(wind_u, wind_v)
-    qs, winds = lax.optimization_barrier((qs, winds))
+    before, after = wind_ends(wind_u, wind_v)
+    qs, before, after = lax.optimization_barrier((qs, before, after))
     arrived = [lax.all_to_all(q, BOTH, split_axis=0, concat_axis=0, tiled=True) for q in qs]
 
     seen = lax.dynamic_slice_in_dim(
@@ -553,7 +562,7 @@
         in_specs=[smem(), smem(), vmem(), vmem()],
         out_specs=vmem(),
         scratch_shapes=[pltpu.VMEM((lev * nx, ny), F32)],
-        compiler_params=params(24),
+        compiler_params=params(12),
         cost_estimate=pl.CostEstimate(flops=2**33, bytes_accessed=2**23, transcendentals=0),
         name="columns",
     )(asked, counts, gathered, increment).reshape(lev, nx, ny)
@@ -627,7 +636,9 @@
         + [jnp.exp(-(ny - float(i)) / length) for i in range(3)],
         (ny,),
     )
-    halo_u, halo_v = padded_winds(wind_u, wind_v, winds)
+    sides = wind_sides(wind_u, wind_v, before, after)
+    g1, *sides = lax.optimization_barrier((g1, *sides))
+    halo_u, halo_v = padded_winds(wind_u, wind_v, (before, after, *sides))
     arrived, halo_u, halo_v, g1 = lax.optimization_barrier((arrived, halo_u, halo_v, g1))
 
     alpha = static = None
@@ -660,6 +671,7 @@
             out_shape=jax.ShapeDtypeStruct(h.shape, F32),
             in_specs=[vmem(), vmem()],
             out_specs=vmem(),
+            compiler_params=params(8),
             name=f"scan_x_{c}",
         )(h, mine_x)
         h = lax.all_to_all(h, GX, split_axis=0, concat_axis=0, tiled=True).reshape(part, 16, ny)

time: 190 us -> 194 us (1.021)
  local copies, waits for them, and re-layouts: 9.2 us -> 24.7 us
  waiting for transfers between devices: 38.7 us -> 23.5 us
  other arithmetic: 9.53 us -> 17.3 us
  Pallas kernels: 72.5 us -> 66.9 us
    unnamed x26 -> x96, local copies, waits for them, and re-layouts: 2.7 us -> 13.4 us
    ppermute x3, waiting for transfers between devices: 11 us -> 2.89 us  [from_after(): return lax.ppermute(array, axis, [(i + 1, i) for i in range(count - 1)])]
    all_to_all x1, waiting for transfers between devices: 5.63 us -> 0.01 us  [body(): lax.all_to_all(q, BOTH, split_axis=0, concat_axis=0, tiled=True)]
    another operation x7, local copies, waits for them, and re-layouts: 0.17 us -> 5.19 us  [body(): jnp.stack(line)]
    ppermute x3, waiting for transfers between devices: 4.29 us -> 0.01 us  [from_before(): return lax.ppermute(array, axis, [(i, i + 1) for i in range(count - 1)])]
    mul x7, other arithmetic: 0.09 us -> 3.56 us  [product(): -2.0 * (count - last) / length]
    all_to_all x1, starting transfers between devices: 3.57 us -> 6.96 us  [body(): lax.all_to_all(h.reshape(count_x, share, 16, ny), GX, split_axis=0, conca...]
    pallas_call x2, Pallas kernels: 7.79 us -> 5.37 us  [the longest x1 3.93 us: wind_sides(): pl.pallas_call(wind_columns_kernel, grid=steps, in_specs=[levels(nx, ny)]...]
  transfers between devices with their start and end apart: 11 -> 11, of which waited for: 8 -> 3; matrix products, arithmetic and copies ran while one was open for 5% -> 16% of each run, Pallas kernels for 19% -> 17%
where the time goes in v2:
time: 194 us; the launch traced here: 192 us
  Pallas kernels  66.9 us (34%)
  starting transfers between devices  54.5 us (28%)
  local copies, waits for them, and re-layouts  24.7 us (13%)
  waiting for transfers between devices  23.5 us (12%)
  other arithmetic  17.3 us (9%)
  matrix products  4.13 us (2%)
    pallas_call x1, Pallas kernels, body(): pl.pallas_call(final_kernel, grid=(steps,), in_specs=[pl.BlockSpec((8, de...  16.2 us
    pallas_call x1, Pallas kernels, body(): pl.pallas_call(columns_kernel, out_shape=jax.ShapeDtypeStruct((lev * nx,...  14 us
    unnamed x96, local copies, waits for them, and re-layouts  13.4 us
    all_to_all x1, starting transfers between devices, body(): lax.all_to_all(q, BOTH, split_axis=0, concat_axis=0, tiled=True)  11.9 us
    all_to_all x1, starting transfers between devices, body(): lax.all_to_all(mine, BOTH, split_axis=0, concat_axis=0, tiled=True)  11.5 us
    all_to_all x1, waiting for transfers between devices, body(): lax.all_to_all(h.reshape(count_x, share, 16, ny), GX, split_axis=0, conca...  11.1 us
    ppermute x3, starting transfers between devices, from_before(): return lax.ppermute(array, axis, [(i, i + 1) for i in range(count - 1)])  10.4 us
    pallas_call x1, Pallas kernels, body(): pl.pallas_call(filter_x_kernel, grid=(steps,), in_specs=[pl.BlockSpec((16...  10 us
  transfers between devices with their start and end apart: 11, of which 3 were waited for; matrix products, arithmetic and copies ran while one was open for 16% of the time, Pallas kernels for 17%

profile of v2, /device:TPU:1, one launch (start us, length us, event | category | flops | bytes accessed | tf_op | source)
XLA Modules:
  0.0 192.3 jit_solution(10070112012741741180)
XLA Ops:
  3.6 1.5 sensor.1
  5.8 11.5 %all-to-all-start.1 = ((bf16[128,48,128]{2,1,0:T(8,128)(2,1)}), bf16[128,48,128]{2,1,0:T(8,128)(2,1)S(1)}, u32[]{:S(2)}, u32[]{:S(2)}) async-start(bf16[128,48,128]{2,1,0:T(8,128)(2,1)} %get-tuple-element.37), calls=%async_computation.1 | async-start | bytes 3145728 | tf_op jit(solution)/shard_map/all_to_all | solution.py:532
  17.3 9.7 %records.1 = bf16[128,64,128]{2,1,0:T(8,128)(2,1)} custom-call(s32[64]{0:T(128)} %home_ref.1, s32[64]{0:T(128)} %count_ref.1, bf16[128,512]{1,0:T(8,128)(2,1)} %copy-done.6, bf16[64,512,128]{2,1,0:T(8,128)(2,1)} %dep_ref.1), custom_call_target="tpu_custom_call" | custom-call | tf_op jit(solution)/shard_map/records/pallas_call | solution.py:535
  28.5 3.3 %collective-permute-start = (bf16[64,16,128]{2,1,0:T(8,128)(2,1)}, bf16[64,16,128]{2,1,0:T(8,128)(2,1)S(1)}, u32[]{:S(2)}, u32[]{:S(2)}) collective-permute-start(bf16[64,16,128]{2,1,0:T(8,128)(2,1)} %get-tuple-element.32), channel_id=1, source_target_pairs={{0,8},{8,16},{16,24},{24,32},{32,40},{40,48},{48,56},{56,64},{64,7... | collective-permute-start | bytes 786440 | tf_op jit(solution)/shard_map/ppermute | solution.py:362
  50.7 2.4 %subtract_convert_fusion.2 = (bf16[64,1,128]{2,1,0:T(2,128)(2,1)}, bf16[64,1,128]{2,1,0:T(2,128)(2,1)}, f32[64,1,128]{2,1,0:T(1,128)}, f32[64,1,128]{2,1,0:T(1,1...) fusion(f32[64,1,128]{2,1,0:T(1,128)S(1)} %bitcast.96, ...), kind=kLoop, calls=%fused_computation.53 | loop fusion | flops 311296 | bytes 367360 | tf_op jit(solution)/shard_map/convert_element_type | solution.py:35
  55.6 11.9 %all-to-all-start = ((bf16[128,64,128]{2,1,0:T(8,128)(2,1)}), bf16[128,64,128]{2,1,0:T(8,128)(2,1)}, u32[]{:S(2)}, u32[]{:S(2)}) async-start(bf16[128,64,128]{2,1,0:T(8,128)(2,1)} %records.1), calls=%async_computation | async-start | bytes 4194304 | tf_op jit(solution)/shard_map/all_to_all | solution.py:553
  67.5 4.7 %subtract_convert_fusion = (bf16[64,128,128]{2,1,0:T(8,128)(2,1)}, bf16[64,128,128]{2,1,0:T(8,128)(2,1)}) fusion(f32[128,128]{1,0:T(8,128)S(1)} %get-tuple-element.137, f32[64]{0:T(128)} %param.17, f32[128,128]{1,0:T(8,128)S(1)} %get-tuple-element.138, f32[64]{0:T(128)S(1)} %copy-done.31), kind=kLoop, calls=%fused_computation.5 | loop fusion | flops 9437184 | bytes 4325888 | tf_op jit(solution)/shard_map/convert_element_type | solution.py:35
  72.2 3.9 %wind_columns.1 = (bf16[64,16,64]{2,1,0:T(8,128)(2,1)}, bf16[64,16,64]{2,1,0:T(8,128)(2,1)}) custom-call(bf16[64,48,128]{2,1,0:T(8,128)(2,1)S(1)} %copy-done, bf16[64,48,128]{2,1,0:T(8,128)(2,1)S(1)} %copy-done.1, bf16[64,16,128]{2,1,0:T(8,128)(2,1)S(1)} %collective-permute-done.before_ref, bf16[64,16,128]{2,1,0:T(8,128)(2,1)} %collective-permute-done.1.after_ref, ...), custom_call_target="tpu_custom_call" | custom-call | tf_op jit(solution)/shard_map/wind_columns/pallas_call | solution.py:443
  76.1 3.5 %collective-permute-start.2 = (bf16[64,16,64]{2,1,0:T(8,128)(2,1)}, bf16[64,16,64]{2,1,0:T(8,128)(2,1)}, u32[]{:S(2)}, u32[]{:S(2)}) collective-permute-start(bf16[64,16,64]{2,1,0:T(8,128)(2,1)} %get-tuple-element.38), channel_id=1, source_target_pairs={{0,1},{1,2},{2,3},{3,4},{4,5},{5,6},{6,7},{8,9},{9,10},{10,11},{11... | collective-permute-start | bytes 393224 | tf_op jit(solution)/shard_map/ppermute | solution.py:362
  79.7 1.9 collective-permute-start.3
  83.1 14.0 %columns.1 = f32[3072,128]{1,0:T(8,128)S(1)} custom-call(s32[128]{0:T(128)S(1)} %get-tuple-element.108.line_ref, s32[128]{0:T(128)S(1)} %get-tuple-element.107.count_ref, bf16[128,48,128]{2,1,0:T(8,128)(2,1)S(1)} %all-to-all-done.1.gathered_ref, bf16[64,48,128]{2,1,0:T(8,128)(2,1)S(1)} %copy-done.11), custom_call_target="tpu_custom_call" | custom-call | flops 8589934592 | bytes 8388608 | tf_op jit(solution)/shard_map/columns/pallas_call | solution.py:559
  98.2 2.9 %wind_pad.1 = (bf16[64,56,256]{2,1,0:T(8,128)(2,1)S(1)}, bf16[64,56,256]{2,1,0:T(8,128)(2,1)S(1)}) custom-call(bf16[64,48,128]{2,1,0:T(8,128)(2,1)S(1)} %copy-done, bf16[64,48,128]{2,1,0:T(8,128)(2,1)S(1)} %copy-done.1, bf16[64,16,128]{2,1,0:T(8,128)(2,1)S(1)} %collective-permute-done.before_ref, bf16[64,16,128]{2,1,0:T(8,128)(2,1)} %collective-permute-done.1.after_ref, ...), custom_call_target="tpu_custom_call" | custom-call | tf_op jit(solution)/shard_map/wind_pad/pallas_call | solution.py:462
  103.6 4.1 %fusion.6.g2_ref = f32[64,48,128]{2,1,0:T(8,128)} fusion(bf16[128,64,128]{2,1,0:T(8,128)(2,1)} %all-to-all-done, s32[128]{0:T(128)S(1)} %get-tuple-element.108.line_ref, s32[48]{0:T(128)S(1)} %copy-done.44), kind=kOutput, calls=%fused_computation.9 | convolution fusion | flops 100669440 | bytes 3670720 | tf_op jit(solution)/shard_map/sx,sly->lxy/dot_general | solution.py:646
  108.5 5.5 %edges_0.1 = f32[64,16,128]{2,1,0:T(8,128)} custom-call(f32[64,48,128]{2,1,0:T(8,128)} %bitcast.91, f32[64,48,128]{2,1,0:T(8,128)} %fusion.6.g2_ref, bf16[4,64,48,128]{3,2,1,0:T(8,128)(2,1)} %ens_ref.3, f32[5,64,128]{2,1,0:T(8,128)} %broadcast_in_dim.12.coef_ref), custom_call_target="tpu_custom_call" | custom-call | tf_op jit(solution)/shard_map/edges_0/pallas_call | solution.py:649
  114.1 7.0 %all-to-all-start.2 = ((f32[16,4,16,128]{3,2,1,0:T(8,128)}), f32[16,4,16,128]{3,2,1,0:T(8,128)S(1)}, u32[]{:S(2)}, u32[]{:S(2)}) async-start(f32[16,4,16,128]{3,2,1,0:T(8,128)} %bitcast.95), calls=%async_computation.2 | async-start | bytes 1048576 | tf_op jit(solution)/shard_map/all_to_all | solution.py:664
  121.8 11.1 %all-to-all-done.2.in_ref = f32[16,4,16,128]{3,2,1,0:T(8,128)S(1)} async-done(((f32[16,4,16,128]{3,2,1,0:T(8,128)}), f32[16,4,16,128]{3,2,1,0:T(8,128)S(1)}, u32[]{:S(2)}, u32[]{:S(2)}) %all-to-all-start.2) | async-done | bytes 524320 | tf_op jit(solution)/shard_map/all_to_all | solution.py:664
  134.0 3.8 %all-to-all-start.3 = ((f32[16,4,16,128]{3,2,1,0:T(8,128)}), f32[16,4,16,128]{3,2,1,0:T(8,128)S(1)}, u32[]{:S(2)}, u32[]{:S(2)}) async-start(f32[16,4,16,128]{3,2,1,0:T(8,128)} %scan_x_0.1), calls=%async_computation.3 | async-start | bytes 1048576 | tf_op jit(solution)/shard_map/all_to_all | solution.py:677
  139.0 9.5 %all-to-all-done.3 = f32[16,4,16,128]{3,2,1,0:T(8,128)S(1)} async-done(((f32[16,4,16,128]{3,2,1,0:T(8,128)}), f32[16,4,16,128]{3,2,1,0:T(8,128)S(1)}, u32[]{:S(2)}, u32[]{:S(2)}) %all-to-all-start.3) | async-done | bytes 524320 | tf_op jit(solution)/shard_map/all_to_all | solution.py:677
  149.3 10.0 %filter_x_0.1 = (bf16[64,256,128]{2,1,0:T(8,128)(2,1)}, bf16[64,256,128]{2,1,0:T(8,128)(2,1)}, bf16[8,2,64,256]{3,2,1,0:T(8,128)(2,1)}, bf16[3,64,128]{2,1,0:T(8,128)(2,1)}, bf16[3,64,128]{2,1,0:T(8,128)(2,1)}) custom-call(f32[64,48,128]{2,1,0:T(8,128)} %bitcast.92, f32[64,48,128]{2,1,0:T(8,128)} %fusion.6.g2_ref, bf16[4,64,48,128]{3,2,1,0:T(8,128)(2,1)} %ens_ref.3, ...), custom_call_target="tpu_custom_call" | custom-call | tf_op jit(solution)/shard_map/filter_x_0/pallas_call | solution.py:678
  159.4 4.9 %all-to-all-start.4 = ((bf16[8,2,64,256]{3,2,1,0:T(8,128)(2,1)}), bf16[8,2,64,256]{3,2,1,0:T(8,128)(2,1)S(1)}, u32[]{:S(2)}, u32[]{:S(2)}) async-start(bf16[8,2,64,256]{3,2,1,0:T(8,128)(2,1)} %get-tuple-element.49), calls=%async_computation.4 | async-start | bytes 1048576 | tf_op jit(solution)/shard_map/all_to_all | solution.py:712
  165.0 3.5 %collective-permute-start.4 = (bf16[3,64,128]{2,1,0:T(8,128)(2,1)}, bf16[3,64,128]{2,1,0:T(8,128)(2,1)S(1)}, u32[]{:S(2)}, u32[]{:S(2)}) collective-permute-start(bf16[3,64,128]{2,1,0:T(8,128)(2,1)} %get-tuple-element.50), channel_id=1, source_target_pairs={{0,1},{1,2},{2,3},{3,4},{4,5},{5,6},{6,7},{8,9},{9,10},{10,11},{11... | collective-permute-start | bytes 147464 | tf_op jit(solution)/shard_map/ppermute | solution.py:362
  168.5 1.9 collective-permute-start.5
  171.6 2.9 %collective-permute-done.5.fr_ref = bf16[3,64,128]{2,1,0:T(8,128)(2,1)S(1)} collective-permute-done((bf16[3,64,128]{2,1,0:T(8,128)(2,1)}, bf16[3,64,128]{2,1,0:T(8,128)(2,1)S(1)}, u32[]{:S(2)}, u32[]{:S(2)}) %collective-permute-start.5) | collective-permute-done | bytes 49184 | tf_op jit(solution)/shard_map/ppermute | solution.py:367
  176.1 16.2 %final_0.1 = (f32[4,64,48,128]{3,2,1,0:T(8,128)}, f32[64,48,128]{2,1,0:T(8,128)}) custom-call(bf16[64,256,128]{2,1,0:T(8,128)(2,1)} %get-tuple-element.47.hi_ref, bf16[64,256,128]{2,1,0:T(8,128)(2,1)} %get-tuple-element.48.lo_ref, bf16[64,128,128]{2,1,0:T(8,128)(2,1)} %get-tuple-element.82.nh_ref, bf16[64,128,128]{2,1,0:T(8,128)(2,1)} %get-tuple-element.81.nl_ref, ...), custom_call_target="tpu_custom_call" | custom-call | tf_op jit(solution)/shard_map/final_0/pallas_call | solution.py:731
  (174 shorter events, 39.3 us)
Async XLA Ops:
  5.8 49.8 %all-to-all-start.1 = ((bf16[128,48,128]{2,1,0:T(8,128)(2,1)}), bf16[128,48,128]{2,1,0:T(8,128)(2,1)S(1)}, u32[]{:S(2)}, u32[]{:S(2)}) async-start(bf16[128,48,128]{2,1,0:T(8,128)(2,1)} %get-tuple-element.37), calls=%async_computation.1 | async-start | bytes 3145728 | tf_op jit(solution)/shard_map/all_to_all | solution.py:532
  17.3 19.8 %copy-start.23 = (f32[64]{0:T(128)S(1)}, f32[64]{0:T(128)}, u32[]{:S(2)}) copy-start(f32[64]{0:T(128)} %param.17) | copy-start | bytes 772
  28.5 27.1 %collective-permute-start = (bf16[64,16,128]{2,1,0:T(8,128)(2,1)}, bf16[64,16,128]{2,1,0:T(8,128)(2,1)S(1)}, u32[]{:S(2)}, u32[]{:S(2)}) collective-permute-start(bf16[64,16,128]{2,1,0:T(8,128)(2,1)} %get-tuple-element.32), channel_id=1, source_target_pairs={{0,8},{8,16},{16,24},{24,32},{32,40},{40,48},{48,56},{56,64},{64,7... | collective-permute-start | bytes 786440 | tf_op jit(solution)/shard_map/ppermute | solution.py:362
  31.8 23.8 %collective-permute-start.1 = (bf16[64,16,128]{2,1,0:T(8,128)(2,1)}, bf16[64,16,128]{2,1,0:T(8,128)(2,1)}, u32[]{:S(2)}, u32[]{:S(2)}) collective-permute-start(bf16[64,16,128]{2,1,0:T(8,128)(2,1)} %get-tuple-element.33), channel_id=1, source_target_pairs={{8,0},{16,8},{24,16},{32,24},{40,32},{48,40},{56,48},{64,56},{72,6... | collective-permute-start | bytes 786440 | tf_op jit(solution)/shard_map/ppermute | solution.py:367
  49.2 18.3 %copy-start.31 = (f32[64]{0:T(128)S(1)}, f32[64]{0:T(128)}, u32[]{:S(2)}) copy-start(f32[64]{0:T(128)} %get-tuple-element.97) | copy-start | bytes 772
  55.6 48.0 %all-to-all-start = ((bf16[128,64,128]{2,1,0:T(8,128)(2,1)}), bf16[128,64,128]{2,1,0:T(8,128)(2,1)}, u32[]{:S(2)}, u32[]{:S(2)}) async-start(bf16[128,64,128]{2,1,0:T(8,128)(2,1)} %records.1), calls=%async_computation | async-start | bytes 4194304 | tf_op jit(solution)/shard_map/all_to_all | solution.py:553
  76.1 22.1 %collective-permute-start.2 = (bf16[64,16,64]{2,1,0:T(8,128)(2,1)}, bf16[64,16,64]{2,1,0:T(8,128)(2,1)}, u32[]{:S(2)}, u32[]{:S(2)}) collective-permute-start(bf16[64,16,64]{2,1,0:T(8,128)(2,1)} %get-tuple-element.38), channel_id=1, source_target_pairs={{0,1},{1,2},{2,3},{3,4},{4,5},{5,6},{6,7},{8,9},{9,10},{10,11},{11... | collective-permute-start | bytes 393224 | tf_op jit(solution)/shard_map/ppermute | solution.py:362
  79.7 18.6 %collective-permute-start.3 = (bf16[64,16,64]{2,1,0:T(8,128)(2,1)}, bf16[64,16,64]{2,1,0:T(8,128)(2,1)}, u32[]{:S(2)}, u32[]{:S(2)}) collective-permute-start(bf16[64,16,64]{2,1,0:T(8,128)(2,1)} %get-tuple-element.39), channel_id=1, source_target_pairs={{1,0},{2,1},{3,2},{4,3},{5,4},{6,5},{7,6},{9,8},{10,9},{11,10},{12... | collective-permute-start | bytes 393224 | tf_op jit(solution)/shard_map/ppermute | solution.py:367
  83.1 15.2 %copy-start.8 = (bf16[32,256]{1,0:T(8,128)(2,1)S(1)}, bf16[32,256]{1,0:T(8,128)(2,1)}, u32[]{:S(2)}) copy-start(bf16[32,256]{1,0:T(8,128)(2,1)} %constant.28.clone.place_ref) | copy-start | bytes 49156
  83.1 20.5 %copy-start.44 = (s32[48]{0:T(128)S(1)}, s32[48]{0:T(128)}, u32[]{:S(2)}) copy-start(s32[48]{0:T(128)} %iota_add_fusion) | copy-start | bytes 580
  108.5 12.8 %copy-start.18 = (f32[64,1,128]{2,1,0:T(1,128)S(1)}, f32[64,1,128]{2,1,0:T(1,128)}, u32[]{:S(2)}) copy-start(f32[64,1,128]{2,1,0:T(1,128)} %get-tuple-element.119) | copy-start | bytes 98308
  108.5 12.8 %copy-start.19 = (f32[64,1,128]{2,1,0:T(1,128)S(1)}, f32[64,1,128]{2,1,0:T(1,128)}, u32[]{:S(2)}) copy-start(f32[64,1,128]{2,1,0:T(1,128)} %get-tuple-element.120) | copy-start | bytes 98308
  114.0 23.8 %copy-start.25 = (f32[1,64]{1,0:T(1,128)S(1)}, f32[1,64]{1,0:T(1,128)}, u32[]{:S(2)}) copy-start(f32[1,64]{1,0:T(1,128)} %get-tuple-element.110) | copy-start | bytes 772
  114.0 23.8 %copy-start.35 = (f32[1,64]{1,0:T(1,128)S(1)}, f32[1,64]{1,0:T(1,128)}, u32[]{:S(2)}) copy-start(f32[1,64]{1,0:T(1,128)} %get-tuple-element.115) | copy-start | bytes 772
  114.0 23.8 %copy-start.43 = (f32[1,64]{1,0:T(1,128)S(1)}, f32[1,64]{1,0:T(1,128)}, u32[]{:S(2)}) copy-start(f32[1,64]{1,0:T(1,128)} %get-tuple-element.109) | copy-start | bytes 772
  114.0 24.6 %copy-start.28 = (f32[64]{0:T(128)S(1)}, f32[64]{0:T(128)}, u32[]{:S(2)}) copy-start(f32[64]{0:T(128)} %copy-done.27) | copy-start | bytes 772
  114.1 24.6 %copy-start.24 = (f32[64]{0:T(128)S(1)}, f32[64]{0:T(128)}, u32[]{:S(2)}) copy-start(f32[64]{0:T(128)} %param.17) | copy-start | bytes 772
  114.1 18.8 %all-to-all-start.2 = ((f32[16,4,16,128]{3,2,1,0:T(8,128)}), f32[16,4,16,128]{3,2,1,0:T(8,128)S(1)}, u32[]{:S(2)}, u32[]{:S(2)}) async-start(f32[16,4,16,128]{3,2,1,0:T(8,128)} %bitcast.95), calls=%async_computation.2 | async-start | bytes 1048576 | tf_op jit(solution)/shard_map/all_to_all | solution.py:664
  134.0 14.5 %all-to-all-start.3 = ((f32[16,4,16,128]{3,2,1,0:T(8,128)}), f32[16,4,16,128]{3,2,1,0:T(8,128)S(1)}, u32[]{:S(2)}, u32[]{:S(2)}) async-start(f32[16,4,16,128]{3,2,1,0:T(8,128)} %scan_x_0.1), calls=%async_computation.3 | async-start | bytes 1048576 | tf_op jit(solution)/shard_map/all_to_all | solution.py:677
  149.3 15.2 %copy-start.13 = (bf16[64,1,128]{2,1,0:T(2,128)(2,1)S(1)}, bf16[64,1,128]{2,1,0:T(2,128)(2,1)}, u32[]{:S(2)}) copy-start(bf16[64,1,128]{2,1,0:T(2,128)(2,1)} %get-tuple-element.57) | copy-start | bytes 49156
  149.3 15.2 %copy-start.14 = (bf16[64,1,128]{2,1,0:T(2,128)(2,1)S(1)}, bf16[64,1,128]{2,1,0:T(2,128)(2,1)}, u32[]{:S(2)}) copy-start(bf16[64,1,128]{2,1,0:T(2,128)(2,1)} %get-tuple-element.56) | copy-start | bytes 49156
  159.4 15.0 %all-to-all-start.4 = ((bf16[8,2,64,256]{3,2,1,0:T(8,128)(2,1)}), bf16[8,2,64,256]{3,2,1,0:T(8,128)(2,1)S(1)}, u32[]{:S(2)}, u32[]{:S(2)}) async-start(bf16[8,2,64,256]{3,2,1,0:T(8,128)(2,1)} %get-tuple-element.49), calls=%async_computation.4 | async-start | bytes 1048576 | tf_op jit(solution)/shard_map/all_to_all | solution.py:712
  165.0 6.6 %collective-permute-start.4 = (bf16[3,64,128]{2,1,0:T(8,128)(2,1)}, bf16[3,64,128]{2,1,0:T(8,128)(2,1)S(1)}, u32[]{:S(2)}, u32[]{:S(2)}) collective-permute-start(bf16[3,64,128]{2,1,0:T(8,128)(2,1)} %get-tuple-element.50), channel_id=1, source_target_pairs={{0,1},{1,2},{2,3},{3,4},{4,5},{5,6},{6,7},{8,9},{9,10},{10,11},{11... | collective-permute-start | bytes 147464 | tf_op jit(solution)/shard_map/ppermute | solution.py:362
  168.5 5.9 %collective-permute-start.5 = (bf16[3,64,128]{2,1,0:T(8,128)(2,1)}, bf16[3,64,128]{2,1,0:T(8,128)(2,1)S(1)}, u32[]{:S(2)}, u32[]{:S(2)}) collective-permute-start(bf16[3,64,128]{2,1,0:T(8,128)(2,1)} %get-tuple-element.51), channel_id=1, source_target_pairs={{1,0},{2,1},{3,2},{4,3},{5,4},{6,5},{7,6},{9,8},{10,9},{11,10},{12... | collective-permute-start | bytes 147464 | tf_op jit(solution)/shard_map/ppermute | solution.py:367
  (32 other events, 245.8 us)

commit v3 on v2

--- a/solution.py
+++ b/solution.py
@@ -224,7 +224,7 @@
     for l in range(block):
         st_ref[pl.ds(l * 16, 16), :] = fb_ref[l]
     for base in range(0, block, 8):
-        d, fc, bc = (coef_ref[k, base : base + 8] for k in range(3))
+        d, fc, bc = (coef_ref[k, base : base + 8] for k in (0, 1, 5))
 
         def at(m, x, base=base):
             return pl.ds(base * wide + m * nx + x, 8, stride=wide)
@@ -473,15 +473,90 @@
     )(wind_u, wind_v, *halos, jnp.asarray(place, BF16))
 
 
+def fell(z):
+    near = z * (1.0 - z * (1.0 / 2 - z * (1.0 / 6 - z * (1.0 / 24 - z * (1.0 / 120 - z / 720)))))
+    return jnp.where(z < 0.25, near, 1.0 - jnp.exp(-z))
+
+
 def product(length, count, i, j):
-    ratio = -jnp.expm1(-1.0 / length) / jnp.sqrt(-jnp.expm1(-2.0 / length))
+    ratio = fell(1.0 / length) / jnp.sqrt(fell(2.0 / length))
     last = jnp.maximum(i, j)
-    return ratio * jnp.exp(-jnp.abs(i - j) / length) * -jnp.expm1(-2.0 * (count - last) / length)
+    return ratio * jnp.exp(-jnp.abs(i - j) / length) * fell(2.0 * (count - last) / length)
 
 
 def entered(length, count, i):
-    ratio = jnp.expm1(-1.0 / length) / jnp.expm1(-2.0 / length)
-    return ratio * jnp.exp(-(i + 1.0) / length) * -jnp.expm1(-2.0 * (count - i) / length)
+    ratio = fell(1.0 / length) / fell(2.0 / length)
+    return ratio * jnp.exp(-(i + 1.0) / length) * fell(2.0 * (count - i) / length)
+
+
+def tables_kernel(
+    nx, share_ref, len_ref, wide_ref, e_ref, x_ref, v_ref, nh_ref, nl_ref, ab_ref, y_ref
+):
+    lev, ny, _ = nh_ref.shape
+    length = wide_ref[...]
+    fc, bc, d = jnp.sqrt(fell(2.0 / length)), fell(1.0 / length), jnp.exp(-1.0 / length)
+    for k, value in enumerate(
+        (d, fc, bc / fc, jnp.exp(-(nx + 1.0) / length), jnp.exp(1.0 / length), bc)
+    ):
+        e_ref[k] = value
+    y_ref[0] = jnp.exp(-ny / length)
+    y_ref[1] = entered(length, ny, 0.0)
+    for i in range(3):
+        y_ref[2 + i] = entered(length, ny, ny - 3.0 + i)
+        y_ref[5 + i] = jnp.exp(-(3.0 - i) / length)
+        y_ref[8 + i] = entered(length, ny, float(i))
+        y_ref[11 + i] = jnp.exp(-(ny - float(i)) / length)
+
+    row = lax.broadcasted_iota(jnp.int32, (8, ny), 0)
+    at = row.astype(F32)
+    top = row < 3
+    for k in range(x_ref.shape[1]):
+        own = jnp.full((8, ny), len_ref[share_ref[0] + k], F32)
+        jump = jnp.exp(-nx / own)
+        bottom = row > 4
+        x_ref[0, k] = jnp.where(top, 0.0, jump)
+        x_ref[1, k] = jnp.where(bottom, 0.0, jump)
+        x_ref[2, k] = jnp.where(bottom, 0.0, entered(own, nx, 0.0))
+        x_ref[3, k] = jnp.where(top, entered(own, nx, at), 0.0)
+        x_ref[4, k] = jnp.where(top, jnp.exp(-(nx - at) / own), 0.0)
+        x_ref[5, k] = jnp.where(bottom, entered(own, nx, nx - 8.0 + at), 0.0)
+        x_ref[6, k] = jnp.where(bottom, jnp.exp(-(8.0 - at) / own), 0.0)
+
+    cell = lax.broadcasted_iota(jnp.int32, (8, ny), 1)
+    cells = cell.astype(F32)
+    line = jnp.where(row < 4, at - 1.0, ny - 7.0 + at)
+    zero = jnp.zeros((8, ny), F32)
+    end, last = row < 3, row < 6
+    lower = jnp.where(last & (cell == jnp.where(end, ny - 3 + row, row - 3)), 1.0, 0.0)
+    place = jnp.concatenate([zero, lower], axis=0)
+    across = lax.broadcasted_iota(jnp.int32, (ny, ny), 0).astype(F32)
+    along = lax.broadcasted_iota(jnp.int32, (ny, ny), 1).astype(F32)
+    apart, beyond = jnp.abs(across - along), ny - jnp.maximum(across, along)
+
+    def level(l, carry):
+        own = jnp.full((8, ny), len_ref[l], F32)
+        root = jnp.sqrt(fell(2.0 / own))
+        edge = jnp.where(
+            row == 0, root * jnp.exp(-(ny - 1.0 - cells) / own), product(own, ny, line, cells)
+        )
+        high, low = split(jnp.where(row == 7, 0.0, edge))
+        v_ref[l] = jnp.concatenate([high, low], axis=0)
+        a, b = entered(own, ny, cells), jnp.exp(-(ny - cells) / own)
+        part = jnp.where(end, a, b)
+        high = part.astype(BF16).astype(F32)
+        part = jnp.where((row == 2) | (row == 5), part - high, high)
+        part = jnp.concatenate([jnp.where(last, part, 0.0), zero], axis=0)
+        ab_ref[l] = jnp.concatenate([part, place], axis=1).astype(BF16)
+        inverse = (1.0 / own)[:1]
+        ratio = (fell(1.0 / own) / root)[:1]
+        high, low = split(
+            ratio * jnp.exp(-apart * inverse) * fell(2.0 * beyond * inverse)
+        )
+        nh_ref[l] = high
+        nl_ref[l] = low
+        return carry
+
+    lax.fori_loop(0, lev, level, 0)
 
 
 def body(
@@ -568,73 +643,25 @@
     )(asked, counts, gathered, increment).reshape(lev, nx, ny)
     select = (asked[:, None] == jnp.arange(1, nx + 1, dtype=jnp.int32)[None, :]).astype(BF16)
 
-    length = filter_length
-    fc = jnp.sqrt(-jnp.expm1(-2.0 / length))
-    bc = -jnp.expm1(-1.0 / length)
-    d = jnp.exp(-1.0 / length)
-
-    def wide(columns, tail):
-        got = jnp.stack(columns).reshape(len(columns), lev, *(1 for _ in tail))
-        return jnp.broadcast_to(got, (len(columns), lev, *tail))
-
-    coef_e = wide([d, fc, bc / fc, jnp.exp(-(nx + 1.0) / length), jnp.exp(1.0 / length)], (ny,))
-    coef_f = wide([d, fc, bc], (ny,))
-    jump, zero = jnp.exp(-nx / length), jnp.zeros_like(length)
-    low = [entered(length, nx, float(i)) for i in range(3)]
-    high = [entered(length, nx, float(nx - 3 + i)) for i in range(3)]
-    low_b = [jnp.exp(-(nx - i) / length) for i in range(3)]
-    high_b = [jnp.exp(-(3.0 - i) / length) for i in range(3)]
-    kappa = entered(length, nx, 0.0)
-    table_x = jnp.stack(
-        [
-            jnp.stack(line)
-            for line in (
-                [zero] * 3 + [jump] * 5,
-                [jump] * 5 + [zero] * 3,
-                [kappa] * 5 + [zero] * 3,
-                low + [zero] * 5,
-                low_b + [zero] * 5,
-                [zero] * 5 + high,
-                [zero] * 5 + high_b,
-            )
-        ]
-    )
-    table_x = jnp.transpose(table_x, (0, 2, 1))
-    cells = jnp.arange(ny, dtype=F32)
-    big = product(length[:, None, None], ny, cells[None, :, None], cells[None, None, :])
-    nh, nl = split(big)
-    edge = jnp.stack(
-        [fc[:, None] * jnp.exp(-(ny - 1.0 - cells)[None] / length[:, None])]
-        + [
-            product(length[:, None], ny, float(i), cells[None, :])
-            for i in (0, 1, 2, ny - 3, ny - 2, ny - 1)
-        ]
-        + [jnp.zeros((lev, ny), F32)],
-        axis=1,
-    )
-    edge = jnp.concatenate(split(edge), axis=1)
-    enter_a = entered(length[:, None], ny, cells[None, :])
-    enter_b = jnp.exp(-(ny - cells)[None, :] / length[:, None])
-    ah, al = split(enter_a)
-    bh, bl = split(enter_b)
-    none = jnp.zeros((lev, ny), BF16)
-    place = jnp.stack([jnp.arange(ny) == k for k in (ny - 3, ny - 2, ny - 1, 0, 1, 2)]).astype(BF16)
-    blank = jnp.zeros((8, ny), BF16)
-    place = jnp.concatenate([blank, place, blank[:2]], axis=0)
-    spread = jnp.concatenate(
-        [
-            jnp.stack([ah, ah, al, bh, bh, bl] + [none] * 10, axis=1),
-            jnp.broadcast_to(place[None], (lev, 16, ny)),
-        ],
-        axis=2,
-    )
-    coef_y = wide(
-        [jnp.exp(-ny / length), entered(length, ny, 0.0)]
-        + [entered(length, ny, ny - 3.0 + i) for i in range(3)]
-        + [jnp.exp(-(3.0 - i) / length) for i in range(3)]
-        + [entered(length, ny, float(i)) for i in range(3)]
-        + [jnp.exp(-(ny - float(i)) / length) for i in range(3)],
-        (ny,),
+    coef, table_x, edge, nh, nl, spread, coef_y = pl.pallas_call(
+        functools.partial(tables_kernel, nx),
+        out_shape=(
+            jax.ShapeDtypeStruct((6, lev, ny), F32),
+            jax.ShapeDtypeStruct((7, share, 8, ny), F32),
+            jax.ShapeDtypeStruct((lev, 16, ny), BF16),
+            jax.ShapeDtypeStruct((lev, ny, ny), BF16),
+            jax.ShapeDtypeStruct((lev, ny, ny), BF16),
+            jax.ShapeDtypeStruct((lev, 16, 2 * ny), BF16),
+            jax.ShapeDtypeStruct((14, lev, ny), F32),
+        ),
+        in_specs=[smem(), smem(), vmem()],
+        out_specs=(vmem(),) * 7,
+        compiler_params=params(12),
+        name="tables",
+    )(
+        (pos_x * share).reshape(1),
+        filter_length,
+        jnp.broadcast_to(filter_length[:, None], (lev, ny)),
     )
     sides = wind_sides(wind_u, wind_v, before, after)
     g1, *sides = lax.optimization_barrier((g1, *sides))
@@ -653,19 +680,17 @@
                 pl.BlockSpec((16, nx, ny), lambda i, off=off: (off + i, 0, 0)),
                 pl.BlockSpec((16, nx, ny), lambda i: (i, 0, 0)),
                 pl.BlockSpec((members, 16, nx, ny), lambda i, off=off: (0, off + i, 0, 0)),
-                pl.BlockSpec((5, 16, ny), lambda i, off=off: (0, off + i, 0)),
+                pl.BlockSpec((6, 16, ny), lambda i, off=off: (0, off + i, 0)),
             ],
             out_specs=pl.BlockSpec((16, 16, ny), lambda i: (i, 0, 0)),
             out_shape=jax.ShapeDtypeStruct((part, 16, ny), F32),
             scratch_shapes=[pltpu.VMEM((16 * rows, ny), F32), pltpu.VMEM((16 * 16, ny), F32)],
             compiler_params=params(56),
             name=f"edges_{c}",
-        )(g1, g2, ensemble, coef_e)
+        )(g1, g2, ensemble, coef)
         h = lax.all_to_all(
             h.reshape(count_x, share, 16, ny), GX, split_axis=0, concat_axis=0, tiled=True
         )
-        mine_x = lax.dynamic_slice_in_dim(table_x, c * part + pos_x * share, share, axis=1)
-        mine_x = jnp.broadcast_to(mine_x[:, :, :, None], (7, share, 8, ny))
         h = pl.pallas_call(
             scan_x_kernel,
             out_shape=jax.ShapeDtypeStruct(h.shape, F32),
@@ -673,7 +698,7 @@
             out_specs=vmem(),
             compiler_params=params(8),
             name=f"scan_x_{c}",
-        )(h, mine_x)
+        )(h, table_x)
         h = lax.all_to_all(h, GX, split_axis=0, concat_axis=0, tiled=True).reshape(part, 16, ny)
         hi, lo, es, to_right, to_left = pl.pallas_call(
             filter_x_kernel,
@@ -683,7 +708,7 @@
                 pl.BlockSpec((16, nx, ny), lambda i: (i, 0, 0)),
                 pl.BlockSpec((members, 16, nx, ny), lambda i, off=off: (0, off + i, 0, 0)),
                 pl.BlockSpec((16, 16, ny), lambda i: (i, 0, 0)),
-                pl.BlockSpec((3, 16, ny), lambda i, off=off: (0, off + i, 0)),
+                pl.BlockSpec((6, 16, ny), lambda i, off=off: (0, off + i, 0)),
                 pl.BlockSpec((16, 16, ny), lambda i, off=off: (off + i, 0, 0)),
             ],
             out_specs=(
@@ -708,7 +733,7 @@
             ],
             compiler_params=params(56),
             name=f"filter_x_{c}",
-        )(g1, g2, ensemble, h, coef_f, edge)
+        )(g1, g2, ensemble, h, coef, edge)
         es = lax.all_to_all(es, GY, split_axis=0, concat_axis=0, tiled=True)
         from_left = from_before(to_right, GY)
         from_right = from_after(to_left, GY)

time: 194 us -> 182 us (0.938)
  blocking collectives: 0 us -> 33 us
  other arithmetic: 17.3 us -> 2.25 us
  starting transfers between devices: 54.5 us -> 43.1 us
  local copies, waits for them, and re-layouts: 24.7 us -> 13.4 us
  waiting for transfers between devices: 23.5 us -> 13.7 us
  Pallas kernels: 66.9 us -> 70 us
    all_to_all x0 -> x2, blocking collectives: none -> 33 us  [the longest x1 18.8 us: body(): lax.all_to_all(h.reshape(count_x, share, 16, ny), GX, split_axis=0, conca...]
    all_to_all x2 -> x0, waiting for transfers between devices: 20.6 us -> none  [the longest x1 11.1 us: body(): lax.all_to_all(h.reshape(count_x, share, 16, ny), GX, split_axis=0, conca...]
    all_to_all x2 -> x0, starting transfers between devices: 10.7 us -> none  [the longest x1 6.96 us: body(): lax.all_to_all(h.reshape(count_x, share, 16, ny), GX, split_axis=0, conca...]
    ppermute x3, waiting for transfers between devices: 0.01 us -> 8.19 us  [from_before(): return lax.ppermute(array, axis, [(i, i + 1) for i in range(count - 1)])]
    another operation x19 -> x0, local copies, waits for them, and re-layouts: 7.42 us -> none  [the longest x7 5.19 us: body(): jnp.stack(line)]
    convert_element_type x5 -> x0, other arithmetic: 7.41 us -> none  [the longest x4 7.4 us: split(): return (high, (value - high.astype(F32)).astype(BF16))]
    pallas_call x0 -> x1, Pallas kernels: none -> 6.54 us  [body(): pl.pallas_call(functools.partial(tables_kernel, nx), out_shape=(jax.Shape...]
    mul x8 -> x0, other arithmetic: 3.57 us -> none  [the longest x7 3.56 us: product(): -2.0 * (count - last) / length]
  transfers between devices with their start and end apart: 11 -> 9, of which waited for: 3 -> 5; matrix products, arithmetic and copies ran while one was open for 16% -> 1% of each run, Pallas kernels for 17% -> 20%
where the time goes in v3:
time: 182 us; the launch traced here: 181 us
  Pallas kernels  70 us (38%)
  starting transfers between devices  43.1 us (24%)
  blocking collectives  33 us (18%)
  waiting for transfers between devices  13.7 us (8%)
  local copies, waits for them, and re-layouts  13.4 us (7%)
  matrix products  4.13 us (2%)
  other arithmetic  2.25 us (1%)
    all_to_all x1, blocking collectives, body(): lax.all_to_all(h.reshape(count_x, share, 16, ny), GX, split_axis=0, conca...  18.8 us
    pallas_call x1, Pallas kernels, body(): pl.pallas_call(final_kernel, grid=(steps,), in_specs=[pl.BlockSpec((8, de...  16.2 us
    all_to_all x1, blocking collectives, body(): lax.all_to_all(h, GX, split_axis=0, concat_axis=0, tiled=True)  14.2 us
    pallas_call x1, Pallas kernels, body(): pl.pallas_call(columns_kernel, out_shape=jax.ShapeDtypeStruct((lev * nx,...  14 us
    unnamed x46, local copies, waits for them, and re-layouts  12.3 us
    all_to_all x1, starting transfers between devices, body(): lax.all_to_all(mine, BOTH, split_axis=0, concat_axis=0, tiled=True)  11.5 us
    all_to_all x1, starting transfers between devices, body(): lax.all_to_all(q, BOTH, split_axis=0, concat_axis=0, tiled=True)  11.2 us
    ppermute x3, starting transfers between devices, from_before(): return lax.ppermute(array, axis, [(i, i + 1) for i in range(count - 1)])  10.4 us
  transfers between devices with their start and end apart: 9, of which 5 were waited for; matrix products, arithmetic and copies ran while one was open for 1% of the time, Pallas kernels for 20%

profile of v3, /device:TPU:1, one launch (start us, length us, event | category | flops | bytes accessed | tf_op | source)
XLA Modules:
  0.0 180.6 jit_solution(1269495086440975421)
XLA Ops:
  3.6 1.5 sensor.1
  5.8 11.5 %all-to-all-start.1 = ((bf16[128,48,128]{2,1,0:T(8,128)(2,1)}), bf16[128,48,128]{2,1,0:T(8,128)(2,1)S(1)}, u32[]{:S(2)}, u32[]{:S(2)}) async-start(bf16[128,48,128]{2,1,0:T(8,128)(2,1)} %get-tuple-element.44), calls=%async_computation.1 | async-start | bytes 3145728 | tf_op jit(solution)/shard_map/all_to_all | solution.py:607
  17.3 9.7 %records.1 = bf16[128,64,128]{2,1,0:T(8,128)(2,1)} custom-call(s32[64]{0:T(128)} %home_ref.1, s32[64]{0:T(128)} %count_ref.1, bf16[128,512]{1,0:T(8,128)(2,1)} %copy-done.16, bf16[64,512,128]{2,1,0:T(8,128)(2,1)} %dep_ref.1), custom_call_target="tpu_custom_call" | custom-call | tf_op jit(solution)/shard_map/records/pallas_call | solution.py:610
  27.2 3.3 %collective-permute-start = (bf16[64,16,128]{2,1,0:T(8,128)(2,1)S(1)}, bf16[64,16,128]{2,1,0:T(8,128)(2,1)S(1)}, u32[]{:S(2)}, u32[]{:S(2)}) collective-permute-start(bf16[64,16,128]{2,1,0:T(8,128)(2,1)S(1)} %get-tuple-element.39), channel_id=1, source_target_pairs={{0,8},{8,16},{16,24},{24,32},{32,40},{40,48},{48,56},{56,64},{64,7... | collective-permute-start | bytes 786440 | tf_op jit(solution)/shard_map/ppermute | solution.py:362
  31.8 6.7 %collective-permute-done.before_ref = bf16[64,16,128]{2,1,0:T(8,128)(2,1)S(1)} collective-permute-done((bf16[64,16,128]{2,1,0:T(8,128)(2,1)S(1)}, bf16[64,16,128]{2,1,0:T(8,128)(2,1)S(1)}, u32[]{:S(2)}, u32[]{:S(2)}) %collective-permute-start) | collective-permute-done | bytes 262176 | tf_op jit(solution)/shard_map/ppermute | solution.py:362
  38.5 2.8 %collective-permute-done.1.after_ref = bf16[64,16,128]{2,1,0:T(8,128)(2,1)S(1)} collective-permute-done((bf16[64,16,128]{2,1,0:T(8,128)(2,1)S(1)}, bf16[64,16,128]{2,1,0:T(8,128)(2,1)S(1)}, u32[]{:S(2)}, u32[]{:S(2)}) %collective-permute-start.1) | collective-permute-done | bytes 262176 | tf_op jit(solution)/shard_map/ppermute | solution.py:367
  42.2 11.2 %all-to-all-start = ((bf16[128,64,128]{2,1,0:T(8,128)(2,1)}), bf16[128,64,128]{2,1,0:T(8,128)(2,1)}, u32[]{:S(2)}, u32[]{:S(2)}) async-start(bf16[128,64,128]{2,1,0:T(8,128)(2,1)} %records.1), calls=%async_computation | async-start | bytes 4194304 | tf_op jit(solution)/shard_map/all_to_all | solution.py:628
  53.5 6.5 %tables.1 = (f32[6,64,128]{2,1,0:T(8,128)S(1)}, f32[7,4,8,128]{3,2,1,0:T(8,128)S(1)}, bf16[64,16,128]{2,1,0:T(8,128)(2,1)S(1)}, bf16[64,128,128]{2,1,0:T(8,128)(...) custom-call(s32[1]{0:T(128)} %bitcast.10.share_ref, ...), custom_call_target="tpu_custom_call" | custom-call | tf_op jit(solution)/shard_map/tables/pallas_call | solution.py:646
  63.9 2.7 %wind_columns.1 = (bf16[64,16,64]{2,1,0:T(8,128)(2,1)}, bf16[64,16,64]{2,1,0:T(8,128)(2,1)}) custom-call(bf16[64,48,128]{2,1,0:T(8,128)(2,1)S(1)} %copy-done, bf16[64,48,128]{2,1,0:T(8,128)(2,1)S(1)} %copy-done.1, bf16[64,16,128]{2,1,0:T(8,128)(2,1)S(1)} %collective-permute-done.before_ref, bf16[64,16,128]{2,1,0:T(8,128)(2,1)S(1)} %copy-done.9, ...), custom_call_target="tpu_custom_call" | custom-call | tf_op jit(solution)/shard_map/wind_columns/pallas_call | solution.py:443
  66.7 3.5 %collective-permute-start.2 = (bf16[64,16,64]{2,1,0:T(8,128)(2,1)}, bf16[64,16,64]{2,1,0:T(8,128)(2,1)}, u32[]{:S(2)}, u32[]{:S(2)}) collective-permute-start(bf16[64,16,64]{2,1,0:T(8,128)(2,1)} %get-tuple-element.45), channel_id=1, source_target_pairs={{0,1},{1,2},{2,3},{3,4},{4,5},{5,6},{6,7},{8,9},{9,10},{10,11},{11... | collective-permute-start | bytes 393224 | tf_op jit(solution)/shard_map/ppermute | solution.py:362
  70.2 1.9 %collective-permute-start.3 = (bf16[64,16,64]{2,1,0:T(8,128)(2,1)}, bf16[64,16,64]{2,1,0:T(8,128)(2,1)}, u32[]{:S(2)}, u32[]{:S(2)}) collective-permute-start(bf16[64,16,64]{2,1,0:T(8,128)(2,1)} %get-tuple-element.46), channel_id=1, source_target_pairs={{1,0},{2,1},{3,2},{4,3},{5,4},{6,5},{7,6},{9,8},{10,9},{11,10},{12... | collective-permute-start | bytes 393224 | tf_op jit(solution)/shard_map/ppermute | solution.py:367
  75.2 14.0 %columns.1 = f32[3072,128]{1,0:T(8,128)S(1)} custom-call(s32[128]{0:T(128)S(1)} %get-tuple-element.71.line_ref, s32[128]{0:T(128)S(1)} %get-tuple-element.70.count_ref, bf16[128,48,128]{2,1,0:T(8,128)(2,1)S(1)} %all-to-all-done.1.gathered_ref, bf16[64,48,128]{2,1,0:T(8,128)(2,1)S(1)} %copy-done.22), custom_call_target="tpu_custom_call" | custom-call | flops 8589934592 | bytes 8388608 | tf_op jit(solution)/shard_map/columns/pallas_call | solution.py:634
  90.3 2.8 %wind_pad.1 = (bf16[64,56,256]{2,1,0:T(8,128)(2,1)S(1)}, bf16[64,56,256]{2,1,0:T(8,128)(2,1)S(1)}) custom-call(bf16[64,48,128]{2,1,0:T(8,128)(2,1)S(1)} %copy-done, bf16[64,48,128]{2,1,0:T(8,128)(2,1)S(1)} %copy-done.1, bf16[64,16,128]{2,1,0:T(8,128)(2,1)S(1)} %collective-permute-done.before_ref, bf16[64,16,128]{2,1,0:T(8,128)(2,1)S(1)} %copy-done.10, ...), custom_call_target="tpu_custom_call" | custom-call | tf_op jit(solution)/shard_map/wind_pad/pallas_call | solution.py:462
  95.6 4.1 %fusion.2.g2_ref = f32[64,48,128]{2,1,0:T(8,128)} fusion(bf16[128,64,128]{2,1,0:T(8,128)(2,1)} %all-to-all-done, s32[128]{0:T(128)S(1)} %get-tuple-element.71.line_ref, s32[48]{0:T(128)S(1)} %iota_add_fusion), kind=kOutput, calls=%fused_computation.2 | convolution fusion | flops 100669440 | bytes 3670720 | tf_op jit(solution)/shard_map/sx,sly->lxy/dot_general | solution.py:673
  99.7 5.4 %edges_0.1 = f32[64,16,128]{2,1,0:T(8,128)} custom-call(f32[64,48,128]{2,1,0:T(8,128)} %bitcast.22, f32[64,48,128]{2,1,0:T(8,128)} %fusion.2.g2_ref, bf16[4,64,48,128]{3,2,1,0:T(8,128)(2,1)} %ens_ref.3, f32[6,64,128]{2,1,0:T(8,128)} %copy-done.11), custom_call_target="tpu_custom_call" | custom-call | tf_op jit(solution)/shard_map/edges_0/pallas_call | solution.py:676
  105.2 18.8 %all_to_all.25.in_ref = f32[16,4,16,128]{3,2,1,0:T(8,128)S(1)} all-to-all(f32[16,4,16,128]{3,2,1,0:T(8,128)} %bitcast.26), channel_id=1, replica_groups=mesh['gx'=16,'gy'=8] {'gx'}, dimensions={0} | all-to-all | bytes 1048576 | tf_op jit(solution)/shard_map/all_to_all | solution.py:691
  124.1 14.2 %all_to_all.26 = f32[16,4,16,128]{3,2,1,0:T(8,128)} all-to-all(f32[16,4,16,128]{3,2,1,0:T(8,128)S(1)} %scan_x_0.1), channel_id=1, replica_groups=mesh['gx'=16,'gy'=8] {'gx'}, dimensions={0} | all-to-all | bytes 1048576 | tf_op jit(solution)/shard_map/all_to_all | solution.py:702
  138.3 10.2 %filter_x_0.1 = (bf16[64,256,128]{2,1,0:T(8,128)(2,1)}, bf16[64,256,128]{2,1,0:T(8,128)(2,1)}, bf16[8,2,64,256]{3,2,1,0:T(8,128)(2,1)}, bf16[3,64,128]{2,1,0:T(8,128)(2,1)}, bf16[3,64,128]{2,1,0:T(8,128)(2,1)}) custom-call(f32[64,48,128]{2,1,0:T(8,128)} %bitcast.23, f32[64,48,128]{2,1,0:T(8,128)} %fusion.2.g2_ref, bf16[4,64,48,128]{3,2,1,0:T(8,128)(2,1)} %ens_ref.3, ...), custom_call_target="tpu_custom_call" | custom-call | tf_op jit(solution)/shard_map/filter_x_0/pallas_call | solution.py:703
  148.5 5.0 %all-to-all-start.4 = ((bf16[8,2,64,256]{3,2,1,0:T(8,128)(2,1)}), bf16[8,2,64,256]{3,2,1,0:T(8,128)(2,1)S(1)}, u32[]{:S(2)}, u32[]{:S(2)}) async-start(bf16[8,2,64,256]{3,2,1,0:T(8,128)(2,1)} %get-tuple-element.61), calls=%async_computation.4 | async-start | bytes 1048576 | tf_op jit(solution)/shard_map/all_to_all | solution.py:737
  153.4 3.5 %collective-permute-start.4 = (bf16[3,64,128]{2,1,0:T(8,128)(2,1)}, bf16[3,64,128]{2,1,0:T(8,128)(2,1)S(1)}, u32[]{:S(2)}, u32[]{:S(2)}) collective-permute-start(bf16[3,64,128]{2,1,0:T(8,128)(2,1)} %get-tuple-element.62), channel_id=1, source_target_pairs={{0,1},{1,2},{2,3},{3,4},{4,5},{5,6},{6,7},{8,9},{9,10},{10,11},{11... | collective-permute-start | bytes 147464 | tf_op jit(solution)/shard_map/ppermute | solution.py:362
  157.0 1.9 %collective-permute-start.5 = (bf16[3,64,128]{2,1,0:T(8,128)(2,1)}, bf16[3,64,128]{2,1,0:T(8,128)(2,1)S(1)}, u32[]{:S(2)}, u32[]{:S(2)}) collective-permute-start(bf16[3,64,128]{2,1,0:T(8,128)(2,1)} %get-tuple-element.63), channel_id=1, source_target_pairs={{1,0},{2,1},{3,2},{4,3},{5,4},{6,5},{7,6},{9,8},{10,9},{11,10},{12... | collective-permute-start | bytes 147464 | tf_op jit(solution)/shard_map/ppermute | solution.py:367
  158.9 1.5 collective-permute-done.4.fl_ref
  160.4 2.4 %collective-permute-done.5.fr_ref = bf16[3,64,128]{2,1,0:T(8,128)(2,1)S(1)} collective-permute-done((bf16[3,64,128]{2,1,0:T(8,128)(2,1)}, bf16[3,64,128]{2,1,0:T(8,128)(2,1)S(1)}, u32[]{:S(2)}, u32[]{:S(2)}) %collective-permute-start.5) | collective-permute-done | bytes 49184 | tf_op jit(solution)/shard_map/ppermute | solution.py:367
  164.4 16.2 %final_0.1 = (f32[4,64,48,128]{3,2,1,0:T(8,128)}, f32[64,48,128]{2,1,0:T(8,128)}) custom-call(bf16[64,256,128]{2,1,0:T(8,128)(2,1)} %get-tuple-element.57.hi_ref, bf16[64,256,128]{2,1,0:T(8,128)(2,1)} %get-tuple-element.58.lo_ref, bf16[64,128,128]{2,1,0:T(8,128)(2,1)} %copy-done.3, bf16[64,128,128]{2,1,0:T(8,128)(2,1)} %copy-done.4, ...), custom_call_target="tpu_custom_call" | custom-call | tf_op jit(solution)/shard_map/final_0/pallas_call | solution.py:756
  (65 shorter events, 18.3 us)
Async XLA Ops:
  5.8 36.4 %all-to-all-start.1 = ((bf16[128,48,128]{2,1,0:T(8,128)(2,1)}), bf16[128,48,128]{2,1,0:T(8,128)(2,1)S(1)}, u32[]{:S(2)}, u32[]{:S(2)}) async-start(bf16[128,48,128]{2,1,0:T(8,128)(2,1)} %get-tuple-element.44), calls=%async_computation.1 | async-start | bytes 3145728 | tf_op jit(solution)/shard_map/all_to_all | solution.py:607
  17.3 9.7 %copy-start = (bf16[64,48,128]{2,1,0:T(8,128)(2,1)S(1)}, bf16[64,48,128]{2,1,0:T(8,128)(2,1)}, u32[]{:S(2)}) copy-start(bf16[64,48,128]{2,1,0:T(8,128)(2,1)} %u_ref.2) | copy-start | bytes 2359300
  17.3 9.7 %copy-start.1 = (bf16[64,48,128]{2,1,0:T(8,128)(2,1)S(1)}, bf16[64,48,128]{2,1,0:T(8,128)(2,1)}, u32[]{:S(2)}) copy-start(bf16[64,48,128]{2,1,0:T(8,128)(2,1)} %v_ref.2) | copy-start | bytes 2359300
  27.2 11.3 %collective-permute-start = (bf16[64,16,128]{2,1,0:T(8,128)(2,1)S(1)}, bf16[64,16,128]{2,1,0:T(8,128)(2,1)S(1)}, u32[]{:S(2)}, u32[]{:S(2)}) collective-permute-start(bf16[64,16,128]{2,1,0:T(8,128)(2,1)S(1)} %get-tuple-element.39), channel_id=1, source_target_pairs={{0,8},{8,16},{16,24},{24,32},{32,40},{40,48},{48,56},{56,64},{64,7... | collective-permute-start | bytes 786440 | tf_op jit(solution)/shard_map/ppermute | solution.py:362
  30.5 22.9 %copy-start.20 = (f32[64]{0:T(128)S(1)}, f32[64]{0:T(128)}, u32[]{:S(2)}) copy-start(f32[64]{0:T(128)} %len_ref.1) | copy-start | bytes 772
  30.5 32.3 %copy-start.19 = (bf16[16,128]{1,0:T(8,128)(2,1)S(1)}, bf16[16,128]{1,0:T(8,128)(2,1)}, u32[]{:S(2)}) copy-start(bf16[16,128]{1,0:T(8,128)(2,1)} %constant.28.clone.pick_ref) | copy-start | bytes 12292
  30.5 10.7 %collective-permute-start.1 = (bf16[64,16,128]{2,1,0:T(8,128)(2,1)S(1)}, bf16[64,16,128]{2,1,0:T(8,128)(2,1)S(1)}, u32[]{:S(2)}, u32[]{:S(2)}) collective-permute-start(bf16[64,16,128]{2,1,0:T(8,128)(2,1)S(1)} %get-tuple-element.40), channel_id=1, source_target_pairs={{8,0},{16,8},{24,16},{32,24},{40,32},{48,40},{56,48},{64,56},{72,6... | collective-permute-start | bytes 786440 | tf_op jit(solution)/shard_map/ppermute | solution.py:367
  42.2 53.4 %all-to-all-start = ((bf16[128,64,128]{2,1,0:T(8,128)(2,1)}), bf16[128,64,128]{2,1,0:T(8,128)(2,1)}, u32[]{:S(2)}, u32[]{:S(2)}) async-start(bf16[128,64,128]{2,1,0:T(8,128)(2,1)} %records.1), calls=%async_computation | async-start | bytes 4194304 | tf_op jit(solution)/shard_map/all_to_all | solution.py:628
  60.0 1.4 copy-start.3
  61.4 1.4 copy-start.4
  62.8 3.9 %copy-start.11 = (f32[6,64,128]{2,1,0:T(8,128)}, f32[6,64,128]{2,1,0:T(8,128)S(1)}, u32[]{:S(2)}) copy-start(f32[6,64,128]{2,1,0:T(8,128)S(1)} %get-tuple-element.54.coef_ref) | copy-start | bytes 589828
  62.8 3.9 %copy-start.12 = (bf16[64,16,256]{2,1,0:T(8,128)(2,1)}, bf16[64,16,256]{2,1,0:T(8,128)(2,1)S(1)}, u32[]{:S(2)}) copy-start(bf16[64,16,256]{2,1,0:T(8,128)(2,1)S(1)} %get-tuple-element.65.ab_ref) | copy-start | bytes 1572868
  62.8 7.4 %copy-start.13 = (f32[14,64,128]{2,1,0:T(8,128)}, f32[14,64,128]{2,1,0:T(8,128)S(1)}, u32[]{:S(2)}) copy-start(f32[14,64,128]{2,1,0:T(8,128)S(1)} %get-tuple-element.64.coef_ref) | copy-start | bytes 1376260
  62.8 7.5 %copy-start.15 = (bf16[64,16,128]{2,1,0:T(8,128)(2,1)}, bf16[64,16,128]{2,1,0:T(8,128)(2,1)S(1)}, u32[]{:S(2)}) copy-start(bf16[64,16,128]{2,1,0:T(8,128)(2,1)S(1)} %get-tuple-element.56.v_ref) | copy-start | bytes 786436
  66.7 23.6 %collective-permute-start.2 = (bf16[64,16,64]{2,1,0:T(8,128)(2,1)}, bf16[64,16,64]{2,1,0:T(8,128)(2,1)}, u32[]{:S(2)}, u32[]{:S(2)}) collective-permute-start(bf16[64,16,64]{2,1,0:T(8,128)(2,1)} %get-tuple-element.45), channel_id=1, source_target_pairs={{0,1},{1,2},{2,3},{3,4},{4,5},{5,6},{6,7},{8,9},{9,10},{10,11},{11... | collective-permute-start | bytes 393224 | tf_op jit(solution)/shard_map/ppermute | solution.py:362
  70.2 20.1 %collective-permute-start.3 = (bf16[64,16,64]{2,1,0:T(8,128)(2,1)}, bf16[64,16,64]{2,1,0:T(8,128)(2,1)}, u32[]{:S(2)}, u32[]{:S(2)}) collective-permute-start(bf16[64,16,64]{2,1,0:T(8,128)(2,1)} %get-tuple-element.46), channel_id=1, source_target_pairs={{1,0},{2,1},{3,2},{4,3},{5,4},{6,5},{7,6},{9,8},{10,9},{11,10},{12... | collective-permute-start | bytes 393224 | tf_op jit(solution)/shard_map/ppermute | solution.py:367
  75.2 15.1 %copy-start.10 = (bf16[64,16,128]{2,1,0:T(8,128)(2,1)S(1)}, bf16[64,16,128]{2,1,0:T(8,128)(2,1)}, u32[]{:S(2)}) copy-start(bf16[64,16,128]{2,1,0:T(8,128)(2,1)} %copy-done.8) | copy-start | bytes 786436
  75.2 15.2 %copy-start.18 = (bf16[32,256]{1,0:T(8,128)(2,1)S(1)}, bf16[32,256]{1,0:T(8,128)(2,1)}, u32[]{:S(2)}) copy-start(bf16[32,256]{1,0:T(8,128)(2,1)} %constant.29.clone.place_ref) | copy-start | bytes 49156
  93.1 1.2 copy-start.6
  94.4 1.2 copy-start.7
  138.3 24.6 %copy-start.14 = (f32[14,64,128]{2,1,0:T(8,128)S(1)}, f32[14,64,128]{2,1,0:T(8,128)}, u32[]{:S(2)}) copy-start(f32[14,64,128]{2,1,0:T(8,128)} %copy-done.13) | copy-start | bytes 1376260
  148.5 14.5 %all-to-all-start.4 = ((bf16[8,2,64,256]{3,2,1,0:T(8,128)(2,1)}), bf16[8,2,64,256]{3,2,1,0:T(8,128)(2,1)S(1)}, u32[]{:S(2)}, u32[]{:S(2)}) async-start(bf16[8,2,64,256]{3,2,1,0:T(8,128)(2,1)} %get-tuple-element.61), calls=%async_computation.4 | async-start | bytes 1048576 | tf_op jit(solution)/shard_map/all_to_all | solution.py:737
  153.4 7.0 %collective-permute-start.4 = (bf16[3,64,128]{2,1,0:T(8,128)(2,1)}, bf16[3,64,128]{2,1,0:T(8,128)(2,1)S(1)}, u32[]{:S(2)}, u32[]{:S(2)}) collective-permute-start(bf16[3,64,128]{2,1,0:T(8,128)(2,1)} %get-tuple-element.62), channel_id=1, source_target_pairs={{0,1},{1,2},{2,3},{3,4},{4,5},{5,6},{6,7},{8,9},{9,10},{10,11},{11... | collective-permute-start | bytes 147464 | tf_op jit(solution)/shard_map/ppermute | solution.py:362
  157.0 5.9 %collective-permute-start.5 = (bf16[3,64,128]{2,1,0:T(8,128)(2,1)}, bf16[3,64,128]{2,1,0:T(8,128)(2,1)S(1)}, u32[]{:S(2)}, u32[]{:S(2)}) collective-permute-start(bf16[3,64,128]{2,1,0:T(8,128)(2,1)} %get-tuple-element.63), channel_id=1, source_target_pairs={{1,0},{2,1},{3,2},{4,3},{5,4},{6,5},{7,6},{9,8},{10,9},{11,10},{12... | collective-permute-start | bytes 147464 | tf_op jit(solution)/shard_map/ppermute | solution.py:367
  (8 other events, 7.1 us)

commit v4 on v3

--- a/solution.py
+++ b/solution.py
@@ -165,7 +165,7 @@
         put(14, rt * (e1 + d * f47 - d * d * d * e))
         put(15, rt * (e - d * d * e))
     for l in range(block):
-        h_ref[l] = tmp_ref[pl.ds(l * 16, 16), :]
+        h_ref[l] = tmp_ref[pl.ds(l * 16, 16), :].astype(BF16)
 
 
 def scan_x_kernel(in_ref, coef_ref, out_ref):
@@ -194,7 +194,7 @@
             before = high[g - 1] if g > 0 else none
             out_ref[g, l] = jnp.concatenate(
                 [jnp.where(row < 3, after, ahead[g]), jnp.where(row < 5, back[g], before)], axis=0
-            )
+            ).astype(BF16)
 
 
 def filter_x_kernel(
@@ -222,7 +222,7 @@
     deep = hi_ref.shape[1]
     wide = deep + 8
     for l in range(block):
-        st_ref[pl.ds(l * 16, 16), :] = fb_ref[l]
+        st_ref[pl.ds(l * 16, 16), :] = fb_ref[l].astype(F32)
     for base in range(0, block, 8):
         d, fc, bc = (coef_ref[k, base : base + 8] for k in (0, 1, 5))
 
@@ -624,26 +624,7 @@
     )(obs_home, obs_count, b, departure)
     qs, wind_u, wind_v = lax.optimization_barrier((qs, wind_u, wind_v))
     before, after = wind_ends(wind_u, wind_v)
-    qs, before, after = lax.optimization_barrier((qs, before, after))
-    arrived = [lax.all_to_all(q, BOTH, split_axis=0, concat_axis=0, tiled=True) for q in qs]
-
-    seen = lax.dynamic_slice_in_dim(
-        gathered[:, lev // 2 + 1 : lev // 2 + 3, :], pos_x * count_y + pos_y, 1, axis=2
-    )[:, :, 0].astype(jnp.int32)
-    asked, counts = seen[:, 0], seen[:, 1]
-    g1 = pl.pallas_call(
-        columns_kernel,
-        out_shape=jax.ShapeDtypeStruct((lev * nx, ny), F32),
-        in_specs=[smem(), smem(), vmem(), vmem()],
-        out_specs=vmem(),
-        scratch_shapes=[pltpu.VMEM((lev * nx, ny), F32)],
-        compiler_params=params(12),
-        cost_estimate=pl.CostEstimate(flops=2**33, bytes_accessed=2**23, transcendentals=0),
-        name="columns",
-    )(asked, counts, gathered, increment).reshape(lev, nx, ny)
-    select = (asked[:, None] == jnp.arange(1, nx + 1, dtype=jnp.int32)[None, :]).astype(BF16)
-
-    coef, table_x, edge, nh, nl, spread, coef_y = pl.pallas_call(
+    tables = pl.pallas_call(
         functools.partial(tables_kernel, nx),
         out_shape=(
             jax.ShapeDtypeStruct((6, lev, ny), F32),
@@ -663,6 +644,26 @@
         filter_length,
         jnp.broadcast_to(filter_length[:, None], (lev, ny)),
     )
+    qs, before, after, tables = lax.optimization_barrier((qs, before, after, tables))
+    arrived = [lax.all_to_all(q, BOTH, split_axis=0, concat_axis=0, tiled=True) for q in qs]
+
+    seen = lax.dynamic_slice_in_dim(
+        gathered[:, lev // 2 + 1 : lev // 2 + 3, :], pos_x * count_y + pos_y, 1, axis=2
+    )[:, :, 0].astype(jnp.int32)
+    asked, counts = seen[:, 0], seen[:, 1]
+    g1 = pl.pallas_call(
+        columns_kernel,
+        out_shape=jax.ShapeDtypeStruct((lev * nx, ny), F32),
+        in_specs=[smem(), smem(), vmem(), vmem()],
+        out_specs=vmem(),
+        scratch_shapes=[pltpu.VMEM((lev * nx, ny), F32)],
+        compiler_params=params(12),
+        cost_estimate=pl.CostEstimate(flops=2**33, bytes_accessed=2**23, transcendentals=0),
+        name="columns",
+    )(asked, counts, gathered, increment).reshape(lev, nx, ny)
+    select = (asked[:, None] == jnp.arange(1, nx + 1, dtype=jnp.int32)[None, :]).astype(BF16)
+
+    coef, table_x, edge, nh, nl, spread, coef_y = tables
     sides = wind_sides(wind_u, wind_v, before, after)
     g1, *sides = lax.optimization_barrier((g1, *sides))
     halo_u, halo_v = padded_winds(wind_u, wind_v, (before, after, *sides))
@@ -683,7 +684,7 @@
                 pl.BlockSpec((6, 16, ny), lambda i, off=off: (0, off + i, 0)),
             ],
             out_specs=pl.BlockSpec((16, 16, ny), lambda i: (i, 0, 0)),
-            out_shape=jax.ShapeDtypeStruct((part, 16, ny), F32),
+            out_shape=jax.ShapeDtypeStruct((part, 16, ny), BF16),
             scratch_shapes=[pltpu.VMEM((16 * rows, ny), F32), pltpu.VMEM((16 * 16, ny), F32)],
             compiler_params=params(56),
             name=f"edges_{c}",
@@ -693,7 +694,7 @@
         )
         h = pl.pallas_call(
             scan_x_kernel,
-            out_shape=jax.ShapeDtypeStruct(h.shape, F32),
+            out_shape=jax.ShapeDtypeStruct(h.shape, BF16),
             in_specs=[vmem(), vmem()],
             out_specs=vmem(),
             compiler_params=params(8),

time: 182 us -> 172 us (0.945)
  waiting for transfers between devices: 13.7 us -> 4.03 us
  blocking collectives: 33 us -> 27.5 us
  Pallas kernels: 70 us -> 72.5 us
    ppermute x3, waiting for transfers between devices: 8.19 us -> 1.55 us  [from_before(): return lax.ppermute(array, axis, [(i, i + 1) for i in range(count - 1)])]
    all_to_all x1, blocking collectives: 18.8 us -> 15.8 us  [body(): lax.all_to_all(h.reshape(count_x, share, 16, ny), GX, split_axis=0, conca...]
    ppermute x3, waiting for transfers between devices: 5.23 us -> 2.44 us  [from_after(): return lax.ppermute(array, axis, [(i + 1, i) for i in range(count - 1)])]
    all_to_all x1, blocking collectives: 14.2 us -> 11.7 us  [body(): lax.all_to_all(h, GX, split_axis=0, concat_axis=0, tiled=True)]
    unnamed x46 -> x40, local copies, waits for them, and re-layouts: 12.3 us -> 13.4 us
  transfers between devices with their start and end apart: 9 -> 9, of which waited for: 5 -> 2; matrix products, arithmetic and copies ran while one was open for 1% -> 1% of each run, Pallas kernels for 20% -> 23%
where the time goes in v4:
time: 172 us; the launch traced here: 170 us
  Pallas kernels  72.5 us (42%)
  starting transfers between devices  44.2 us (26%)
  blocking collectives  27.5 us (16%)
  local copies, waits for them, and re-layouts  14.5 us (8%)
  matrix products  4.13 us (2%)
  waiting for transfers between devices  4.03 us (2%)
  other arithmetic  2.25 us (1%)
    pallas_call x1, Pallas kernels, body(): pl.pallas_call(final_kernel, grid=(steps,), in_specs=[pl.BlockSpec((8, de...  16.2 us
    all_to_all x1, blocking collectives, body(): lax.all_to_all(h.reshape(count_x, share, 16, ny), GX, split_axis=0, conca...  15.8 us
    pallas_call x1, Pallas kernels, body(): pl.pallas_call(columns_kernel, out_shape=jax.ShapeDtypeStruct((lev * nx,...  14 us
    unnamed x40, local copies, waits for them, and re-layouts  13.4 us
    all_to_all x1, starting transfers between devices, body(): lax.all_to_all(q, BOTH, split_axis=0, concat_axis=0, tiled=True)  11.9 us
    all_to_all x1, blocking collectives, body(): lax.all_to_all(h, GX, split_axis=0, concat_axis=0, tiled=True)  11.7 us
    all_to_all x1, starting transfers between devices, body(): lax.all_to_all(mine, BOTH, split_axis=0, concat_axis=0, tiled=True)  11.5 us
    ppermute x3, starting transfers between devices, from_before(): return lax.ppermute(array, axis, [(i, i + 1) for i in range(count - 1)])  10.4 us
  transfers between devices with their start and end apart: 9, of which 2 were waited for; matrix products, arithmetic and copies ran while one was open for 1% of the time, Pallas kernels for 23%

profile of v4, /device:TPU:1, one launch (start us, length us, event | category | flops | bytes accessed | tf_op | source)
XLA Modules:
  0.0 170.1 jit_solution(3053055151790620385)
XLA Ops:
  3.6 1.5 sensor.1
  5.8 11.5 %all-to-all-start.1 = ((bf16[128,48,128]{2,1,0:T(8,128)(2,1)}), bf16[128,48,128]{2,1,0:T(8,128)(2,1)S(1)}, u32[]{:S(2)}, u32[]{:S(2)}) async-start(bf16[128,48,128]{2,1,0:T(8,128)(2,1)} %get-tuple-element.58), calls=%async_computation.1 | async-start | bytes 3145728 | tf_op jit(solution)/shard_map/all_to_all | solution.py:607
  17.3 9.7 %records.1 = bf16[128,64,128]{2,1,0:T(8,128)(2,1)} custom-call(s32[64]{0:T(128)} %home_ref.1, s32[64]{0:T(128)} %count_ref.1, bf16[128,512]{1,0:T(8,128)(2,1)} %copy-done.13, bf16[64,512,128]{2,1,0:T(8,128)(2,1)} %dep_ref.1), custom_call_target="tpu_custom_call" | custom-call | tf_op jit(solution)/shard_map/records/pallas_call | solution.py:610
  27.0 1.4 wind_rows.1
  28.5 3.3 %collective-permute-start = (bf16[64,16,128]{2,1,0:T(8,128)(2,1)}, bf16[64,16,128]{2,1,0:T(8,128)(2,1)S(1)}, u32[]{:S(2)}, u32[]{:S(2)}) collective-permute-start(bf16[64,16,128]{2,1,0:T(8,128)(2,1)} %get-tuple-element.46), channel_id=1, source_target_pairs={{0,8},{8,16},{16,24},{24,32},{32,40},{40,48},{48,56},{56,64},{64,7... | collective-permute-start | bytes 786440 | tf_op jit(solution)/shard_map/ppermute | solution.py:362
  33.1 6.5 %tables.1 = (f32[6,64,128]{2,1,0:T(8,128)S(1)}, f32[7,4,8,128]{3,2,1,0:T(8,128)S(1)}, bf16[64,16,128]{2,1,0:T(8,128)(2,1)S(1)}, bf16[64,128,128]{2,1,0:T(8,128)(...) custom-call(s32[1]{0:T(128)} %bitcast.4.share_ref, ...), custom_call_target="tpu_custom_call" | custom-call | tf_op jit(solution)/shard_map/tables/pallas_call | solution.py:627
  41.1 1.4 copy-done.4
  45.4 11.9 %all-to-all-start = ((bf16[128,64,128]{2,1,0:T(8,128)(2,1)}), bf16[128,64,128]{2,1,0:T(8,128)(2,1)}, u32[]{:S(2)}, u32[]{:S(2)}) async-start(bf16[128,64,128]{2,1,0:T(8,128)(2,1)} %records.1), calls=%async_computation | async-start | bytes 4194304 | tf_op jit(solution)/shard_map/all_to_all | solution.py:648
  57.3 3.9 %wind_columns.1 = (bf16[64,16,64]{2,1,0:T(8,128)(2,1)}, bf16[64,16,64]{2,1,0:T(8,128)(2,1)}) custom-call(bf16[64,48,128]{2,1,0:T(8,128)(2,1)S(1)} %copy-done, bf16[64,48,128]{2,1,0:T(8,128)(2,1)S(1)} %copy-done.1, bf16[64,16,128]{2,1,0:T(8,128)(2,1)S(1)} %collective-permute-done.before_ref, bf16[64,16,128]{2,1,0:T(8,128)(2,1)} %collective-permute-done.1.after_ref, ...), custom_call_target="tpu_custom_call" | custom-call | tf_op jit(solution)/shard_map/wind_columns/pallas_call | solution.py:443
  61.2 3.5 %collective-permute-start.2 = (bf16[64,16,64]{2,1,0:T(8,128)(2,1)}, bf16[64,16,64]{2,1,0:T(8,128)(2,1)}, u32[]{:S(2)}, u32[]{:S(2)}) collective-permute-start(bf16[64,16,64]{2,1,0:T(8,128)(2,1)} %get-tuple-element.59), channel_id=1, source_target_pairs={{0,1},{1,2},{2,3},{3,4},{4,5},{5,6},{6,7},{8,9},{9,10},{10,11},{11... | collective-permute-start | bytes 393224 | tf_op jit(solution)/shard_map/ppermute | solution.py:362
  64.8 1.9 %collective-permute-start.3 = (bf16[64,16,64]{2,1,0:T(8,128)(2,1)}, bf16[64,16,64]{2,1,0:T(8,128)(2,1)}, u32[]{:S(2)}, u32[]{:S(2)}) collective-permute-start(bf16[64,16,64]{2,1,0:T(8,128)(2,1)} %get-tuple-element.60), channel_id=1, source_target_pairs={{1,0},{2,1},{3,2},{4,3},{5,4},{6,5},{7,6},{9,8},{10,9},{11,10},{12... | collective-permute-start | bytes 393224 | tf_op jit(solution)/shard_map/ppermute | solution.py:367
  69.7 14.0 %columns.1 = f32[3072,128]{1,0:T(8,128)S(1)} custom-call(s32[128]{0:T(128)S(1)} %get-tuple-element.85.line_ref, s32[128]{0:T(128)S(1)} %get-tuple-element.84.count_ref, bf16[128,48,128]{2,1,0:T(8,128)(2,1)S(1)} %all-to-all-done.1.gathered_ref, bf16[64,48,128]{2,1,0:T(8,128)(2,1)S(1)} %copy-done.19), custom_call_target="tpu_custom_call" | custom-call | flops 8589934592 | bytes 8388608 | tf_op jit(solution)/shard_map/columns/pallas_call | solution.py:654
  84.8 2.9 %wind_pad.1 = (bf16[64,56,256]{2,1,0:T(8,128)(2,1)S(1)}, bf16[64,56,256]{2,1,0:T(8,128)(2,1)S(1)}) custom-call(bf16[64,48,128]{2,1,0:T(8,128)(2,1)S(1)} %copy-done, bf16[64,48,128]{2,1,0:T(8,128)(2,1)S(1)} %copy-done.1, bf16[64,16,128]{2,1,0:T(8,128)(2,1)S(1)} %collective-permute-done.before_ref, bf16[64,16,128]{2,1,0:T(8,128)(2,1)} %collective-permute-done.1.after_ref, ...), custom_call_target="tpu_custom_call" | custom-call | tf_op jit(solution)/shard_map/wind_pad/pallas_call | solution.py:462
  90.2 4.1 %fusion.2.g2_ref = f32[64,48,128]{2,1,0:T(8,128)} fusion(bf16[128,64,128]{2,1,0:T(8,128)(2,1)} %all-to-all-done, s32[128]{0:T(128)S(1)} %get-tuple-element.85.line_ref, s32[48]{0:T(128)S(1)} %iota_add_fusion), kind=kOutput, calls=%fused_computation.2 | convolution fusion | flops 100669440 | bytes 3670720 | tf_op jit(solution)/shard_map/sx,sly->lxy/dot_general | solution.py:674
  94.4 5.4 %edges_0.1 = bf16[64,16,128]{2,1,0:T(8,128)(2,1)} custom-call(f32[64,48,128]{2,1,0:T(8,128)} %bitcast.22, f32[64,48,128]{2,1,0:T(8,128)} %fusion.2.g2_ref, bf16[4,64,48,128]{3,2,1,0:T(8,128)(2,1)} %ens_ref.3, f32[6,64,128]{2,1,0:T(8,128)} %copy-done.8), custom_call_target="tpu_custom_call" | custom-call | tf_op jit(solution)/shard_map/edges_0/pallas_call | solution.py:677
  99.7 15.8 %all_to_all.25.in_ref = bf16[16,4,16,128]{3,2,1,0:T(8,128)(2,1)S(1)} all-to-all(bf16[16,4,16,128]{3,2,1,0:T(8,128)(2,1)} %bitcast.25), channel_id=1, replica_groups=mesh['gx'=16,'gy'=8] {'gx'}, dimensions={0} | all-to-all | bytes 524288 | tf_op jit(solution)/shard_map/all_to_all | solution.py:692
  115.7 11.7 %all_to_all.26 = bf16[16,4,16,128]{3,2,1,0:T(8,128)(2,1)} all-to-all(bf16[16,4,16,128]{3,2,1,0:T(8,128)(2,1)S(1)} %scan_x_0.1), channel_id=1, replica_groups=mesh['gx'=16,'gy'=8] {'gx'}, dimensions={0} | all-to-all | bytes 524288 | tf_op jit(solution)/shard_map/all_to_all | solution.py:703
  127.4 10.1 %filter_x_0.1 = (bf16[64,256,128]{2,1,0:T(8,128)(2,1)}, bf16[64,256,128]{2,1,0:T(8,128)(2,1)}, bf16[8,2,64,256]{3,2,1,0:T(8,128)(2,1)}, bf16[3,64,128]{2,1,0:T(8,128)(2,1)}, bf16[3,64,128]{2,1,0:T(8,128)(2,1)}) custom-call(f32[64,48,128]{2,1,0:T(8,128)} %bitcast.23, f32[64,48,128]{2,1,0:T(8,128)} %fusion.2.g2_ref, bf16[4,64,48,128]{3,2,1,0:T(8,128)(2,1)} %ens_ref.3, ...), custom_call_target="tpu_custom_call" | custom-call | tf_op jit(solution)/shard_map/filter_x_0/pallas_call | solution.py:704
  137.5 5.4 %all-to-all-start.4 = ((bf16[8,2,64,256]{3,2,1,0:T(8,128)(2,1)}), bf16[8,2,64,256]{3,2,1,0:T(8,128)(2,1)S(1)}, u32[]{:S(2)}, u32[]{:S(2)}) async-start(bf16[8,2,64,256]{3,2,1,0:T(8,128)(2,1)} %get-tuple-element.75), calls=%async_computation.4 | async-start | bytes 1048576 | tf_op jit(solution)/shard_map/all_to_all | solution.py:738
  142.9 3.5 %collective-permute-start.4 = (bf16[3,64,128]{2,1,0:T(8,128)(2,1)}, bf16[3,64,128]{2,1,0:T(8,128)(2,1)S(1)}, u32[]{:S(2)}, u32[]{:S(2)}) collective-permute-start(bf16[3,64,128]{2,1,0:T(8,128)(2,1)} %get-tuple-element.76), channel_id=1, source_target_pairs={{0,1},{1,2},{2,3},{3,4},{4,5},{5,6},{6,7},{8,9},{9,10},{10,11},{11... | collective-permute-start | bytes 147464 | tf_op jit(solution)/shard_map/ppermute | solution.py:362
  146.5 1.9 %collective-permute-start.5 = (bf16[3,64,128]{2,1,0:T(8,128)(2,1)}, bf16[3,64,128]{2,1,0:T(8,128)(2,1)S(1)}, u32[]{:S(2)}, u32[]{:S(2)}) collective-permute-start(bf16[3,64,128]{2,1,0:T(8,128)(2,1)} %get-tuple-element.77), channel_id=1, source_target_pairs={{1,0},{2,1},{3,2},{4,3},{5,4},{6,5},{7,6},{9,8},{10,9},{11,10},{12... | collective-permute-start | bytes 147464 | tf_op jit(solution)/shard_map/ppermute | solution.py:367
  148.4 1.5 collective-permute-done.4.fl_ref
  149.9 2.4 %collective-permute-done.5.fr_ref = bf16[3,64,128]{2,1,0:T(8,128)(2,1)S(1)} collective-permute-done((bf16[3,64,128]{2,1,0:T(8,128)(2,1)}, bf16[3,64,128]{2,1,0:T(8,128)(2,1)S(1)}, u32[]{:S(2)}, u32[]{:S(2)}) %collective-permute-start.5) | collective-permute-done | bytes 49184 | tf_op jit(solution)/shard_map/ppermute | solution.py:367
  153.9 16.2 %final_0.1 = (f32[4,64,48,128]{3,2,1,0:T(8,128)}, f32[64,48,128]{2,1,0:T(8,128)}) custom-call(bf16[64,256,128]{2,1,0:T(8,128)(2,1)} %get-tuple-element.71.hi_ref, bf16[64,256,128]{2,1,0:T(8,128)(2,1)} %get-tuple-element.72.lo_ref, bf16[64,128,128]{2,1,0:T(8,128)(2,1)} %copy-done.3, bf16[64,128,128]{2,1,0:T(8,128)(2,1)} %copy-done.4, ...), custom_call_target="tpu_custom_call" | custom-call | tf_op jit(solution)/shard_map/final_0/pallas_call | solution.py:757
  (59 shorter events, 17.6 us)
Async XLA Ops:
  2.1 0.8 copy-start.14
  5.8 39.6 %all-to-all-start.1 = ((bf16[128,48,128]{2,1,0:T(8,128)(2,1)}), bf16[128,48,128]{2,1,0:T(8,128)(2,1)S(1)}, u32[]{:S(2)}, u32[]{:S(2)}) async-start(bf16[128,48,128]{2,1,0:T(8,128)(2,1)} %get-tuple-element.58), calls=%async_computation.1 | async-start | bytes 3145728 | tf_op jit(solution)/shard_map/all_to_all | solution.py:607
  17.3 9.8 %copy-start = (bf16[64,48,128]{2,1,0:T(8,128)(2,1)S(1)}, bf16[64,48,128]{2,1,0:T(8,128)(2,1)}, u32[]{:S(2)}) copy-start(bf16[64,48,128]{2,1,0:T(8,128)(2,1)} %u_ref.2) | copy-start | bytes 2359300
  17.3 9.7 %copy-start.1 = (bf16[64,48,128]{2,1,0:T(8,128)(2,1)S(1)}, bf16[64,48,128]{2,1,0:T(8,128)(2,1)}, u32[]{:S(2)}) copy-start(bf16[64,48,128]{2,1,0:T(8,128)(2,1)} %v_ref.2) | copy-start | bytes 2359300
  17.3 15.8 %copy-start.17 = (f32[64]{0:T(128)S(1)}, f32[64]{0:T(128)}, u32[]{:S(2)}) copy-start(f32[64]{0:T(128)} %len_ref.1) | copy-start | bytes 772
  28.5 17.0 %collective-permute-start = (bf16[64,16,128]{2,1,0:T(8,128)(2,1)}, bf16[64,16,128]{2,1,0:T(8,128)(2,1)S(1)}, u32[]{:S(2)}, u32[]{:S(2)}) collective-permute-start(bf16[64,16,128]{2,1,0:T(8,128)(2,1)} %get-tuple-element.46), channel_id=1, source_target_pairs={{0,8},{8,16},{16,24},{24,32},{32,40},{40,48},{48,56},{56,64},{64,7... | collective-permute-start | bytes 786440 | tf_op jit(solution)/shard_map/ppermute | solution.py:362
  31.8 13.7 %collective-permute-start.1 = (bf16[64,16,128]{2,1,0:T(8,128)(2,1)}, bf16[64,16,128]{2,1,0:T(8,128)(2,1)}, u32[]{:S(2)}, u32[]{:S(2)}) collective-permute-start(bf16[64,16,128]{2,1,0:T(8,128)(2,1)} %get-tuple-element.47), channel_id=1, source_target_pairs={{8,0},{16,8},{24,16},{32,24},{40,32},{48,40},{56,48},{64,56},{72,6... | collective-permute-start | bytes 786440 | tf_op jit(solution)/shard_map/ppermute | solution.py:367
  39.7 1.4 copy-start.3
  41.1 1.4 copy-start.4
  43.1 0.8 copy-start.9
  43.9 0.8 copy-start.10
  45.4 11.9 %copy-start.16 = (bf16[16,128]{1,0:T(8,128)(2,1)S(1)}, bf16[16,128]{1,0:T(8,128)(2,1)}, u32[]{:S(2)}) copy-start(bf16[16,128]{1,0:T(8,128)(2,1)} %constant.28.clone.pick_ref) | copy-start | bytes 12292
  45.4 44.8 %all-to-all-start = ((bf16[128,64,128]{2,1,0:T(8,128)(2,1)}), bf16[128,64,128]{2,1,0:T(8,128)(2,1)}, u32[]{:S(2)}, u32[]{:S(2)}) async-start(bf16[128,64,128]{2,1,0:T(8,128)(2,1)} %records.1), calls=%async_computation | async-start | bytes 4194304 | tf_op jit(solution)/shard_map/all_to_all | solution.py:648
  61.2 23.6 %collective-permute-start.2 = (bf16[64,16,64]{2,1,0:T(8,128)(2,1)}, bf16[64,16,64]{2,1,0:T(8,128)(2,1)}, u32[]{:S(2)}, u32[]{:S(2)}) collective-permute-start(bf16[64,16,64]{2,1,0:T(8,128)(2,1)} %get-tuple-element.59), channel_id=1, source_target_pairs={{0,1},{1,2},{2,3},{3,4},{4,5},{5,6},{6,7},{8,9},{9,10},{10,11},{11... | collective-permute-start | bytes 393224 | tf_op jit(solution)/shard_map/ppermute | solution.py:362
  64.8 20.1 %collective-permute-start.3 = (bf16[64,16,64]{2,1,0:T(8,128)(2,1)}, bf16[64,16,64]{2,1,0:T(8,128)(2,1)}, u32[]{:S(2)}, u32[]{:S(2)}) collective-permute-start(bf16[64,16,64]{2,1,0:T(8,128)(2,1)} %get-tuple-element.60), channel_id=1, source_target_pairs={{1,0},{2,1},{3,2},{4,3},{5,4},{6,5},{7,6},{9,8},{10,9},{11,10},{12... | collective-permute-start | bytes 393224 | tf_op jit(solution)/shard_map/ppermute | solution.py:367
  68.5 1.2 copy-start.19
  69.7 15.1 %copy-start.15 = (bf16[32,256]{1,0:T(8,128)(2,1)S(1)}, bf16[32,256]{1,0:T(8,128)(2,1)}, u32[]{:S(2)}) copy-start(bf16[32,256]{1,0:T(8,128)(2,1)} %constant.29.clone.place_ref) | copy-start | bytes 49156
  83.7 1.1 copy-start.2
  87.7 1.2 copy-start.6
  89.0 1.2 copy-start.7
  127.4 25.0 %copy-start.11 = (f32[14,64,128]{2,1,0:T(8,128)S(1)}, f32[14,64,128]{2,1,0:T(8,128)}, u32[]{:S(2)}) copy-start(f32[14,64,128]{2,1,0:T(8,128)} %copy-done.10) | copy-start | bytes 1376260
  137.5 14.9 %all-to-all-start.4 = ((bf16[8,2,64,256]{3,2,1,0:T(8,128)(2,1)}), bf16[8,2,64,256]{3,2,1,0:T(8,128)(2,1)S(1)}, u32[]{:S(2)}, u32[]{:S(2)}) async-start(bf16[8,2,64,256]{3,2,1,0:T(8,128)(2,1)} %get-tuple-element.75), calls=%async_computation.4 | async-start | bytes 1048576 | tf_op jit(solution)/shard_map/all_to_all | solution.py:738
  142.9 7.0 %collective-permute-start.4 = (bf16[3,64,128]{2,1,0:T(8,128)(2,1)}, bf16[3,64,128]{2,1,0:T(8,128)(2,1)S(1)}, u32[]{:S(2)}, u32[]{:S(2)}) collective-permute-start(bf16[3,64,128]{2,1,0:T(8,128)(2,1)} %get-tuple-element.76), channel_id=1, source_target_pairs={{0,1},{1,2},{2,3},{3,4},{4,5},{5,6},{6,7},{8,9},{9,10},{10,11},{11... | collective-permute-start | bytes 147464 | tf_op jit(solution)/shard_map/ppermute | solution.py:362
  146.5 5.9 %collective-permute-start.5 = (bf16[3,64,128]{2,1,0:T(8,128)(2,1)}, bf16[3,64,128]{2,1,0:T(8,128)(2,1)S(1)}, u32[]{:S(2)}, u32[]{:S(2)}) collective-permute-start(bf16[3,64,128]{2,1,0:T(8,128)(2,1)} %get-tuple-element.77), channel_id=1, source_target_pairs={{1,0},{2,1},{3,2},{4,3},{5,4},{6,5},{7,6},{9,8},{10,9},{11,10},{12... | collective-permute-start | bytes 147464 | tf_op jit(solution)/shard_map/ppermute | solution.py:367
  (5 other events, 3.5 us)

commit v5 on v4

--- a/solution.py
+++ b/solution.py
@@ -665,9 +665,7 @@
 
     coef, table_x, edge, nh, nl, spread, coef_y = tables
     sides = wind_sides(wind_u, wind_v, before, after)
-    g1, *sides = lax.optimization_barrier((g1, *sides))
-    halo_u, halo_v = padded_winds(wind_u, wind_v, (before, after, *sides))
-    arrived, halo_u, halo_v, g1 = lax.optimization_barrier((arrived, halo_u, halo_v, g1))
+    arrived, g1 = lax.optimization_barrier((arrived, g1))
 
     alpha = static = None
     for c in range(CHUNKS):
@@ -689,6 +687,9 @@
             compiler_params=params(56),
             name=f"edges_{c}",
         )(g1, g2, ensemble, coef)
+        if c == 0:
+            h, *sides = lax.optimization_barrier((h, *sides))
+            halo_u, halo_v = padded_winds(wind_u, wind_v, (before, after, *sides))
         h = lax.all_to_all(
             h.reshape(count_x, share, 16, ny), GX, split_axis=0, concat_axis=0, tiled=True
         )

time: 172 us -> 168 us (0.977)
  blocking collectives: 27.5 us -> 23.7 us
    all_to_all x1, blocking collectives: 15.8 us -> 12.9 us  [body(): lax.all_to_all(h.reshape(count_x, share, 16, ny), GX, split_axis=0, conca...]
    all_to_all x1, waiting for transfers between devices: 0.01 us -> 2.6 us  [body(): lax.all_to_all(q, BOTH, split_axis=0, concat_axis=0, tiled=True)]
    ppermute x3, waiting for transfers between devices: 2.44 us -> 0.01 us  [from_after(): return lax.ppermute(array, axis, [(i + 1, i) for i in range(count - 1)])]
  transfers between devices with their start and end apart: 9 -> 9, of which waited for: 2 -> 1; matrix products, arithmetic and copies ran while one was open for 1% -> 4% of each run, Pallas kernels for 23% -> 26%
where the time goes in v5:
time: 168 us; the launch traced here: 166 us
  Pallas kernels  72.5 us (43%)
  starting transfers between devices  45.6 us (27%)
  blocking collectives  23.7 us (14%)
  local copies, waits for them, and re-layouts  14.5 us (9%)
  matrix products  4.13 us (2%)
  waiting for transfers between devices  2.62 us (2%)
  other arithmetic  2.25 us (1%)
    pallas_call x1, Pallas kernels, body(): pl.pallas_call(final_kernel, grid=(steps,), in_specs=[pl.BlockSpec((8, de...  16.2 us
    pallas_call x1, Pallas kernels, body(): pl.pallas_call(columns_kernel, out_shape=jax.ShapeDtypeStruct((lev * nx,...  14 us
    unnamed x40, local copies, waits for them, and re-layouts  13.4 us
    all_to_all x1, blocking collectives, body(): lax.all_to_all(h.reshape(count_x, share, 16, ny), GX, split_axis=0, conca...  12.9 us
    all_to_all x1, starting transfers between devices, body(): lax.all_to_all(q, BOTH, split_axis=0, concat_axis=0, tiled=True)  11.9 us
    all_to_all x1, starting transfers between devices, body(): lax.all_to_all(mine, BOTH, split_axis=0, concat_axis=0, tiled=True)  11.5 us
    all_to_all x1, blocking collectives, body(): lax.all_to_all(h, GX, split_axis=0, concat_axis=0, tiled=True)  10.8 us
    ppermute x3, starting transfers between devices, from_before(): return lax.ppermute(array, axis, [(i, i + 1) for i in range(count - 1)])  10.4 us
  transfers between devices with their start and end apart: 9, of which 1 were waited for; matrix products, arithmetic and copies ran while one was open for 4% of the time, Pallas kernels for 26%

profile of v5, /device:TPU:1, one launch (start us, length us, event | category | flops | bytes accessed | tf_op | source)
XLA Modules:
  0.0 166.2 jit_solution(2269262645690881511)
XLA Ops:
  3.6 1.5 sensor.1
  5.8 11.5 %all-to-all-start.1 = ((bf16[128,48,128]{2,1,0:T(8,128)(2,1)}), bf16[128,48,128]{2,1,0:T(8,128)(2,1)S(1)}, u32[]{:S(2)}, u32[]{:S(2)}) async-start(bf16[128,48,128]{2,1,0:T(8,128)(2,1)} %get-tuple-element.54), calls=%async_computation.1 | async-start | bytes 3145728 | tf_op jit(solution)/shard_map/all_to_all | solution.py:607
  17.3 9.7 %records.1 = bf16[128,64,128]{2,1,0:T(8,128)(2,1)} custom-call(s32[64]{0:T(128)} %home_ref.1, s32[64]{0:T(128)} %count_ref.1, bf16[128,512]{1,0:T(8,128)(2,1)} %copy-done.13, bf16[64,512,128]{2,1,0:T(8,128)(2,1)} %dep_ref.1), custom_call_target="tpu_custom_call" | custom-call | tf_op jit(solution)/shard_map/records/pallas_call | solution.py:610
  27.0 1.4 wind_rows.1
  28.4 3.3 %collective-permute-start = (bf16[64,16,128]{2,1,0:T(8,128)(2,1)}, bf16[64,16,128]{2,1,0:T(8,128)(2,1)S(1)}, u32[]{:S(2)}, u32[]{:S(2)}) collective-permute-start(bf16[64,16,128]{2,1,0:T(8,128)(2,1)} %get-tuple-element.44), channel_id=1, source_target_pairs={{0,8},{8,16},{16,24},{24,32},{32,40},{40,48},{48,56},{56,64},{64,7... | collective-permute-start | bytes 786440 | tf_op jit(solution)/shard_map/ppermute | solution.py:362
  33.1 6.5 %tables.1 = (f32[6,64,128]{2,1,0:T(8,128)S(1)}, f32[7,4,8,128]{3,2,1,0:T(8,128)S(1)}, bf16[64,16,128]{2,1,0:T(8,128)(2,1)S(1)}, bf16[64,128,128]{2,1,0:T(8,128)(...) custom-call(s32[1]{0:T(128)} %bitcast.4.share_ref, ...), custom_call_target="tpu_custom_call" | custom-call | tf_op jit(solution)/shard_map/tables/pallas_call | solution.py:627
  39.7 1.4 copy-done.3
  41.1 1.4 copy-done.4
  45.4 11.9 %all-to-all-start = ((bf16[128,64,128]{2,1,0:T(8,128)(2,1)}), bf16[128,64,128]{2,1,0:T(8,128)(2,1)}, u32[]{:S(2)}, u32[]{:S(2)}) async-start(bf16[128,64,128]{2,1,0:T(8,128)(2,1)} %records.1), calls=%async_computation | async-start | bytes 4194304 | tf_op jit(solution)/shard_map/all_to_all | solution.py:648
  57.3 3.9 %wind_columns.1 = (bf16[64,16,64]{2,1,0:T(8,128)(2,1)}, bf16[64,16,64]{2,1,0:T(8,128)(2,1)}) custom-call(bf16[64,48,128]{2,1,0:T(8,128)(2,1)S(1)} %copy-done, bf16[64,48,128]{2,1,0:T(8,128)(2,1)S(1)} %copy-done.1, bf16[64,16,128]{2,1,0:T(8,128)(2,1)S(1)} %collective-permute-done.before_ref, bf16[64,16,128]{2,1,0:T(8,128)(2,1)} %collective-permute-done.1.after_ref, ...), custom_call_target="tpu_custom_call" | custom-call | tf_op jit(solution)/shard_map/wind_columns/pallas_call | solution.py:443
  61.2 3.5 %collective-permute-start.2 = (bf16[64,16,64]{2,1,0:T(8,128)(2,1)}, bf16[64,16,64]{2,1,0:T(8,128)(2,1)}, u32[]{:S(2)}, u32[]{:S(2)}) collective-permute-start(bf16[64,16,64]{2,1,0:T(8,128)(2,1)} %get-tuple-element.60), channel_id=1, source_target_pairs={{0,1},{1,2},{2,3},{3,4},{4,5},{5,6},{6,7},{8,9},{9,10},{10,11},{11... | collective-permute-start | bytes 393224 | tf_op jit(solution)/shard_map/ppermute | solution.py:362
  64.8 1.9 %collective-permute-start.3 = (bf16[64,16,64]{2,1,0:T(8,128)(2,1)}, bf16[64,16,64]{2,1,0:T(8,128)(2,1)}, u32[]{:S(2)}, u32[]{:S(2)}) collective-permute-start(bf16[64,16,64]{2,1,0:T(8,128)(2,1)} %get-tuple-element.61), channel_id=1, source_target_pairs={{1,0},{2,1},{3,2},{4,3},{5,4},{6,5},{7,6},{9,8},{10,9},{11,10},{12... | collective-permute-start | bytes 393224 | tf_op jit(solution)/shard_map/ppermute | solution.py:367
  69.7 14.0 %columns.1 = f32[3072,128]{1,0:T(8,128)S(1)} custom-call(s32[128]{0:T(128)S(1)} %get-tuple-element.81.line_ref, s32[128]{0:T(128)S(1)} %get-tuple-element.80.count_ref, bf16[128,48,128]{2,1,0:T(8,128)(2,1)S(1)} %all-to-all-done.1.gathered_ref, bf16[64,48,128]{2,1,0:T(8,128)(2,1)S(1)} %copy-done.19), custom_call_target="tpu_custom_call" | custom-call | flops 8589934592 | bytes 8388608 | tf_op jit(solution)/shard_map/columns/pallas_call | solution.py:654
  84.9 2.6 %all-to-all-done = bf16[128,64,128]{2,1,0:T(8,128)(2,1)} async-done(((bf16[128,64,128]{2,1,0:T(8,128)(2,1)}), bf16[128,64,128]{2,1,0:T(8,128)(2,1)}, u32[]{:S(2)}, u32[]{:S(2)}) %all-to-all-start) | async-done | bytes 2097184 | tf_op jit(solution)/shard_map/all_to_all | solution.py:648
  87.5 4.1 %fusion.2.g2_ref = f32[64,48,128]{2,1,0:T(8,128)} fusion(bf16[128,64,128]{2,1,0:T(8,128)(2,1)} %all-to-all-done, s32[128]{0:T(128)S(1)} %get-tuple-element.81.line_ref, s32[48]{0:T(128)S(1)} %iota_add_fusion), kind=kOutput, calls=%fused_computation.2 | convolution fusion | flops 100669440 | bytes 3670720 | tf_op jit(solution)/shard_map/sx,sly->lxy/dot_general | solution.py:672
  91.6 5.4 %edges_0.1 = bf16[64,16,128]{2,1,0:T(8,128)(2,1)} custom-call(f32[64,48,128]{2,1,0:T(8,128)} %bitcast.22, f32[64,48,128]{2,1,0:T(8,128)} %fusion.2.g2_ref, bf16[4,64,48,128]{3,2,1,0:T(8,128)(2,1)} %ens_ref.3, f32[6,64,128]{2,1,0:T(8,128)} %copy-done.8), custom_call_target="tpu_custom_call" | custom-call | tf_op jit(solution)/shard_map/edges_0/pallas_call | solution.py:675
  97.0 12.9 %all_to_all.25.in_ref = bf16[16,4,16,128]{3,2,1,0:T(8,128)(2,1)S(1)} all-to-all(bf16[16,4,16,128]{3,2,1,0:T(8,128)(2,1)} %bitcast.25), channel_id=1, replica_groups=mesh['gx'=16,'gy'=8] {'gx'}, dimensions={0} | all-to-all | bytes 524288 | tf_op jit(solution)/shard_map/all_to_all | solution.py:693
  110.1 10.8 %all_to_all.26 = bf16[16,4,16,128]{3,2,1,0:T(8,128)(2,1)} all-to-all(bf16[16,4,16,128]{3,2,1,0:T(8,128)(2,1)S(1)} %scan_x_0.1), channel_id=1, replica_groups=mesh['gx'=16,'gy'=8] {'gx'}, dimensions={0} | all-to-all | bytes 524288 | tf_op jit(solution)/shard_map/all_to_all | solution.py:704
  120.9 10.0 %filter_x_0.1 = (bf16[64,256,128]{2,1,0:T(8,128)(2,1)}, bf16[64,256,128]{2,1,0:T(8,128)(2,1)}, bf16[8,2,64,256]{3,2,1,0:T(8,128)(2,1)}, bf16[3,64,128]{2,1,0:T(8,128)(2,1)}, bf16[3,64,128]{2,1,0:T(8,128)(2,1)}) custom-call(f32[64,48,128]{2,1,0:T(8,128)} %bitcast.23, f32[64,48,128]{2,1,0:T(8,128)} %fusion.2.g2_ref, bf16[4,64,48,128]{3,2,1,0:T(8,128)(2,1)} %ens_ref.3, ...), custom_call_target="tpu_custom_call" | custom-call | tf_op jit(solution)/shard_map/filter_x_0/pallas_call | solution.py:705
  130.9 6.7 %all-to-all-start.4 = ((bf16[8,2,64,256]{3,2,1,0:T(8,128)(2,1)}), bf16[8,2,64,256]{3,2,1,0:T(8,128)(2,1)S(1)}, u32[]{:S(2)}, u32[]{:S(2)}) async-start(bf16[8,2,64,256]{3,2,1,0:T(8,128)(2,1)} %get-tuple-element.69), calls=%async_computation.4 | async-start | bytes 1048576 | tf_op jit(solution)/shard_map/all_to_all | solution.py:739
  137.7 3.5 %collective-permute-start.4 = (bf16[3,64,128]{2,1,0:T(8,128)(2,1)}, bf16[3,64,128]{2,1,0:T(8,128)(2,1)S(1)}, u32[]{:S(2)}, u32[]{:S(2)}) collective-permute-start(bf16[3,64,128]{2,1,0:T(8,128)(2,1)} %get-tuple-element.70), channel_id=1, source_target_pairs={{0,1},{1,2},{2,3},{3,4},{4,5},{5,6},{6,7},{8,9},{9,10},{10,11},{11... | collective-permute-start | bytes 147464 | tf_op jit(solution)/shard_map/ppermute | solution.py:362
  141.2 1.9 %collective-permute-start.5 = (bf16[3,64,128]{2,1,0:T(8,128)(2,1)}, bf16[3,64,128]{2,1,0:T(8,128)(2,1)S(1)}, u32[]{:S(2)}, u32[]{:S(2)}) collective-permute-start(bf16[3,64,128]{2,1,0:T(8,128)(2,1)} %get-tuple-element.71), channel_id=1, source_target_pairs={{1,0},{2,1},{3,2},{4,3},{5,4},{6,5},{7,6},{9,8},{10,9},{11,10},{12... | collective-permute-start | bytes 147464 | tf_op jit(solution)/shard_map/ppermute | solution.py:367
  143.2 2.9 %wind_pad.1 = (bf16[64,56,256]{2,1,0:T(8,128)(2,1)S(1)}, bf16[64,56,256]{2,1,0:T(8,128)(2,1)S(1)}) custom-call(bf16[64,48,128]{2,1,0:T(8,128)(2,1)S(1)} %copy-done, bf16[64,48,128]{2,1,0:T(8,128)(2,1)S(1)} %copy-done.1, bf16[64,16,128]{2,1,0:T(8,128)(2,1)S(1)} %collective-permute-done.before_ref, bf16[64,16,128]{2,1,0:T(8,128)(2,1)} %collective-permute-done.1.after_ref, ...), custom_call_target="tpu_custom_call" | custom-call | tf_op jit(solution)/shard_map/wind_pad/pallas_call | solution.py:462
  150.0 16.2 %final_0.1 = (f32[4,64,48,128]{3,2,1,0:T(8,128)}, f32[64,48,128]{2,1,0:T(8,128)}) custom-call(bf16[64,256,128]{2,1,0:T(8,128)(2,1)} %get-tuple-element.65.hi_ref, bf16[64,256,128]{2,1,0:T(8,128)(2,1)} %get-tuple-element.66.lo_ref, bf16[64,128,128]{2,1,0:T(8,128)(2,1)} %copy-done.3, bf16[64,128,128]{2,1,0:T(8,128)(2,1)} %copy-done.4, ...), custom_call_target="tpu_custom_call" | custom-call | tf_op jit(solution)/shard_map/final_0/pallas_call | solution.py:758
  (59 shorter events, 16.3 us)
Async XLA Ops:
  2.1 0.8 copy-start.14
  5.8 39.6 %all-to-all-start.1 = ((bf16[128,48,128]{2,1,0:T(8,128)(2,1)}), bf16[128,48,128]{2,1,0:T(8,128)(2,1)S(1)}, u32[]{:S(2)}, u32[]{:S(2)}) async-start(bf16[128,48,128]{2,1,0:T(8,128)(2,1)} %get-tuple-element.54), calls=%async_computation.1 | async-start | bytes 3145728 | tf_op jit(solution)/shard_map/all_to_all | solution.py:607
  17.3 9.8 %copy-start = (bf16[64,48,128]{2,1,0:T(8,128)(2,1)S(1)}, bf16[64,48,128]{2,1,0:T(8,128)(2,1)}, u32[]{:S(2)}) copy-start(bf16[64,48,128]{2,1,0:T(8,128)(2,1)} %u_ref.2) | copy-start | bytes 2359300
  17.3 9.7 %copy-start.1 = (bf16[64,48,128]{2,1,0:T(8,128)(2,1)S(1)}, bf16[64,48,128]{2,1,0:T(8,128)(2,1)}, u32[]{:S(2)}) copy-start(bf16[64,48,128]{2,1,0:T(8,128)(2,1)} %v_ref.2) | copy-start | bytes 2359300
  17.3 15.7 %copy-start.17 = (f32[64]{0:T(128)S(1)}, f32[64]{0:T(128)}, u32[]{:S(2)}) copy-start(f32[64]{0:T(128)} %len_ref.1) | copy-start | bytes 772
  28.4 17.0 %collective-permute-start = (bf16[64,16,128]{2,1,0:T(8,128)(2,1)}, bf16[64,16,128]{2,1,0:T(8,128)(2,1)S(1)}, u32[]{:S(2)}, u32[]{:S(2)}) collective-permute-start(bf16[64,16,128]{2,1,0:T(8,128)(2,1)} %get-tuple-element.44), channel_id=1, source_target_pairs={{0,8},{8,16},{16,24},{24,32},{32,40},{40,48},{48,56},{56,64},{64,7... | collective-permute-start | bytes 786440 | tf_op jit(solution)/shard_map/ppermute | solution.py:362
  31.7 13.7 %collective-permute-start.1 = (bf16[64,16,128]{2,1,0:T(8,128)(2,1)}, bf16[64,16,128]{2,1,0:T(8,128)(2,1)}, u32[]{:S(2)}, u32[]{:S(2)}) collective-permute-start(bf16[64,16,128]{2,1,0:T(8,128)(2,1)} %get-tuple-element.45), channel_id=1, source_target_pairs={{8,0},{16,8},{24,16},{32,24},{40,32},{48,40},{56,48},{64,56},{72,6... | collective-permute-start | bytes 786440 | tf_op jit(solution)/shard_map/ppermute | solution.py:367
  39.7 1.4 copy-start.3
  41.0 1.4 copy-start.4
  43.1 0.8 copy-start.9
  43.9 0.8 copy-start.10
  45.4 11.9 %copy-start.16 = (bf16[16,128]{1,0:T(8,128)(2,1)S(1)}, bf16[16,128]{1,0:T(8,128)(2,1)}, u32[]{:S(2)}) copy-start(bf16[16,128]{1,0:T(8,128)(2,1)} %constant.28.clone.pick_ref) | copy-start | bytes 12292
  45.4 42.0 %all-to-all-start = ((bf16[128,64,128]{2,1,0:T(8,128)(2,1)}), bf16[128,64,128]{2,1,0:T(8,128)(2,1)}, u32[]{:S(2)}, u32[]{:S(2)}) async-start(bf16[128,64,128]{2,1,0:T(8,128)(2,1)} %records.1), calls=%async_computation | async-start | bytes 4194304 | tf_op jit(solution)/shard_map/all_to_all | solution.py:648
  61.2 35.7 %collective-permute-start.2 = (bf16[64,16,64]{2,1,0:T(8,128)(2,1)}, bf16[64,16,64]{2,1,0:T(8,128)(2,1)}, u32[]{:S(2)}, u32[]{:S(2)}) collective-permute-start(bf16[64,16,64]{2,1,0:T(8,128)(2,1)} %get-tuple-element.60), channel_id=1, source_target_pairs={{0,1},{1,2},{2,3},{3,4},{4,5},{5,6},{6,7},{8,9},{9,10},{10,11},{11... | collective-permute-start | bytes 393224 | tf_op jit(solution)/shard_map/ppermute | solution.py:362
  64.8 32.2 %collective-permute-start.3 = (bf16[64,16,64]{2,1,0:T(8,128)(2,1)}, bf16[64,16,64]{2,1,0:T(8,128)(2,1)}, u32[]{:S(2)}, u32[]{:S(2)}) collective-permute-start(bf16[64,16,64]{2,1,0:T(8,128)(2,1)} %get-tuple-element.61), channel_id=1, source_target_pairs={{1,0},{2,1},{3,2},{4,3},{5,4},{6,5},{7,6},{9,8},{10,9},{11,10},{12... | collective-permute-start | bytes 393224 | tf_op jit(solution)/shard_map/ppermute | solution.py:367
  68.6 1.2 copy-start.19
  83.7 1.1 copy-start.2
  120.9 22.3 %copy-start.15 = (bf16[32,256]{1,0:T(8,128)(2,1)S(1)}, bf16[32,256]{1,0:T(8,128)(2,1)}, u32[]{:S(2)}) copy-start(bf16[32,256]{1,0:T(8,128)(2,1)} %constant.29.clone.place_ref) | copy-start | bytes 49156
  130.9 17.6 %copy-start.11 = (f32[14,64,128]{2,1,0:T(8,128)S(1)}, f32[14,64,128]{2,1,0:T(8,128)}, u32[]{:S(2)}) copy-start(f32[14,64,128]{2,1,0:T(8,128)} %copy-done.10) | copy-start | bytes 1376260
  130.9 17.6 %all-to-all-start.4 = ((bf16[8,2,64,256]{3,2,1,0:T(8,128)(2,1)}), bf16[8,2,64,256]{3,2,1,0:T(8,128)(2,1)S(1)}, u32[]{:S(2)}, u32[]{:S(2)}) async-start(bf16[8,2,64,256]{3,2,1,0:T(8,128)(2,1)} %get-tuple-element.69), calls=%async_computation.4 | async-start | bytes 1048576 | tf_op jit(solution)/shard_map/all_to_all | solution.py:739
  137.7 10.8 %collective-permute-start.4 = (bf16[3,64,128]{2,1,0:T(8,128)(2,1)}, bf16[3,64,128]{2,1,0:T(8,128)(2,1)S(1)}, u32[]{:S(2)}, u32[]{:S(2)}) collective-permute-start(bf16[3,64,128]{2,1,0:T(8,128)(2,1)} %get-tuple-element.70), channel_id=1, source_target_pairs={{0,1},{1,2},{2,3},{3,4},{4,5},{5,6},{6,7},{8,9},{9,10},{10,11},{11... | collective-permute-start | bytes 147464 | tf_op jit(solution)/shard_map/ppermute | solution.py:362
  141.2 7.3 %collective-permute-start.5 = (bf16[3,64,128]{2,1,0:T(8,128)(2,1)}, bf16[3,64,128]{2,1,0:T(8,128)(2,1)S(1)}, u32[]{:S(2)}, u32[]{:S(2)}) collective-permute-start(bf16[3,64,128]{2,1,0:T(8,128)(2,1)} %get-tuple-element.71), channel_id=1, source_target_pairs={{1,0},{2,1},{3,2},{4,3},{5,4},{6,5},{7,6},{9,8},{10,9},{11,10},{12... | collective-permute-start | bytes 147464 | tf_op jit(solution)/shard_map/ppermute | solution.py:367
  146.1 1.2 copy-start.6
  147.3 1.2 copy-start.7
  (5 other events, 3.5 us)
